TPU v7x, 512 devices: a whole 4x8x8 slice. The times are simulated.
512 devices in a mesh: line: 64 (over y, z_lo, core), bus: 8 (over x, z_hi).
Axes of the slice: x: 4, y: 8, z: 8 (z_hi: 2, z_lo: 4; z = z_hi * 4 + z_lo), core: 2. Of those that a mesh axis runs over, the one named last changes fastest.
Arguments:
- shift_factors: float32 [8192, 60416], P('line', 'bus'), may hold values from -2 to 2
- injection: float32 [32, 60416], P(None, 'bus'), may hold values from -0.046875 to 0.046875
- rating: float32 [8192], P('line'), may hold values from 0.5 to 4
- monitored: int32 [4096, 8], P('line'), may hold values from 0 to 63, all different within a row; in each aligned block of 64 rows (0 to 63, 64 to 127, ...) at most 12 rows name the same one
- live_count: int32 [4096], P('line'), may hold values from 4 to 8
- outage_offset: int32 [4096], P('line'), may hold values from 0 to 127
- outage_ends: int32 [4096, 2], P('line'), may hold values from 0 to 60415
Outputs:
- loading: float32 [4096, 8, 128], P('line', None, 'bus')
Inputs may be any that keep to these rules, and one draw needn't show every extreme that they name: `monitored`: each row names 8 different blocks; among the 64 outages of one index of line (aligned blocks of rows) no block is named in more than 12 rows, and some block in exactly 12.
All inputs are finite; a program needn't handle non-finite values.
Results may differ from a plain program's by a relative error of at most 0.0003.
Values sent between devices are 32-bit elements; how exact they have to be, the bound alone decides.
No kernel may reach another device: no remote copies, remote signals or barrier semaphores. Data moves between devices by JAX's collectives and lax.ppermute only.
A program may use at most 64 MiB of HBM per device.

v0:
```python
import jax
import jax.numpy as jnp
from jax import lax
from jax.sharding import PartitionSpec as P

floor_value = 0.25


def local(shift_factors, injection, rating, monitored, live_count, outage_offset, outage_ends):
    bus_count = lax.axis_size("bus")
    line_count = lax.axis_size("line")
    bus_place = lax.axis_index("bus")
    block_rows, bus_width = shift_factors.shape
    sub_rows = block_rows // bus_count
    outages, slot_count = monitored.shape
    capacity = 3 * outages * slot_count // (2 * line_count)
    entries = outages * slot_count
    row_start = bus_place * sub_rows
    partial_value = lax.dot_general(
        injection,
        shift_factors,
        (((1,), (1,)), ((), ())),
        precision=lax.Precision.HIGHEST,
        preferred_element_type=jnp.float32,
    )
    summed = lax.psum(partial_value, "bus")
    flow_part = lax.dynamic_slice_in_dim(summed, row_start, sub_rows, 1)
    rate_part = lax.dynamic_slice_in_dim(rating, row_start, sub_rows, 0)
    flow_all, rate_all = (
        lax.all_gather(flow_part, "line", axis=1, tiled=True),
        lax.all_gather(rate_part, "line", axis=0, tiled=True),
    )
    target = monitored.reshape(entries)
    one_hot = (target[:, None] == jnp.arange(line_count, dtype=jnp.int32)[None, :]).astype(
        jnp.int32
    )
    slot_rank = jnp.sum((jnp.cumsum(one_hot, axis=0) - 1) * one_hot, axis=1)
    position = target * capacity + slot_rank
    is_live = (jnp.arange(slot_count, dtype=jnp.int32)[None, :] < live_count[:, None]).reshape(
        entries
    )
    ends_each = jnp.broadcast_to(outage_ends[:, None, :], (outages, slot_count, 2)).reshape(
        entries, 2
    )
    ends_sent = jnp.where(is_live[:, None], ends_each, -1)
    requests = jnp.full((2, line_count * capacity), -1, jnp.int32).at[:, position].set(ends_sent.T)
    received = lax.all_to_all(requests, "line", split_axis=1, concat_axis=1, tiled=True)
    columns = received - bus_place * bus_width
    inside = (columns >= 0) & (columns < bus_width)
    clipped = jnp.clip(columns, 0, bus_width - 1)
    picked = jnp.take(shift_factors, clipped.reshape(-1), axis=1).reshape(
        block_rows, 2, line_count * capacity
    )
    picked = jnp.where(inside[None], picked, 0.0)
    partial_sens = picked[:, 0] - picked[:, 1]
    sens_summed = lax.psum(partial_sens, "bus")
    sens_part = lax.dynamic_slice_in_dim(sens_summed, row_start, sub_rows, 0)
    returned = lax.all_to_all(sens_part, "line", split_axis=1, concat_axis=1, tiled=True)
    own_sens = returned[:, position]
    first_entry = jnp.arange(outages, dtype=jnp.int32) * slot_count
    local_offset = outage_offset - row_start
    holds = (local_offset >= 0) & (local_offset < sub_rows)
    offset_clip = jnp.clip(local_offset, 0, sub_rows - 1)
    self_part = jnp.where(holds, own_sens[offset_clip, first_entry], 0.0)
    lost_rows = monitored[:, 0] * sub_rows + offset_clip
    lost_part = jnp.where(holds[None, :], flow_all[:, lost_rows], 0.0)
    self_sens, lost_flow = lax.psum((self_part, lost_part), "bus")
    divisor = jnp.maximum(1.0 - self_sens, floor_value)
    entry_index = jnp.arange(entries, dtype=jnp.int32)
    outage_of = entry_index // slot_count
    factor = own_sens / divisor[outage_of][None, :]
    row_index = jnp.arange(sub_rows, dtype=jnp.int32)
    monitored_rows = target[None, :] * sub_rows + row_index[:, None]
    post_flow = flow_all[:, monitored_rows] + factor[None] * lost_flow[:, outage_of][:, None, :]
    outaged_here = (entry_index % slot_count == 0)[None, :] & (
        row_index[:, None] == local_offset[outage_of][None, :]
    )
    post_flow = jnp.where(outaged_here[None], 0.0, post_flow)
    loading = jnp.max(jnp.abs(post_flow), axis=0) / rate_all[monitored_rows]
    loading = jnp.where(is_live[None, :], loading, 0.0)
    return loading.T.reshape(outages, slot_count, sub_rows)


def solution(mesh):
    return jax.shard_map(
        local,
        mesh=mesh,
        in_specs=(
            P("line", "bus"),
            P(None, "bus"),
            P("line"),
            P("line", None),
            P("line"),
            P("line"),
            P("line", None),
        ),
        out_specs=P("line", None, "bus"),
        check_vma=False,
    )
```

profile of v0, /device:TPU:1, one launch (start us, length us, event | category | flops | bytes accessed | tf_op | source)
XLA Modules:
  0.0 546.2 jit_solution(6886065449234569589)
XLA Ops:
  6.5 0.9 copy.74
  8.3 1.2 reduce-window.6
  9.9 0.7 iota_compare_fusion.3
  10.8 0.8 copy.78
  11.7 1.9 scatter_custom_fusion
  14.6 14.6 %all-to-all-start = ((s32[2,64,12]{2,0,1:T(2,128)}), s32[2,64,12]{2,0,1:T(2,128)S(1)}, u32[]{:S(2)}, u32[]{:S(2)}) async-start(s32[2,64,12]{2,0,1:T(2,128)} %copy.80), calls=%async_computation | async-start | bytes 131072 | tf_op jit(solution)/shard_map/all_to_all | solution.py:47
  30.6 0.7 fusion.28
  31.4 0.7 fusion.29
  33.5 5.3 fusion.31
  38.8 48.2 %psum.28 = f32[32,128]{0,1:T(8,128)S(1)} all-reduce(f32[32,128]{0,1:T(8,128)S(1)} %fusion.31), channel_id=1, replica_groups=mesh['line'=64,'bus'=8] {'bus'}, use_global_device_ids=true, to_apply=%region_0.0 | all-reduce | flops 4096 | bytes 32768 | tf_op jit(solution)/shard_map/psum | solution.py:26
  87.1 40.0 %select_select_fusion.2 = (s32[512]{0:T(512)S(1)}, pred[512]{0:T(512)(128)(4,1)S(1)}, pred[512]{0:T(512)(128)(4,1)S(1)}, pred[512]{0:T(512)(128)(4,1)S(1)}, pred...) fusion(s32[]{:T(128)} %bitcast.1, s32[]{:T(128)} %bitcast.2, ...), kind=kLoop, calls=%fused_computation.57 | loop fusion | flops 64512 | bytes 36608 | tf_op jit(solution)/shard_map/gather | solution.py:76
  127.1 1.3 dynamic-slice
  129.3 5.4 copy.85
  135.2 4.7 gather_fusion.1
  140.6 0.8 fusion
  141.4 89.0 %all_gather.6 = f32[32,1024]{0,1:T(8,128)S(1)} all-gather(f32[32,16]{0,1:T(8,128)S(1)} %constant_dynamic-slice_fusion.1), channel_id=1, replica_groups=mesh['line'=64,'bus'=8] {'line'}, dimensions={1}, use_global_device_ids=true | all-gather | bytes 133120 | tf_op jit(solution)/shard_map/all_gather | solution.py:30
  231.0 27.7 %gather_fusion = f32[8192,32]{1,0:T(8,128)} fusion(f32[32,1024]{0,1:T(8,128)S(1)} %all_gather.6, s32[8192]{0:T(1024)S(1)} %broadcast_clamp_fusion), kind=kCustom, calls=%fused_computation | custom fusion | bytes 2129920 | tf_op jit(solution)/shard_map/gather | solution.py:74
  258.7 133.0 %all-reduce = f32[1024]{0:T(1024)S(1)} all-reduce(f32[1024]{0:T(1024)S(1)} %dynamic-slice_dynamic-update-slice_fusion), channel_id=1, replica_groups=mesh['line'=64,'bus'=8] {'line'}, use_global_device_ids=true, to_apply=%add | all-reduce | flops 1024 | bytes 8192
  391.6 32.9 %gather_fusion.6 = f32[8192]{0:T(1024)S(1)} fusion(f32[1024]{0:T(1024)S(1)} %all-reduce, s32[8192]{0:T(1024)S(1)} %broadcast_clamp_fusion), kind=kCustom, calls=%fused_computation.6 | custom fusion | bytes 98304 | tf_op jit(solution)/shard_map/gather | solution.py:79
  424.6 0.8 constant_dynamic-slice_fusion
  426.3 1.0 reshape.545
  427.4 5.7 %all-to-all-start.1 = ((f32[64,1,192]{2,1,0:T(1,128)}), f32[64,1,192]{2,1,0:T(1,128)S(1)}, u32[]{:S(2)}, u32[]{:S(2)}) async-start(f32[64,1,192]{2,1,0:T(1,128)} %reshape.545), calls=%async_computation.1 | async-start | bytes 131072 | tf_op jit(solution)/shard_map/all_to_all | solution.py:58
  433.1 10.1 %all-to-all-done.1 = f32[64,1,192]{2,1,0:T(1,128)S(1)} async-done(((f32[64,1,192]{2,1,0:T(1,128)}), f32[64,1,192]{2,1,0:T(1,128)S(1)}, u32[]{:S(2)}, u32[]{:S(2)}) %all-to-all-start.1) | async-done | bytes 49184 | tf_op jit(solution)/shard_map/all_to_all | solution.py:58
  443.8 0.8 reduce.4
  445.4 1.0 gather_fusion.2
  446.5 0.9 gather_fusion.3
  447.4 40.1 %all-reduce.1 = (f32[32,64]{0,1:T(8,128)S(1)}, f32[64]{0:T(128)S(1)}) all-reduce(f32[32,64]{0,1:T(8,128)S(1)} %select_bitcast_fusion, f32[64]{0:T(128)S(1)} %broadcast_select_fusion), channel_id=1, replica_groups=mesh['line'=64,'bus'=8] {'bus'}, use_global_device_ids=true, to_apply=%region_7.8 | all-reduce | flops 2112 | bytes 16896 | tf_op jit(solution)/shard_map/psum | solution.py:67
  487.5 0.7 fusion.24
  490.4 40.1 %select_select_fusion.1 = f32[512]{0:T(512)S(1)} fusion(pred[512]{0:T(512)(128)(4,1)S(1)} %get-tuple-element.70, pred[512]{0:T(512)(128)(4,1)S(1)} %get-tuple-element.69, pred[512]{0:T(512)(128)(4,1)S(1)} %get-tuple-element.68, pred[512]{0:T(512)(128)(4,1)S(1)} %get-tuple-element.67, pred[512]{0:T(512)(128)(4,1)S(1)} %get-tuple-element.66, ...), kind=kLoop, calls=%fused_computation.56 | loop fusion | flops 32256 | bytes 34560 | tf_op jit(solution)/shard_map/gather | solution.py:71
  530.5 1.0 gather_fusion.5
  531.5 6.9 %abs_reduce_fusion = f32[16,512]{1,0:T(8,128)S(1)} fusion(f32[32,16,512]{0,2,1:T(8,128)} %bitcast.191, f32[32,512]{0,1:T(8,128)S(1)} %bitcast.196, f32[16,512]{1,0:T(8,128)S(1)} %broadcast_divide_fusion, pred[16,512]{1,0:T(8,128)(4,1)S(1)} %fusion.10), kind=kLoop, calls=%fused_computation.8 | loop fusion | flops 1302528 | bytes 1187840 | tf_op jit(solution)/shard_map/reduce_max | solution.py:79
  538.6 0.8 copy.92
  (72 shorter events, 11.9 us)
Async XLA Ops:
  6.5 27.0 %copy-start = (f32[32,7552]{1,0:T(8,128)S(1)}, f32[32,7552]{1,0:T(8,128)}, u32[]{:S(2)}) copy-start(f32[32,7552]{1,0:T(8,128)} %param.8) | copy-start | bytes 2899972
  6.5 122.6 %copy-start.1 = (f32[128]{0:T(128)S(1)}, f32[128]{0:T(128)}, u32[]{:S(2)}) copy-start(f32[128]{0:T(128)} %param.9) | copy-start | bytes 1540
  14.6 120.2 %all-to-all-start = ((s32[2,64,12]{2,0,1:T(2,128)}), s32[2,64,12]{2,0,1:T(2,128)S(1)}, u32[]{:S(2)}, u32[]{:S(2)}) async-start(s32[2,64,12]{2,0,1:T(2,128)} %copy.80), calls=%async_computation | async-start | bytes 131072 | tf_op jit(solution)/shard_map/all_to_all | solution.py:47
  29.2 395.4 %all-reduce.4.cloned.1.call-start = ((), (), s32[]{:S(2)}) async-start(), calls=%async_computation.2 | async-start | bytes 786432 | tf_op jit(solution)/shard_map/psum | solution.py:56
  427.4 15.9 %all-to-all-start.1 = ((f32[64,1,192]{2,1,0:T(1,128)}), f32[64,1,192]{2,1,0:T(1,128)S(1)}, u32[]{:S(2)}, u32[]{:S(2)}) async-start(f32[64,1,192]{2,1,0:T(1,128)} %reshape.545), calls=%async_computation.1 | async-start | bytes 131072 | tf_op jit(solution)/shard_map/all_to_all | solution.py:58
Sparse Core Ops, SparseCore 0:
  141.5 113.4 all-reduce.3
where the time goes:
time: 553 us; the launch traced here: 546 us
  blocking collectives  310 us (56%)
  other arithmetic  94.9 us (17%)
  local copies, waits for them, and re-layouts  90.7 us (16%)
  starting transfers between devices  20.4 us (4%)
  between operations  14.5 us (3%)
  waiting for transfers between devices  10.2 us (2%)
    unnamed x1, blocking collectives  133 us
    all_gather x1, blocking collectives, local(): lax.all_gather(flow_part, 'line', axis=1, tiled=True)  89 us
    psum x1, blocking collectives, local(): summed = lax.psum(partial_value, 'bus')  48.2 us
    psum x1, blocking collectives, local(): self_sens, lost_flow = lax.psum((self_part, lost_part), 'bus')  40.1 us
    gather x1, other arithmetic, local(): factor = own_sens / divisor[outage_of][None, :]  40.1 us
    gather x1, other arithmetic, local(): local_offset[outage_of][None, :]  40 us
    gather x2, local copies, waits for them, and re-layouts, local(): loading = jnp.max(jnp.abs(post_flow), axis=0) / rate_all[monitored_rows]  32.9 us
    gather x1, local copies, waits for them, and re-layouts, local(): flow_all[:, monitored_rows]  27.7 us
  transfers between devices with their start and end apart: 3, of which 1 were waited for; matrix products, arithmetic and copies ran while one was open for 22% of the time, Pallas kernels for 0%

commit v1 on v0

v1 whole, which is shorter than its diff:
```python
import functools

import jax
import jax.numpy as jnp
from jax import lax
from jax.experimental import pallas as pl
from jax.experimental.pallas import tpu as pltpu
from jax.sharding import PartitionSpec as P

floor_value = 0.25
F32 = jnp.float32
BF16 = jnp.bfloat16
NT = (((1,), (1,)), ((), ()))
TN = (((0,), (0,)), ((), ()))
HOURS = 32
CAP = 12
CHUNK = 512


def iota(shape, axis):
    return lax.broadcasted_iota(jnp.int32, shape, axis)


def split2(value):
    high = value.astype(BF16)
    return high, (value - high.astype(F32)).astype(BF16)


def request_kernel(mon_ref, ends_ref, off_ref, out_ref):
    outages, slots = mon_ref.shape
    lane = iota((outages, 128), 1)
    names = jnp.zeros((outages, 128), F32)
    for s in range(slots):
        names = jnp.where(mon_ref[:, s : s + 1] == lane, 1.0, names)
    before = jnp.where(iota((outages, outages), 1) < iota((outages, outages), 0), 1.0, 0.0)
    rank = lax.dot_general(
        before.astype(BF16), names.astype(BF16), (((1,), (0,)), ((), ())), preferred_element_type=F32
    )
    square_row, square_lane = iota((outages, outages), 0), iota((outages, outages), 1)
    off = jnp.sum(jnp.where(square_row == square_lane, off_ref[...], 0), axis=1, keepdims=True)
    ones = jnp.ones((outages, 128), jnp.int32)
    start = (ends_ref[:, 0:1] + 1) * ones
    end = (ends_ref[:, 1:2] + 1) * ones
    place = (off + 1) * ones
    chosen, values = [], []
    for c in range(CAP):
        chosen.append(jnp.where(rank == float(c), names, 0.0).astype(BF16))
        value = jnp.where(lane == c, start, jnp.where(lane == 16 + c, end, jnp.where(lane == 32 + c, place, 0)))
        values.append(
            jnp.concatenate([(value >> 8).astype(F32), (value & 255).astype(F32)], axis=1).astype(BF16)
        )
    both = lax.dot_general(
        jnp.concatenate(chosen, axis=0), jnp.concatenate(values, axis=0), TN, preferred_element_type=F32
    )
    packed = 256.0 * both[:, :128] + both[:, 128:]
    out_ref[...] = packed[: out_ref.shape[0]]


def flow_kernel(s_ref, inj_ref, split_ref, part_ref):
    rows, width = s_ref.shape
    total = jnp.zeros((2 * HOURS, 2 * rows), F32)

    def step(at, size, total):
        cols = pl.ds(at, size)
        s_high, s_low = split2(s_ref[:, cols])
        both = jnp.concatenate([s_high, s_low], axis=0)
        split_ref[:, cols] = both
        i_high, i_low = split2(inj_ref[:, cols])
        return total + lax.dot_general(
            jnp.concatenate([i_high, i_low], axis=0), both, NT, preferred_element_type=F32
        )

    whole = width // CHUNK
    total = lax.fori_loop(0, whole, lambda q, t: step(pl.multiple_of(q * CHUNK, CHUNK), CHUNK, t), total)
    if width % CHUNK:
        total = step(whole * CHUNK, width % CHUNK, total)
    part_ref[...] = (
        total[:HOURS, :rows] + (total[:HOURS, rows:] + total[HOURS:, :rows]) + total[HOURS:, rows:]
    )


def pick_kernel(req_ref, split_ref, part_ref, out_ref, from_ref, to_ref, sum_ref):
    lines = req_ref.shape[0]
    both_rows, width = split_ref.shape
    rows = both_rows // 2
    buses, _, entries = out_ref.shape
    sub = rows // buses
    base = lax.axis_index("bus") * width + 1
    req = req_ref[...]
    lane = iota((lines, 128), 1)
    for c in range(CAP):
        first = req[:, c : c + 1].astype(jnp.int32) - base
        second = req[:, 16 + c : 17 + c].astype(jnp.int32) - base
        same = first == second
        first = jnp.where(same, -1, first)
        second = jnp.where(same, -1, second)
        from_ref[c * lines : (c + 1) * lines, :] = jnp.broadcast_to(first, (lines, 128))
        to_ref[c * lines : (c + 1) * lines, :] = jnp.broadcast_to(second, (lines, 128))
    sum_ref[...] = jnp.zeros_like(sum_ref)

    def step(at, size):
        columns = []
        for t in range(size // 128):
            spot = iota((entries, 128), 1) + (at + t * 128)
            hot = jnp.where(from_ref[...] == spot, 1.0, jnp.where(to_ref[...] == spot, -1.0, 0.0))
            columns.append(hot.astype(BF16))
        sum_ref[...] += lax.dot_general(
            jnp.concatenate(columns, axis=1), split_ref[:, pl.ds(at, size)], NT, preferred_element_type=F32
        )

    whole = width // CHUNK

    def body(q, carry):
        step(pl.multiple_of(q * CHUNK, CHUNK), CHUNK)
        return carry

    lax.fori_loop(0, whole, body, 0)
    if width % CHUNK:
        step(whole * CHUNK, width % CHUNK)
    picked = sum_ref[:, :rows] + sum_ref[:, rows:]
    own = jnp.zeros((lines, 128), F32)
    for c in range(CAP):
        off = req[:, 32 + c : 33 + c].astype(jnp.int32) - 1
        value = jnp.sum(
            jnp.where(lane == off, picked[c * lines : (c + 1) * lines], 0.0), axis=1, keepdims=True
        )
        own = jnp.where(lane == c, value, own)
    turned = jnp.transpose(picked)
    own_turned = jnp.transpose(jnp.concatenate([own, jnp.zeros((128 - lines, 128), F32)], axis=0))
    part = part_ref[...]
    extra = jnp.concatenate(
        [part[8 * t : 8 * t + 8] for t in range(4)] + [own_turned[0:8], own_turned[8:16]], axis=1
    )
    for b in range(buses):
        out_ref[b, :sub, :] = turned[b * sub : (b + 1) * sub]
        out_ref[b, sub:, :] = extra


def reply_kernel(got_ref, req_ref, rate_ref, out_ref, rate_scratch):
    buses, _, _ = got_ref.shape
    lines = req_ref.shape[0]
    rows = rate_ref.shape[1]
    sub = rows // buses
    place = lax.axis_index("bus")
    total = got_ref[0]
    for b in range(1, buses):
        total = total + got_ref[b]
    flows = jnp.concatenate([total[sub : sub + 8, 128 * t : 128 * t + 128] for t in range(4)], axis=0)
    lane = iota((HOURS, 128), 1)
    hour = iota((HOURS, 128), 0)
    wanted = iota((128, 128), 0) == place * sub + iota((128, 128), 1) % sub
    select = jnp.where(wanted, 1.0, 0.0).astype(BF16)
    f_high, f_low = split2(flows)
    f_rest = (flows - f_high.astype(F32) - f_low.astype(F32)).astype(BF16)
    spread = lax.dot_general(
        jnp.concatenate([f_high, f_low, f_rest], axis=0),
        select,
        (((1,), (0,)), ((), ())),
        preferred_element_type=F32,
    )
    spread = spread[:HOURS] + spread[HOURS : 2 * HOURS] + spread[2 * HOURS :]
    spread = jnp.where(lane // sub == hour % 8, spread, 0.0)
    for t in range(4):
        row = jnp.sum(spread[8 * t : 8 * t + 8], axis=0, keepdims=True)
        out_ref[:, 128 * t : 128 * t + 128] = jnp.broadcast_to(row, (lines, 128))
    req = req_ref[...]
    lane_line = iota((lines, 128), 1)
    hots = [
        jnp.where(lane_line == req[:, 32 + c : 33 + c].astype(jnp.int32) - 1, 1.0, 0.0).astype(BF16)
        for c in range(CAP)
    ]
    left = jnp.concatenate([jnp.concatenate(hots[4 * q : 4 * q + 4], axis=1) for q in range(3)], axis=0)

    def diagonal(block):
        blank = jnp.zeros_like(block)
        return jnp.concatenate(
            [jnp.concatenate([block if v == u else blank for v in range(4)], axis=1) for u in range(4)], axis=0
        )

    lost = lax.dot_general(
        left, diagonal(f_high), NT, preferred_element_type=F32
    ) + lax.dot_general(left, diagonal(f_low), NT, preferred_element_type=F32)
    for q in range(3):
        out_ref[:, 512 + 128 * q : 640 + 128 * q] = lost[q * lines : (q + 1) * lines]
    rate_scratch[...] = jnp.transpose(jnp.broadcast_to(rate_ref[...], (128, 128)))
    rate = rate_scratch[pl.ds(pl.multiple_of(place * sub, sub), sub), :]
    sens = total[:sub]

    def wide(block):
        return jnp.concatenate([block, jnp.zeros((block.shape[0], 128 - lines), F32)], axis=1)

    blocks = [wide(sens[:, c * lines : (c + 1) * lines]) for c in range(CAP)]
    one = jnp.concatenate(blocks[:8], axis=0)
    two = jnp.concatenate(
        blocks[8:] + [total[sub : sub + 8, 512:640], total[sub : sub + 8, 640:768], rate, jnp.zeros((32, 128), F32)],
        axis=0,
    )
    out_ref[:, 896:1024] = jnp.transpose(one)[:lines]
    out_ref[:, 1024:1152] = jnp.transpose(two)[:lines]


def screen_kernel(got_ref, mon_ref, off_ref, live_ref, out_ref):
    lines = got_ref.shape[0]
    outages, slots = mon_ref.shape
    sub = out_ref.shape[1]
    place = lax.axis_index("bus")
    pieces = []
    for t in range(9):
        block = got_ref[:, 128 * t : 128 * t + 128]
        high = block.astype(BF16).astype(F32)
        low = (block - high).astype(BF16).astype(F32)
        pieces.append(jnp.transpose(jnp.concatenate([high, low], axis=0)).astype(BF16))
    shared = jnp.concatenate(pieces[:4] + pieces[7:], axis=0)
    own = jnp.concatenate(pieces[4:7] + pieces[8:], axis=0)
    mon = jnp.concatenate([mon_ref[...].astype(F32), jnp.zeros((outages, 128 - slots), F32)], axis=1)
    named = jnp.transpose(jnp.concatenate([mon, mon], axis=0))[:slots].astype(jnp.int32)
    line_row = iota((lines, 128), 0)
    lane = iota((1, 128), 1)
    outage = lane % outages
    names = jnp.zeros((lines, 128), F32)
    for s in range(slots):
        names = jnp.where(named[s : s + 1] == line_row, 1.0, names)
    earlier = iota((128, 128), 0) < iota((128, 128), 1) % outages
    rank = lax.dot_general(
        names.astype(BF16),
        jnp.where(earlier, 1.0, 0.0).astype(BF16),
        (((1,), (0,)), ((), ())),
        preferred_element_type=F32,
    )

    def hot_of(target):
        hot = jnp.where(line_row == target, 1.0, 0.0)
        turn = jnp.sum(hot * rank, axis=0, keepdims=True)
        hot = hot.astype(BF16)
        return jnp.concatenate([hot, hot], axis=0), turn

    plain = (((1,), (0,)), ((), ()))
    hot_own, turn_own = hot_of(named[0:1])
    got_own = lax.dot_general(own, hot_own, plain, preferred_element_type=F32)
    lost = jnp.zeros((HOURS, 128), F32)
    self_sens = jnp.zeros((1, 128), F32)
    for c in range(CAP):
        mine = turn_own == float(c)
        lost = jnp.where(mine, got_own[HOURS * c : HOURS * c + HOURS], lost)
        self_sens = jnp.where(mine, got_own[448 + c : 449 + c], self_sens)
    divisor = jnp.maximum(1.0 - self_sens, floor_value)
    off = jnp.concatenate([off_ref[...], off_ref[...]], axis=1)
    live = jnp.concatenate([live_ref[...], live_ref[...]], axis=1)
    lost_scaled = lost
    row = iota((sub, 128), 0)
    for t in range(slots // 2):
        target = jnp.where(lane < outages, named[2 * t : 2 * t + 1], named[2 * t + 1 : 2 * t + 2])
        hot, turn = hot_of(target)
        got = lax.dot_general(shared, hot, plain, preferred_element_type=F32)
        sens = jnp.zeros((sub, 128), F32)
        for c in range(CAP):
            sens = jnp.where(turn == float(c), got[512 + sub * c : 512 + sub * c + sub], sens)
        factor = sens / divisor
        worst = jnp.zeros((sub, 128), F32)
        for h in range(HOURS):
            worst = jnp.maximum(worst, jnp.abs(got[sub * h : sub * h + sub] + factor * lost_scaled[h : h + 1]))
        result = worst / got[720:736]
        slot = 2 * t + jnp.where(lane < outages, 0, 1)
        keep = slot < live
        if t == 0:
            keep = keep & ~((slot == 0) & (row == off - place * sub))
        result = jnp.where(keep, result, 0.0)
        turned = jnp.transpose(jnp.concatenate([result, jnp.zeros((128 - sub, 128), F32)], axis=0))
        out_ref[pl.ds(2 * t, outages, stride=slots), :] = turned[:outages, :sub]
        out_ref[pl.ds(2 * t + 1, outages, stride=slots), :] = turned[outages:, :sub]


def call(kernel, out_shape, scratch=(), flops=0, moved=0):
    single = not isinstance(out_shape, (tuple, list))
    spec = pl.BlockSpec(memory_space=pltpu.VMEM)
    return pl.pallas_call(
        kernel,
        out_shape=out_shape,
        out_specs=spec if single else tuple(spec for _ in out_shape),
        scratch_shapes=list(scratch),
        compiler_params=pltpu.CompilerParams(vmem_limit_bytes=32 * 1024 * 1024),
        cost_estimate=pl.CostEstimate(flops=flops, bytes_accessed=moved, transcendentals=0),
    )


def local(shift_factors, injection, rating, monitored, live_count, outage_offset, outage_ends):
    bus_count = lax.axis_size("bus")
    line_count = lax.axis_size("line")
    block_rows, bus_width = shift_factors.shape
    sub_rows = block_rows // bus_count
    outages, slot_count = monitored.shape
    entries = CAP * line_count
    shape = jax.ShapeDtypeStruct
    off_row = outage_offset.reshape(1, outages)
    live_row = live_count.reshape(1, outages)
    rate_row = rating.reshape(1, block_rows)
    with jax.named_scope("requests"):
        requests = call(request_kernel, shape((line_count, 128), F32))(monitored, outage_ends, off_row)
        asked = lax.all_to_all(requests, "line", split_axis=0, concat_axis=0, tiled=True)
    with jax.named_scope("flows"):
        split, part = call(
            flow_kernel,
            (shape((2 * block_rows, bus_width), BF16), shape((HOURS, block_rows), F32)),
            flops=8 * HOURS * block_rows * bus_width,
            moved=3 * 4 * block_rows * bus_width,
        )(shift_factors, injection)
    with jax.named_scope("picks"):
        partial_sens = call(
            pick_kernel,
            shape((bus_count, sub_rows + 8, entries), F32),
            scratch=(
                pltpu.VMEM((entries, 128), jnp.int32),
                pltpu.VMEM((entries, 128), jnp.int32),
                pltpu.VMEM((entries, 2 * block_rows), F32),
            ),
            flops=4 * entries * block_rows * bus_width,
            moved=4 * block_rows * bus_width,
        )(asked, split, part)
        sens = lax.all_to_all(partial_sens, "bus", split_axis=0, concat_axis=0, tiled=True)
    with jax.named_scope("reply"):
        reply = call(reply_kernel, shape((line_count, 1152), F32), scratch=(pltpu.VMEM((128, 128), F32),))(
            sens, asked, rate_row
        )
        got = lax.all_to_all(reply, "line", split_axis=0, concat_axis=0, tiled=True)
    with jax.named_scope("screen"):
        loading = call(screen_kernel, shape((outages * slot_count, sub_rows), F32))(
            got, monitored, off_row, live_row
        )
    return loading.reshape(outages, slot_count, sub_rows)


def solution(mesh):
    return jax.shard_map(
        local,
        mesh=mesh,
        in_specs=(
            P("line", "bus"),
            P(None, "bus"),
            P("line"),
            P("line", None),
            P("line"),
            P("line"),
            P("line", None),
        ),
        out_specs=P("line", None, "bus"),
        check_vma=False,
    )
```

time: 553 us -> 92.3 us (0.17); the launches traced: 546 us -> 91.9 us
  blocking collectives: 310 us -> 52.7 us
  other arithmetic: 94.9 us -> 0 us
  local copies, waits for them, and re-layouts: 90.7 us -> 10.5 us
  between operations: 14.5 us -> 0.09 us
  Pallas kernels: 0 us -> 12.8 us
  waiting for transfers between devices: 10.2 us -> 1.19 us
  starting transfers between devices: 20.4 us -> 14.6 us
    unnamed x1 -> x0, blocking collectives: 133 us -> none
    all_gather x1 -> x0, blocking collectives: 89 us -> none  [local(): lax.all_gather(flow_part, 'line', axis=1, tiled=True)]
    psum x2 -> x0, blocking collectives: 88.3 us -> none  [the longest x1 48.2 us: local(): summed = lax.psum(partial_value, 'bus')]
    gather x7 -> x0, other arithmetic: 80.1 us -> none  [the longest x1 40.1 us: local(): factor = own_sens / divisor[outage_of][None, :]]
    gather x18 -> x0, local copies, waits for them, and re-layouts: 74.9 us -> none  [the longest x2 32.9 us: local(): loading = jnp.max(jnp.abs(post_flow), axis=0) / rate_all[monitored_rows]]
    all_to_all x0 -> x2, blocking collectives: none -> 52.7 us  [the longest x1 28.2 us: local(): got = lax.all_to_all(reply, 'line', split_axis=0, concat_axis=0, tiled=True)]
    pallas_call x0 -> x5, Pallas kernels: none -> 12.8 us  [the longest x1 7.4 us: local(): call(pick_kernel, shape((bus_count, sub_rows + 8, entries), F32), scratch...]
    all_to_all x2 -> x1, waiting for transfers between devices: 10.1 us -> 1.19 us  [local(): lax.all_to_all(requests, 'line', split_axis=0, concat_axis=0, tiled=True)]
  transfers between devices with their start and end apart: 3 -> 1, of which waited for: 1 -> 1; matrix products, arithmetic and copies ran while one was open for 22% -> 0% of each run, Pallas kernels for 0% -> 4%
where the time goes in v1:
time: 92.3 us; the launch traced here: 91.9 us
  blocking collectives  52.7 us (57%)
  starting transfers between devices  14.6 us (16%)
  Pallas kernels  12.8 us (14%)
  local copies, waits for them, and re-layouts  10.5 us (11%)
  waiting for transfers between devices  1.19 us (1%)
    all_to_all x1, blocking collectives, local(): got = lax.all_to_all(reply, 'line', split_axis=0, concat_axis=0, tiled=True)  28.2 us
    all_to_all x1, blocking collectives, local(): lax.all_to_all(partial_sens, 'bus', split_axis=0, concat_axis=0, tiled=True)  24.5 us
    all_to_all x1, starting transfers between devices, local(): lax.all_to_all(requests, 'line', split_axis=0, concat_axis=0, tiled=True)  14.6 us
    unnamed x19, local copies, waits for them, and re-layouts  9.45 us
    pallas_call x1, Pallas kernels, local(): call(pick_kernel, shape((bus_count, sub_rows + 8, entries), F32), scratch...  7.4 us
    pallas_call x1, Pallas kernels, local(): call(flow_kernel, (shape((2 * block_rows, bus_width), BF16), shape((HOURS...  3.22 us
  transfers between devices with their start and end apart: 1, of which 1 were waited for; matrix products, arithmetic and copies ran while one was open for 0% of the time, Pallas kernels for 4%

profile of v1, /device:TPU:1, one launch (start us, length us, event | category | flops | bytes accessed | tf_op | source)
XLA Modules:
  0.0 91.9 jit_solution(6747999057566838906)
XLA Ops:
  0.0 0.8 copy.12.mon_ref
  0.8 0.8 copy.13.ends_ref
  1.5 0.0 copy-start.2
  1.5 0.7 copy-done.2
  2.2 1.2 %requests.1 = f32[64,128]{1,0:T(8,128)} custom-call(s32[64,8]{1,0:T(8,128)S(1)} %copy.12.mon_ref, s32[64,2]{1,0:T(8,128)S(1)} %copy.13.ends_ref, s32[1,64]{1,0:T(1,128)S(1)} %bitcast.17), custom_call_target="tpu_custom_call" | custom-call | tf_op jit(solution)/shard_map/requests/pallas_call | solution.py:298
  3.3 14.6 %all-to-all-start = ((f32[64,1,128]{2,1,0:T(1,128)}), f32[64,1,128]{2,1,0:T(1,128)S(1)}, u32[]{:S(2)}, u32[]{:S(2)}) async-start(f32[64,1,128]{2,1,0:T(1,128)} %bitcast.2), calls=%async_computation | async-start | bytes 65536 | tf_op jit(solution)/shard_map/requests/all_to_all | solution.py:299
  17.9 0.0 copy-start
  18.0 2.1 %copy-done = f32[128,7552]{1,0:T(8,128)S(1)} copy-done((f32[128,7552]{1,0:T(8,128)S(1)}, f32[128,7552]{1,0:T(8,128)}, u32[]{:S(2)}) %copy-start) | copy-done | bytes 3866648
  20.0 0.0 copy-start.1
  20.0 1.2 %copy-done.1 = f32[32,7552]{1,0:T(8,128)S(1)} copy-done((f32[32,7552]{1,0:T(8,128)S(1)}, f32[32,7552]{1,0:T(8,128)}, u32[]{:S(2)}) %copy-start.1) | copy-done | bytes 966680
  21.2 3.2 %flows.1 = (bf16[256,7552]{1,0:T(8,128)(2,1)S(1)}, f32[32,128]{1,0:T(8,128)S(1)}) custom-call(f32[128,7552]{1,0:T(8,128)S(1)} %copy-done, f32[32,7552]{1,0:T(8,128)S(1)} %copy-done.1), custom_call_target="tpu_custom_call" | custom-call | flops 247463936 | bytes 11599872 | tf_op jit(solution)/shard_map/flows/pallas_call | solution.py:301
  24.5 0.0 copy-start.6
  24.5 1.8 %copy-done.6 = bf16[256,7552]{1,0:T(8,128)(2,1)} copy-done((bf16[256,7552]{1,0:T(8,128)(2,1)}, bf16[256,7552]{1,0:T(8,128)(2,1)S(1)}, u32[]{:S(2)}) %copy-start.6) | copy-done | bytes 3866648
  26.3 1.2 %all-to-all-done = f32[64,1,128]{2,1,0:T(1,128)S(1)} async-done(((f32[64,1,128]{2,1,0:T(1,128)}), f32[64,1,128]{2,1,0:T(1,128)S(1)}, u32[]{:S(2)}, u32[]{:S(2)}) %all-to-all-start) | async-done | bytes 32800 | tf_op jit(solution)/shard_map/requests/all_to_all | solution.py:299
  27.5 0.0 copy-start.7
  27.5 2.1 %copy-done.7 = bf16[256,7552]{1,0:T(8,128)(2,1)S(1)} copy-done((bf16[256,7552]{1,0:T(8,128)(2,1)S(1)}, bf16[256,7552]{1,0:T(8,128)(2,1)}, u32[]{:S(2)}) %copy-start.7) | copy-done | bytes 3866648
  29.6 0.0 copy-start.4
  29.6 7.4 %picks.1 = f32[8,24,768]{2,1,0:T(8,128)S(1)} custom-call(f32[64,128]{1,0:T(8,128)S(1)} %bitcast.15, bf16[256,7552]{1,0:T(8,128)(2,1)S(1)} %copy-done.7, f32[32,128]{1,0:T(8,128)S(1)} %get-tuple-element.8.part_ref), custom_call_target="tpu_custom_call" | custom-call | flops 2969567232 | bytes 3866624 | tf_op jit(solution)/shard_map/picks/pallas_call | solution.py:308
  37.0 0.0 copy-start.3
  37.0 0.0 copy-start.5
  37.0 24.5 %all_to_all.27.got_ref = f32[8,24,768]{2,1,0:T(8,128)S(1)} all-to-all(f32[8,24,768]{2,1,0:T(8,128)S(1)} %picks.1), channel_id=1, replica_groups=mesh['line'=64,'bus'=8] {'bus'}, dimensions={0} | all-to-all | bytes 1179648 | tf_op jit(solution)/shard_map/picks/all_to_all | solution.py:319
  61.5 0.0 copy-done.4
  61.5 0.3 reply.1
  61.9 0.3 copy.15
  62.2 28.2 %all_to_all.28 = f32[64,1,1152]{2,1,0:T(1,128)S(1)} all-to-all(f32[64,1,1152]{2,1,0:T(1,128)S(1)} %copy.15), channel_id=1, replica_groups=mesh['line'=64,'bus'=8] {'line'}, dimensions={0} | all-to-all | bytes 589824 | tf_op jit(solution)/shard_map/reply/all_to_all | solution.py:324
  90.4 0.0 copy-done.3
  90.5 0.0 copy-done.5
  90.5 0.7 screen.1
  91.1 0.8 copy.17
  (1 shorter events, 0.0 us)
Async XLA Ops:
  1.5 0.7 copy-start.2
  3.3 24.2 %all-to-all-start = ((f32[64,1,128]{2,1,0:T(1,128)}), f32[64,1,128]{2,1,0:T(1,128)S(1)}, u32[]{:S(2)}, u32[]{:S(2)}) async-start(f32[64,1,128]{2,1,0:T(1,128)} %bitcast.2), calls=%async_computation | async-start | bytes 65536 | tf_op jit(solution)/shard_map/requests/all_to_all | solution.py:299
  17.9 2.1 %copy-start = (f32[128,7552]{1,0:T(8,128)S(1)}, f32[128,7552]{1,0:T(8,128)}, u32[]{:S(2)}) copy-start(f32[128,7552]{1,0:T(8,128)} %s_ref.1) | copy-start | bytes 11599876
  20.0 1.2 %copy-start.1 = (f32[32,7552]{1,0:T(8,128)S(1)}, f32[32,7552]{1,0:T(8,128)}, u32[]{:S(2)}) copy-start(f32[32,7552]{1,0:T(8,128)} %inj_ref.1) | copy-start | bytes 2899972
  24.5 1.9 %copy-start.6 = (bf16[256,7552]{1,0:T(8,128)(2,1)}, bf16[256,7552]{1,0:T(8,128)(2,1)S(1)}, u32[]{:S(2)}) copy-start(bf16[256,7552]{1,0:T(8,128)(2,1)S(1)} %get-tuple-element.7.split_ref) | copy-start | bytes 11599876
  27.5 2.1 %copy-start.7 = (bf16[256,7552]{1,0:T(8,128)(2,1)S(1)}, bf16[256,7552]{1,0:T(8,128)(2,1)}, u32[]{:S(2)}) copy-start(bf16[256,7552]{1,0:T(8,128)(2,1)} %copy-done.6) | copy-start | bytes 11599876
  29.6 31.9 %copy-start.4 = (f32[128]{0:T(128)S(1)}, f32[128]{0:T(128)}, u32[]{:S(2)}) copy-start(f32[128]{0:T(128)} %param.9) | copy-start | bytes 1540
  37.0 53.4 %copy-start.3 = (s32[64]{0:T(128)S(1)}, s32[64]{0:T(128)}, u32[]{:S(2)}) copy-start(s32[64]{0:T(128)} %param.12) | copy-start | bytes 772
  37.0 53.4 %copy-start.5 = (s32[64]{0:T(128)S(1)}, s32[64]{0:T(128)}, u32[]{:S(2)}) copy-start(s32[64]{0:T(128)} %param.11) | copy-start | bytes 772

commit v2 on v1

--- a/solution.py
+++ b/solution.py
@@ -1,5 +1,3 @@
-import functools
-
 import jax
 import jax.numpy as jnp
 from jax import lax
@@ -11,10 +9,12 @@
 F32 = jnp.float32
 BF16 = jnp.bfloat16
 NT = (((1,), (1,)), ((), ()))
-TN = (((0,), (0,)), ((), ()))
+NN = (((1,), (0,)), ((), ()))
 HOURS = 32
 CAP = 12
-CHUNK = 512
+CHUNK = 1920
+PEERS = 4
+PASS = 2
 
 
 def iota(shape, axis):
@@ -27,64 +27,47 @@
 
 
 def request_kernel(mon_ref, ends_ref, off_ref, out_ref):
-    outages, slots = mon_ref.shape
-    lane = iota((outages, 128), 1)
-    names = jnp.zeros((outages, 128), F32)
+    slots, outages = mon_ref.shape
+    lines = out_ref.shape[0]
+
+    def twice(row):
+        return jnp.concatenate([row, row], axis=1)
+
+    named = twice(mon_ref[...])
+    line_row = iota((lines, 128), 0)
+    names = jnp.zeros((lines, 128), F32)
     for s in range(slots):
-        names = jnp.where(mon_ref[:, s : s + 1] == lane, 1.0, names)
-    before = jnp.where(iota((outages, outages), 1) < iota((outages, outages), 0), 1.0, 0.0)
+        names = jnp.where(named[s : s + 1] == line_row, 1.0, names)
+    earlier = iota((128, 128), 0) < iota((128, 128), 1) % outages
     rank = lax.dot_general(
-        before.astype(BF16), names.astype(BF16), (((1,), (0,)), ((), ())), preferred_element_type=F32
-    )
-    square_row, square_lane = iota((outages, outages), 0), iota((outages, outages), 1)
-    off = jnp.sum(jnp.where(square_row == square_lane, off_ref[...], 0), axis=1, keepdims=True)
-    ones = jnp.ones((outages, 128), jnp.int32)
-    start = (ends_ref[:, 0:1] + 1) * ones
-    end = (ends_ref[:, 1:2] + 1) * ones
-    place = (off + 1) * ones
-    chosen, values = [], []
-    for c in range(CAP):
-        chosen.append(jnp.where(rank == float(c), names, 0.0).astype(BF16))
-        value = jnp.where(lane == c, start, jnp.where(lane == 16 + c, end, jnp.where(lane == 32 + c, place, 0)))
-        values.append(
-            jnp.concatenate([(value >> 8).astype(F32), (value & 255).astype(F32)], axis=1).astype(BF16)
-        )
-    both = lax.dot_general(
-        jnp.concatenate(chosen, axis=0), jnp.concatenate(values, axis=0), TN, preferred_element_type=F32
-    )
-    packed = 256.0 * both[:, :128] + both[:, 128:]
-    out_ref[...] = packed[: out_ref.shape[0]]
-
-
-def flow_kernel(s_ref, inj_ref, split_ref, part_ref):
+        names.astype(BF16), jnp.where(earlier, 1.0, 0.0).astype(BF16), NN, preferred_element_type=F32
+    )
+    rank = jnp.where(names > 0.0, rank, -1.0)
+    start = twice(ends_ref[0:1, :]) + 1
+    end = twice(ends_ref[1:2, :]) + 1
+    place = twice(off_ref[...]) + 1
+    second = iota((1, 128), 1) // outages
+    spot = iota((128, 128), 0)
+    chosen, high, low = [], [], []
+    for t in range(CAP // 2):
+        turn = 2 * t + second
+        chosen.append(jnp.where(rank == turn.astype(F32), 1.0, 0.0).astype(BF16))
+        value = jnp.where(
+            spot == turn, start, jnp.where(spot == 16 + turn, end, jnp.where(spot == 32 + turn, place, 0))
+        )
+        high.append((value >> 8).astype(F32).astype(BF16))
+        low.append((value & 255).astype(F32).astype(BF16))
+    chosen = jnp.concatenate(chosen, axis=1)
+    high = lax.dot_general(chosen, jnp.concatenate(high, axis=1), NT, preferred_element_type=F32)
+    low = lax.dot_general(chosen, jnp.concatenate(low, axis=1), NT, preferred_element_type=F32)
+    out_ref[...] = 256.0 * high + low
+
+
+def pick_kernel(req_ref, s_ref, inj_ref, out_ref, from_ref, to_ref, sum_ref, flow_ref):
+    lines = req_ref.shape[0]
     rows, width = s_ref.shape
-    total = jnp.zeros((2 * HOURS, 2 * rows), F32)
-
-    def step(at, size, total):
-        cols = pl.ds(at, size)
-        s_high, s_low = split2(s_ref[:, cols])
-        both = jnp.concatenate([s_high, s_low], axis=0)
-        split_ref[:, cols] = both
-        i_high, i_low = split2(inj_ref[:, cols])
-        return total + lax.dot_general(
-            jnp.concatenate([i_high, i_low], axis=0), both, NT, preferred_element_type=F32
-        )
-
-    whole = width // CHUNK
-    total = lax.fori_loop(0, whole, lambda q, t: step(pl.multiple_of(q * CHUNK, CHUNK), CHUNK, t), total)
-    if width % CHUNK:
-        total = step(whole * CHUNK, width % CHUNK, total)
-    part_ref[...] = (
-        total[:HOURS, :rows] + (total[:HOURS, rows:] + total[HOURS:, :rows]) + total[HOURS:, rows:]
-    )
-
-
-def pick_kernel(req_ref, split_ref, part_ref, out_ref, from_ref, to_ref, sum_ref):
-    lines = req_ref.shape[0]
-    both_rows, width = split_ref.shape
-    rows = both_rows // 2
-    buses, _, entries = out_ref.shape
-    sub = rows // buses
+    peers, _, entries = out_ref.shape
+    deep = rows // peers
     base = lax.axis_index("bus") * width + 1
     req = req_ref[...]
     lane = iota((lines, 128), 1)
@@ -92,20 +75,31 @@
         first = req[:, c : c + 1].astype(jnp.int32) - base
         second = req[:, 16 + c : 17 + c].astype(jnp.int32) - base
         same = first == second
-        first = jnp.where(same, -1, first)
-        second = jnp.where(same, -1, second)
-        from_ref[c * lines : (c + 1) * lines, :] = jnp.broadcast_to(first, (lines, 128))
-        to_ref[c * lines : (c + 1) * lines, :] = jnp.broadcast_to(second, (lines, 128))
+        first = jnp.where(same | (first < 0) | (first >= width), -1, first)
+        second = jnp.where(same | (second < 0) | (second >= width), -1, second)
+        from_ref[c * lines : (c + 1) * lines, :] = jnp.broadcast_to(first, (lines, 128)).astype(jnp.int16)
+        to_ref[c * lines : (c + 1) * lines, :] = jnp.broadcast_to(second, (lines, 128)).astype(jnp.int16)
     sum_ref[...] = jnp.zeros_like(sum_ref)
+    flow_ref[...] = jnp.zeros_like(flow_ref)
+    one, minus, zero = jnp.asarray(1, BF16), jnp.asarray(-1, BF16), jnp.asarray(0, BF16)
 
     def step(at, size):
         columns = []
         for t in range(size // 128):
-            spot = iota((entries, 128), 1) + (at + t * 128)
-            hot = jnp.where(from_ref[...] == spot, 1.0, jnp.where(to_ref[...] == spot, -1.0, 0.0))
-            columns.append(hot.astype(BF16))
+            spot = (iota((16, 128), 1) + (at + t * 128)).astype(jnp.int16)
+            spot = jnp.broadcast_to(spot[None], (entries // 16, 16, 128)).reshape(entries, 128)
+            columns.append(
+                jnp.where(from_ref[...] == spot, one, jnp.where(to_ref[...] == spot, minus, zero))
+            )
+        cols = pl.ds(at, size)
+        s_high, s_low = split2(s_ref[:, cols])
+        both = jnp.concatenate([s_high, s_low], axis=0)
+        i_high, i_low = split2(inj_ref[:, cols])
         sum_ref[...] += lax.dot_general(
-            jnp.concatenate(columns, axis=1), split_ref[:, pl.ds(at, size)], NT, preferred_element_type=F32
+            jnp.concatenate(columns, axis=1), both, NT, preferred_element_type=F32
+        )
+        flow_ref[...] += lax.dot_general(
+            jnp.concatenate([i_high, i_low], axis=0), both, NT, preferred_element_type=F32
         )
 
     whole = width // CHUNK
@@ -117,6 +111,11 @@
     lax.fori_loop(0, whole, body, 0)
     if width % CHUNK:
         step(whole * CHUNK, width % CHUNK)
+    part = (
+        flow_ref[:HOURS, :rows]
+        + (flow_ref[:HOURS, rows:] + flow_ref[HOURS:, :rows])
+        + flow_ref[HOURS:, rows:]
+    )
     picked = sum_ref[:, :rows] + sum_ref[:, rows:]
     own = jnp.zeros((lines, 128), F32)
     for c in range(CAP):
@@ -127,23 +126,31 @@
         own = jnp.where(lane == c, value, own)
     turned = jnp.transpose(picked)
     own_turned = jnp.transpose(jnp.concatenate([own, jnp.zeros((128 - lines, 128), F32)], axis=0))
-    part = part_ref[...]
     extra = jnp.concatenate(
         [part[8 * t : 8 * t + 8] for t in range(4)] + [own_turned[0:8], own_turned[8:16]], axis=1
     )
-    for b in range(buses):
-        out_ref[b, :sub, :] = turned[b * sub : (b + 1) * sub]
-        out_ref[b, sub:, :] = extra
+    for b in range(peers):
+        out_ref[b, :deep, :] = turned[b * deep : (b + 1) * deep]
+        out_ref[b, deep:, :] = extra
+
+
+def sum_kernel(got_ref, out_ref):
+    peers, deep, _ = out_ref.shape
+    rows = deep - 8
+    total = got_ref[0]
+    for b in range(1, got_ref.shape[0]):
+        total = total + got_ref[b]
+    for b in range(peers):
+        out_ref[b, :rows, :] = total[b * rows : (b + 1) * rows]
+        out_ref[b, rows:, :] = total[peers * rows :]
 
 
 def reply_kernel(got_ref, req_ref, rate_ref, out_ref, rate_scratch):
-    buses, _, _ = got_ref.shape
+    sub = got_ref.shape[1] - 8
     lines = req_ref.shape[0]
-    rows = rate_ref.shape[1]
-    sub = rows // buses
     place = lax.axis_index("bus")
     total = got_ref[0]
-    for b in range(1, buses):
+    for b in range(1, got_ref.shape[0]):
         total = total + got_ref[b]
     flows = jnp.concatenate([total[sub : sub + 8, 128 * t : 128 * t + 128] for t in range(4)], axis=0)
     lane = iota((HOURS, 128), 1)
@@ -201,7 +208,7 @@
 
 def screen_kernel(got_ref, mon_ref, off_ref, live_ref, out_ref):
     lines = got_ref.shape[0]
-    outages, slots = mon_ref.shape
+    slots, outages = mon_ref.shape
     sub = out_ref.shape[1]
     place = lax.axis_index("bus")
     pieces = []
@@ -212,8 +219,7 @@
         pieces.append(jnp.transpose(jnp.concatenate([high, low], axis=0)).astype(BF16))
     shared = jnp.concatenate(pieces[:4] + pieces[7:], axis=0)
     own = jnp.concatenate(pieces[4:7] + pieces[8:], axis=0)
-    mon = jnp.concatenate([mon_ref[...].astype(F32), jnp.zeros((outages, 128 - slots), F32)], axis=1)
-    named = jnp.transpose(jnp.concatenate([mon, mon], axis=0))[:slots].astype(jnp.int32)
+    named = jnp.concatenate([mon_ref[...], mon_ref[...]], axis=1)
     line_row = iota((lines, 128), 0)
     lane = iota((1, 128), 1)
     outage = lane % outages
@@ -265,9 +271,8 @@
         if t == 0:
             keep = keep & ~((slot == 0) & (row == off - place * sub))
         result = jnp.where(keep, result, 0.0)
-        turned = jnp.transpose(jnp.concatenate([result, jnp.zeros((128 - sub, 128), F32)], axis=0))
-        out_ref[pl.ds(2 * t, outages, stride=slots), :] = turned[:outages, :sub]
-        out_ref[pl.ds(2 * t + 1, outages, stride=slots), :] = turned[outages:, :sub]
+        out_ref[2 * t] = result[:, :outages]
+        out_ref[2 * t + 1] = result[:, outages:]
 
 
 def call(kernel, out_shape, scratch=(), flops=0, moved=0):
@@ -291,42 +296,42 @@
     outages, slot_count = monitored.shape
     entries = CAP * line_count
     shape = jax.ShapeDtypeStruct
+    groups_x = [[first + other * PASS for other in range(PEERS)] for first in range(PASS)]
+    groups_z = [[PASS * first + other for other in range(PASS)] for first in range(PEERS)]
     off_row = outage_offset.reshape(1, outages)
     live_row = live_count.reshape(1, outages)
     rate_row = rating.reshape(1, block_rows)
+    named = monitored.T
     with jax.named_scope("requests"):
-        requests = call(request_kernel, shape((line_count, 128), F32))(monitored, outage_ends, off_row)
+        requests = call(request_kernel, shape((line_count, 128), F32))(named, outage_ends.T, off_row)
         asked = lax.all_to_all(requests, "line", split_axis=0, concat_axis=0, tiled=True)
-    with jax.named_scope("flows"):
-        split, part = call(
-            flow_kernel,
-            (shape((2 * block_rows, bus_width), BF16), shape((HOURS, block_rows), F32)),
-            flops=8 * HOURS * block_rows * bus_width,
-            moved=3 * 4 * block_rows * bus_width,
-        )(shift_factors, injection)
     with jax.named_scope("picks"):
         partial_sens = call(
             pick_kernel,
-            shape((bus_count, sub_rows + 8, entries), F32),
+            shape((PEERS, PASS * sub_rows + 8, entries), F32),
             scratch=(
-                pltpu.VMEM((entries, 128), jnp.int32),
-                pltpu.VMEM((entries, 128), jnp.int32),
+                pltpu.VMEM((entries, 128), jnp.int16),
+                pltpu.VMEM((entries, 128), jnp.int16),
                 pltpu.VMEM((entries, 2 * block_rows), F32),
+                pltpu.VMEM((2 * HOURS, 2 * block_rows), F32),
             ),
             flops=4 * entries * block_rows * bus_width,
             moved=4 * block_rows * bus_width,
-        )(asked, split, part)
-        sens = lax.all_to_all(partial_sens, "bus", split_axis=0, concat_axis=0, tiled=True)
+        )(asked, shift_factors, injection)
+        partial_sens = lax.all_to_all(
+            partial_sens, "bus", split_axis=0, concat_axis=0, tiled=True, axis_index_groups=groups_x
+        )
+    with jax.named_scope("sums"):
+        half = call(sum_kernel, shape((PASS, sub_rows + 8, entries), F32))(partial_sens)
+        sens = lax.all_to_all(half, "bus", split_axis=0, concat_axis=0, tiled=True, axis_index_groups=groups_z)
     with jax.named_scope("reply"):
         reply = call(reply_kernel, shape((line_count, 1152), F32), scratch=(pltpu.VMEM((128, 128), F32),))(
             sens, asked, rate_row
         )
         got = lax.all_to_all(reply, "line", split_axis=0, concat_axis=0, tiled=True)
     with jax.named_scope("screen"):
-        loading = call(screen_kernel, shape((outages * slot_count, sub_rows), F32))(
-            got, monitored, off_row, live_row
-        )
-    return loading.reshape(outages, slot_count, sub_rows)
+        loading = call(screen_kernel, shape((slot_count, sub_rows, outages), F32))(got, named, off_row, live_row)
+    return jnp.transpose(loading, (2, 0, 1))
 
 
 def solution(mesh):

time: 92.3 us -> 84.7 us (0.918)
  blocking collectives: 52.7 us -> 70.5 us
  starting transfers between devices: 14.6 us -> 0 us
  local copies, waits for them, and re-layouts: 10.5 us -> 5.66 us
  Pallas kernels: 12.8 us -> 8.07 us
  waiting for transfers between devices: 1.19 us -> 0 us
    all_to_all x1 -> x3, blocking collectives: 24.5 us -> 51.5 us  [the longest x1 24 us: local(): lax.all_to_all(requests, 'line', split_axis=0, concat_axis=0, tiled=True)]
    all_to_all x1 -> x0, starting transfers between devices: 14.6 us -> none  [local(): lax.all_to_all(requests, 'line', split_axis=0, concat_axis=0, tiled=True)]
    all_to_all x1, blocking collectives: 28.2 us -> 19 us  [local(): got = lax.all_to_all(reply, 'line', split_axis=0, concat_axis=0, tiled=True)]
    unnamed x19, local copies, waits for them, and re-layouts: 9.45 us -> 5.35 us
    pallas_call x3, Pallas kernels: 11.3 us -> 7.3 us  [the longest x1 6.04 us: local(): call(pick_kernel, shape((PEERS, PASS * sub_rows + 8, entries), F32), scra...]
    all_to_all x1 -> x0, waiting for transfers between devices: 1.19 us -> none  [local(): lax.all_to_all(requests, 'line', split_axis=0, concat_axis=0, tiled=True)]
  transfers between devices with their start and end apart: 1 -> 0, of which waited for: 1 -> 0; matrix products, arithmetic and copies ran while one was open for 0% -> 0% of each run, Pallas kernels for 4% -> 0%
where the time goes in v2:
time: 84.7 us; the launch traced here: 84.3 us
  blocking collectives  70.5 us (83%)
  Pallas kernels  8.07 us (10%)
  local copies, waits for them, and re-layouts  5.66 us (7%)
    all_to_all x1, blocking collectives, local(): lax.all_to_all(requests, 'line', split_axis=0, concat_axis=0, tiled=True)  24 us
    all_to_all x1, blocking collectives, local(): got = lax.all_to_all(reply, 'line', split_axis=0, concat_axis=0, tiled=True)  19 us
    all_to_all x1, blocking collectives, local(): lax.all_to_all(half, 'bus', split_axis=0, concat_axis=0, tiled=True, axis...  15.3 us
    all_to_all x1, blocking collectives, local(): lax.all_to_all(partial_sens, 'bus', split_axis=0, concat_axis=0, tiled=Tr...  12.2 us
    pallas_call x1, Pallas kernels, local(): call(pick_kernel, shape((PEERS, PASS * sub_rows + 8, entries), F32), scra...  6.04 us
    unnamed x19, local copies, waits for them, and re-layouts  5.35 us

profile of v2, /device:TPU:1, one launch (start us, length us, event | category | flops | bytes accessed | tf_op | source)
XLA Modules:
  0.0 84.3 jit_solution(16039435512081911040)
XLA Ops:
  0.0 0.0 copy-start
  0.0 0.7 copy-done
  0.7 0.0 copy-start.2
  0.7 0.7 copy-done.2
  1.3 0.0 copy-start.4
  1.3 0.7 copy-done.4
  2.0 0.4 requests.1
  2.5 24.0 %all_to_all.32 = f32[64,1,128]{2,1,0:T(1,128)S(1)} all-to-all(f32[64,1,128]{2,1,0:T(1,128)S(1)} %bitcast.18), channel_id=1, replica_groups=mesh['line'=64,'bus'=8] {'line'}, dimensions={0} | all-to-all | bytes 65536 | tf_op jit(solution)/shard_map/requests/all_to_all | solution.py:307
  26.5 0.0 copy-start.7
  26.5 2.1 %copy-done.7 = f32[128,7552]{1,0:T(8,128)S(1)} copy-done((f32[128,7552]{1,0:T(8,128)S(1)}, f32[128,7552]{1,0:T(8,128)}, u32[]{:S(2)}) %copy-start.7) | copy-done | bytes 3866648
  28.6 0.0 copy-start.8
  28.6 1.2 %copy-done.8 = f32[32,7552]{1,0:T(8,128)S(1)} copy-done((f32[32,7552]{1,0:T(8,128)S(1)}, f32[32,7552]{1,0:T(8,128)}, u32[]{:S(2)}) %copy-start.8) | copy-done | bytes 966680
  29.8 0.0 copy-start.5
  29.8 6.0 %picks.1 = f32[4,40,768]{2,1,0:T(8,128)S(1)} custom-call(f32[64,128]{1,0:T(8,128)S(1)} %bitcast.16, f32[128,7552]{1,0:T(8,128)S(1)} %copy-done.7, f32[32,7552]{1,0:T(8,128)S(1)} %copy-done.8), custom_call_target="tpu_custom_call" | custom-call | flops 2969567232 | bytes 3866624 | tf_op jit(solution)/shard_map/picks/pallas_call | solution.py:309
  35.8 0.0 copy-start.1
  35.8 0.0 copy-start.3
  35.8 0.0 copy-start.6
  35.8 12.2 %all_to_all.33.got_ref = f32[4,40,768]{2,1,0:T(8,128)S(1)} all-to-all(f32[4,40,768]{2,1,0:T(8,128)S(1)} %picks.1), channel_id=1, replica_groups={{0,2,4,6},{1,3,5,7},{8,10,12,14},{9,11,13,15},{16,18,20,22},{17,19,21,2..., dimensions={0} | all-to-all | bytes 983040 | tf_op jit(solution)/shard_map/picks/all_to_all | solution.py:321
  48.1 15.3 %all_to_all.34.got_ref = f32[2,24,768]{2,1,0:T(8,128)S(1)} all-to-all(f32[2,24,768]{2,1,0:T(8,128)S(1)} %sums.1), channel_id=1, replica_groups={{0,1},{2,3},{4,5},{6,7},{8,9},{10,11},{12,13},{14,15},{16,17},{18,19},{..., dimensions={0} | all-to-all | bytes 294912 | tf_op jit(solution)/shard_map/sums/all_to_all | solution.py:326
  63.4 0.0 copy-done.5
  63.4 0.3 reply.1
  63.7 0.3 copy.9
  64.1 19.0 %all_to_all.35 = f32[64,1,1152]{2,1,0:T(1,128)S(1)} all-to-all(f32[64,1,1152]{2,1,0:T(1,128)S(1)} %copy.9), channel_id=1, replica_groups=mesh['line'=64,'bus'=8] {'line'}, dimensions={0} | all-to-all | bytes 589824 | tf_op jit(solution)/shard_map/reply/all_to_all | solution.py:331
  83.1 0.0 copy-done.1
  83.1 0.0 copy-done.3
  83.1 0.0 copy-done.6
  83.1 1.2 %screen.1 = f32[8,16,64]{2,1,0:T(8,128)} custom-call(f32[64,1152]{1,0:T(8,128)S(1)} %bitcast.15, s32[8,64]{1,0:T(8,128)S(1)} %bitcast.20, s32[1,64]{1,0:T(1,128)S(1)} %bitcast.22, s32[1,64]{1,0:T(1,128)S(1)} %bitcast.25), custom_call_target="tpu_custom_call" | custom-call | tf_op jit(solution)/shard_map/screen/pallas_call | solution.py:333
  (2 shorter events, 0.0 us)
Async XLA Ops:
  0.0 0.7 copy-start
  0.7 0.7 copy-start.2
  1.3 0.7 copy-start.4
  26.5 2.1 %copy-start.7 = (f32[128,7552]{1,0:T(8,128)S(1)}, f32[128,7552]{1,0:T(8,128)}, u32[]{:S(2)}) copy-start(f32[128,7552]{1,0:T(8,128)} %s_ref.1) | copy-start | bytes 11599876
  28.6 1.2 %copy-start.8 = (f32[32,7552]{1,0:T(8,128)S(1)}, f32[32,7552]{1,0:T(8,128)}, u32[]{:S(2)}) copy-start(f32[32,7552]{1,0:T(8,128)} %inj_ref.1) | copy-start | bytes 2899972
  29.8 33.6 %copy-start.5 = (f32[128]{0:T(128)S(1)}, f32[128]{0:T(128)}, u32[]{:S(2)}) copy-start(f32[128]{0:T(128)} %param.9) | copy-start | bytes 1540
  35.8 47.2 %copy-start.1 = (s32[64,8]{0,1:T(8,128)S(1)}, s32[64,8]{0,1:T(8,128)}, u32[]{:S(2)}) copy-start(s32[64,8]{0,1:T(8,128)} %param.10) | copy-start | bytes 6148
  35.8 47.3 %copy-start.3 = (s32[64]{0:T(128)S(1)}, s32[64]{0:T(128)}, u32[]{:S(2)}) copy-start(s32[64]{0:T(128)} %param.12) | copy-start | bytes 772
  35.8 47.2 %copy-start.6 = (s32[64]{0:T(128)S(1)}, s32[64]{0:T(128)}, u32[]{:S(2)}) copy-start(s32[64]{0:T(128)} %param.11) | copy-start | bytes 772

commit v3 on v2

--- a/solution.py
+++ b/solution.py
@@ -13,8 +13,9 @@
 HOURS = 32
 CAP = 12
 CHUNK = 1920
-PEERS = 4
 PASS = 2
+IN_VMEM = pl.BlockSpec(memory_space=pltpu.VMEM)
+IN_PLACE = pl.BlockSpec(memory_space=pl.ANY)
 
 
 def iota(shape, axis):
@@ -63,12 +64,28 @@
     out_ref[...] = 256.0 * high + low
 
 
-def pick_kernel(req_ref, s_ref, inj_ref, out_ref, from_ref, to_ref, sum_ref, flow_ref):
+def pick_kernel(
+    req_ref, s_hbm, inj_hbm, out_ref, s_ref, inj_ref, from_ref, to_ref, sum_ref, flow_ref, s_sems, inj_sem
+):
     lines = req_ref.shape[0]
     rows, width = s_ref.shape
     peers, _, entries = out_ref.shape
     deep = rows // peers
-    base = lax.axis_index("bus") * width + 1
+    whole, rest = width // CHUNK, width % CHUNK
+
+    def copy(at, size, q):
+        cols = pl.ds(at, size)
+        return pltpu.make_async_copy(s_hbm.at[:, cols], s_ref.at[:, cols], s_sems.at[q])
+
+    inj_copy = pltpu.make_async_copy(inj_hbm, inj_ref, inj_sem)
+    for q in range(whole):
+        copy(q * CHUNK, CHUNK, q).start()
+        if q == 0:
+            inj_copy.start()
+    if rest:
+        copy(whole * CHUNK, rest, whole).start()
+    bus = lax.axis_index("bus_x") * lax.axis_size("bus_z") + lax.axis_index("bus_z")
+    base = bus * width + 1
     req = req_ref[...]
     lane = iota((lines, 128), 1)
     for c in range(CAP):
@@ -102,15 +119,18 @@
             jnp.concatenate([i_high, i_low], axis=0), both, NT, preferred_element_type=F32
         )
 
-    whole = width // CHUNK
+    inj_copy.wait()
 
     def body(q, carry):
-        step(pl.multiple_of(q * CHUNK, CHUNK), CHUNK)
+        at = pl.multiple_of(q * CHUNK, CHUNK)
+        copy(at, CHUNK, q).wait()
+        step(at, CHUNK)
         return carry
 
     lax.fori_loop(0, whole, body, 0)
-    if width % CHUNK:
-        step(whole * CHUNK, width % CHUNK)
+    if rest:
+        copy(whole * CHUNK, rest, whole).wait()
+        step(whole * CHUNK, rest)
     part = (
         flow_ref[:HOURS, :rows]
         + (flow_ref[:HOURS, rows:] + flow_ref[HOURS:, :rows])
@@ -134,42 +154,23 @@
         out_ref[b, deep:, :] = extra
 
 
-def sum_kernel(got_ref, out_ref):
-    peers, deep, _ = out_ref.shape
-    rows = deep - 8
+def reply_kernel(got_ref, req_ref, rate_ref, out_ref, rate_scratch):
+    peers = got_ref.shape[0]
+    lines = req_ref.shape[0]
+    rows = rate_ref.shape[1]
+    passes = out_ref.shape[0] // lines
+    sub = (got_ref.shape[1] - 8) // passes
+    place = lax.axis_index("bus_x") * passes
     total = got_ref[0]
-    for b in range(1, got_ref.shape[0]):
+    for b in range(1, peers):
         total = total + got_ref[b]
-    for b in range(peers):
-        out_ref[b, :rows, :] = total[b * rows : (b + 1) * rows]
-        out_ref[b, rows:, :] = total[peers * rows :]
-
-
-def reply_kernel(got_ref, req_ref, rate_ref, out_ref, rate_scratch):
-    sub = got_ref.shape[1] - 8
-    lines = req_ref.shape[0]
-    place = lax.axis_index("bus")
-    total = got_ref[0]
-    for b in range(1, got_ref.shape[0]):
-        total = total + got_ref[b]
-    flows = jnp.concatenate([total[sub : sub + 8, 128 * t : 128 * t + 128] for t in range(4)], axis=0)
+    sens, rest = total[: passes * sub], total[passes * sub :]
+    flows = jnp.concatenate([rest[:, 128 * t : 128 * t + 128] for t in range(4)], axis=0)
     lane = iota((HOURS, 128), 1)
     hour = iota((HOURS, 128), 0)
-    wanted = iota((128, 128), 0) == place * sub + iota((128, 128), 1) % sub
-    select = jnp.where(wanted, 1.0, 0.0).astype(BF16)
     f_high, f_low = split2(flows)
     f_rest = (flows - f_high.astype(F32) - f_low.astype(F32)).astype(BF16)
-    spread = lax.dot_general(
-        jnp.concatenate([f_high, f_low, f_rest], axis=0),
-        select,
-        (((1,), (0,)), ((), ())),
-        preferred_element_type=F32,
-    )
-    spread = spread[:HOURS] + spread[HOURS : 2 * HOURS] + spread[2 * HOURS :]
-    spread = jnp.where(lane // sub == hour % 8, spread, 0.0)
-    for t in range(4):
-        row = jnp.sum(spread[8 * t : 8 * t + 8], axis=0, keepdims=True)
-        out_ref[:, 128 * t : 128 * t + 128] = jnp.broadcast_to(row, (lines, 128))
+    f_all = jnp.concatenate([f_high, f_low, f_rest], axis=0)
     req = req_ref[...]
     lane_line = iota((lines, 128), 1)
     hots = [
@@ -187,33 +188,44 @@
     lost = lax.dot_general(
         left, diagonal(f_high), NT, preferred_element_type=F32
     ) + lax.dot_general(left, diagonal(f_low), NT, preferred_element_type=F32)
-    for q in range(3):
-        out_ref[:, 512 + 128 * q : 640 + 128 * q] = lost[q * lines : (q + 1) * lines]
-    rate_scratch[...] = jnp.transpose(jnp.broadcast_to(rate_ref[...], (128, 128)))
-    rate = rate_scratch[pl.ds(pl.multiple_of(place * sub, sub), sub), :]
-    sens = total[:sub]
+    rate_scratch[...] = 0.5 * jnp.transpose(jnp.broadcast_to(rate_ref[...], (rows, 128)))
 
     def wide(block):
         return jnp.concatenate([block, jnp.zeros((block.shape[0], 128 - lines), F32)], axis=1)
 
-    blocks = [wide(sens[:, c * lines : (c + 1) * lines]) for c in range(CAP)]
-    one = jnp.concatenate(blocks[:8], axis=0)
-    two = jnp.concatenate(
-        blocks[8:] + [total[sub : sub + 8, 512:640], total[sub : sub + 8, 640:768], rate, jnp.zeros((32, 128), F32)],
-        axis=0,
-    )
-    out_ref[:, 896:1024] = jnp.transpose(one)[:lines]
-    out_ref[:, 1024:1152] = jnp.transpose(two)[:lines]
+    for p in range(passes):
+        at = slice(p * lines, (p + 1) * lines)
+        wanted = iota((128, 128), 0) == (place + p) * sub + iota((128, 128), 1) % sub
+        spread = lax.dot_general(f_all, jnp.where(wanted, 1.0, 0.0).astype(BF16), NN, preferred_element_type=F32)
+        spread = spread[:HOURS] + spread[HOURS : 2 * HOURS] + spread[2 * HOURS :]
+        spread = jnp.where(lane // sub == hour % 8, spread, 0.0)
+        for t in range(4):
+            row = jnp.sum(spread[8 * t : 8 * t + 8], axis=0, keepdims=True)
+            out_ref[at, 128 * t : 128 * t + 128] = jnp.broadcast_to(row, (lines, 128))
+        for q in range(3):
+            out_ref[at, 512 + 128 * q : 640 + 128 * q] = lost[q * lines : (q + 1) * lines]
+        rate = rate_scratch[pl.ds(pl.multiple_of((place + p) * sub, sub), sub), :]
+        part = sens[p * sub : (p + 1) * sub]
+        blocks = [wide(part[:, c * lines : (c + 1) * lines]) for c in range(CAP)]
+        one = jnp.concatenate(blocks[:8], axis=0)
+        two = jnp.concatenate(
+            blocks[8:] + [rest[:, 512:640], rest[:, 640:768], rate, jnp.zeros((32, 128), F32)], axis=0
+        )
+        out_ref[at, 896:1024] = jnp.transpose(one)[:lines]
+        out_ref[at, 1024:1152] = jnp.transpose(two)[:lines]
 
 
 def screen_kernel(got_ref, mon_ref, off_ref, live_ref, out_ref):
-    lines = got_ref.shape[0]
     slots, outages = mon_ref.shape
     sub = out_ref.shape[1]
-    place = lax.axis_index("bus")
+    passes = lax.axis_size("bus_z")
+    lines = got_ref.shape[0] // passes
+    place = lax.axis_index("bus_x") * passes + lax.axis_index("bus_z")
     pieces = []
     for t in range(9):
-        block = got_ref[:, 128 * t : 128 * t + 128]
+        block = got_ref[:lines, 128 * t : 128 * t + 128]
+        for p in range(1, passes):
+            block = block + got_ref[p * lines : (p + 1) * lines, 128 * t : 128 * t + 128]
         high = block.astype(BF16).astype(F32)
         low = (block - high).astype(BF16).astype(F32)
         pieces.append(jnp.transpose(jnp.concatenate([high, low], axis=0)).astype(BF16))
@@ -275,78 +287,86 @@
         out_ref[2 * t + 1] = result[:, outages:]
 
 
-def call(kernel, out_shape, scratch=(), flops=0, moved=0):
-    single = not isinstance(out_shape, (tuple, list))
-    spec = pl.BlockSpec(memory_space=pltpu.VMEM)
+def call(kernel, out_shape, in_specs, scratch=(), flops=0, moved=0, limit=16):
     return pl.pallas_call(
         kernel,
         out_shape=out_shape,
-        out_specs=spec if single else tuple(spec for _ in out_shape),
+        in_specs=in_specs,
+        out_specs=IN_VMEM,
         scratch_shapes=list(scratch),
-        compiler_params=pltpu.CompilerParams(vmem_limit_bytes=32 * 1024 * 1024),
+        compiler_params=pltpu.CompilerParams(vmem_limit_bytes=limit * 1024 * 1024),
         cost_estimate=pl.CostEstimate(flops=flops, bytes_accessed=moved, transcendentals=0),
     )
 
 
 def local(shift_factors, injection, rating, monitored, live_count, outage_offset, outage_ends):
-    bus_count = lax.axis_size("bus")
+    peers = lax.axis_size("bus_x")
+    passes = lax.axis_size("bus_z")
     line_count = lax.axis_size("line")
     block_rows, bus_width = shift_factors.shape
-    sub_rows = block_rows // bus_count
+    sub_rows = block_rows // (peers * passes)
     outages, slot_count = monitored.shape
     entries = CAP * line_count
     shape = jax.ShapeDtypeStruct
-    groups_x = [[first + other * PASS for other in range(PEERS)] for first in range(PASS)]
-    groups_z = [[PASS * first + other for other in range(PASS)] for first in range(PEERS)]
     off_row = outage_offset.reshape(1, outages)
     live_row = live_count.reshape(1, outages)
     rate_row = rating.reshape(1, block_rows)
     named = monitored.T
     with jax.named_scope("requests"):
-        requests = call(request_kernel, shape((line_count, 128), F32))(named, outage_ends.T, off_row)
+        requests = call(request_kernel, shape((line_count, 128), F32), [IN_VMEM] * 3, limit=56)(
+            named, outage_ends.T, off_row
+        )
         asked = lax.all_to_all(requests, "line", split_axis=0, concat_axis=0, tiled=True)
     with jax.named_scope("picks"):
         partial_sens = call(
             pick_kernel,
-            shape((PEERS, PASS * sub_rows + 8, entries), F32),
+            shape((peers, passes * sub_rows + 8, entries), F32),
+            [IN_VMEM, IN_PLACE, IN_PLACE],
             scratch=(
+                pltpu.VMEM((block_rows, bus_width), F32),
+                pltpu.VMEM((HOURS, bus_width), F32),
                 pltpu.VMEM((entries, 128), jnp.int16),
                 pltpu.VMEM((entries, 128), jnp.int16),
                 pltpu.VMEM((entries, 2 * block_rows), F32),
                 pltpu.VMEM((2 * HOURS, 2 * block_rows), F32),
+                pltpu.SemaphoreType.DMA((-(-bus_width // CHUNK),)),
+                pltpu.SemaphoreType.DMA,
             ),
             flops=4 * entries * block_rows * bus_width,
             moved=4 * block_rows * bus_width,
+            limit=56,
         )(asked, shift_factors, injection)
-        partial_sens = lax.all_to_all(
-            partial_sens, "bus", split_axis=0, concat_axis=0, tiled=True, axis_index_groups=groups_x
-        )
-    with jax.named_scope("sums"):
-        half = call(sum_kernel, shape((PASS, sub_rows + 8, entries), F32))(partial_sens)
-        sens = lax.all_to_all(half, "bus", split_axis=0, concat_axis=0, tiled=True, axis_index_groups=groups_z)
+        half_sens = lax.all_to_all(partial_sens, "bus_x", split_axis=0, concat_axis=0, tiled=True)
     with jax.named_scope("reply"):
-        reply = call(reply_kernel, shape((line_count, 1152), F32), scratch=(pltpu.VMEM((128, 128), F32),))(
-            sens, asked, rate_row
-        )
-        got = lax.all_to_all(reply, "line", split_axis=0, concat_axis=0, tiled=True)
+        reply = call(
+            reply_kernel,
+            shape((passes * line_count, 1152), F32),
+            [IN_VMEM] * 3,
+            scratch=(pltpu.VMEM((block_rows, block_rows), F32),),
+        )(half_sens, asked, rate_row)
+        got = lax.all_to_all(reply, ("bus_z", "line"), split_axis=0, concat_axis=0, tiled=True)
     with jax.named_scope("screen"):
-        loading = call(screen_kernel, shape((slot_count, sub_rows, outages), F32))(got, named, off_row, live_row)
+        loading = call(screen_kernel, shape((slot_count, sub_rows, outages), F32), [IN_VMEM] * 4)(
+            got, named, off_row, live_row
+        )
     return jnp.transpose(loading, (2, 0, 1))
 
 
 def solution(mesh):
+    lines, buses = mesh.devices.shape
+    bus = ("bus_x", "bus_z")
     return jax.shard_map(
         local,
-        mesh=mesh,
+        mesh=jax.sharding.Mesh(mesh.devices.reshape(lines, buses // PASS, PASS), ("line",) + bus),
         in_specs=(
-            P("line", "bus"),
-            P(None, "bus"),
+            P("line", bus),
+            P(None, bus),
             P("line"),
             P("line", None),
             P("line"),
             P("line"),
             P("line", None),
         ),
-        out_specs=P("line", None, "bus"),
+        out_specs=P("line", None, bus),
         check_vma=False,
     )

time: 84.7 us -> 83.1 us (0.981)
  local copies, waits for them, and re-layouts: 5.66 us -> 0.67 us
  Pallas kernels: 8.07 us -> 12.5 us
  blocking collectives: 70.5 us -> 69.5 us
    unnamed x19 -> x11, local copies, waits for them, and re-layouts: 5.35 us -> 0.07 us
    pallas_call x5 -> x4, Pallas kernels: 8.07 us -> 12.5 us  [the longest x1 9.11 us: local(): call(pick_kernel, shape((peers, passes * sub_rows + 8, entries), F32), [I...]
    all_to_all x3 -> x2, blocking collectives: 46.5 us -> 45.4 us  [the longest x1 33.4 us: local(): lax.all_to_all(reply, ('bus_z', 'line'), split_axis=0, concat_axis=0, til...]
where the time goes in v3:
time: 83.1 us; the launch traced here: 82.8 us
  blocking collectives  69.5 us (84%)
  Pallas kernels  12.5 us (15%)
    all_to_all x1, blocking collectives, local(): lax.all_to_all(reply, ('bus_z', 'line'), split_axis=0, concat_axis=0, til...  33.4 us
    all_to_all x1, blocking collectives, local(): lax.all_to_all(requests, 'line', split_axis=0, concat_axis=0, tiled=True)  24.1 us
    all_to_all x1, blocking collectives, local(): lax.all_to_all(partial_sens, 'bus_x', split_axis=0, concat_axis=0, tiled=...  12 us
    pallas_call x1, Pallas kernels, local(): call(pick_kernel, shape((peers, passes * sub_rows + 8, entries), F32), [I...  9.11 us
    pallas_call x1, Pallas kernels, local(): call(request_kernel, shape((line_count, 128), F32), [IN_VMEM] * 3, limit=56)  1.76 us

profile of v3, /device:TPU:1, one launch (start us, length us, event | category | flops | bytes accessed | tf_op | source)
XLA Modules:
  0.0 82.8 jit_solution(12174476725160538116)
XLA Ops:
  0.0 1.8 %requests.1 = f32[64,128]{1,0:T(8,128)} custom-call(s32[8,64]{1,0:T(8,128)} %bitcast.18, s32[2,64]{1,0:T(2,128)} %bitcast.25, s32[1,64]{1,0:T(1,128)} %bitcast.20), custom_call_target="tpu_custom_call" | custom-call | tf_op jit(solution)/shard_map/requests/pallas_call | solution.py:316
  1.8 24.1 %all_to_all.27 = f32[64,1,128]{2,1,0:T(1,128)} all-to-all(f32[64,1,128]{2,1,0:T(1,128)} %bitcast.24), channel_id=1, replica_groups=mesh['line'=64,'bus_x'=4,'bus_z'=2] {'line'}, dimensions={0} | all-to-all | bytes 65536 | tf_op jit(solution)/shard_map/requests/all_to_all | solution.py:319
  25.9 0.0 copy-start
  25.9 0.0 copy-start.3
  25.9 9.1 %picks.1 = f32[4,40,768]{2,1,0:T(8,128)} custom-call(f32[64,128]{1,0:T(8,128)} %bitcast.16, f32[128,7552]{1,0:T(8,128)} %s_hbm.1, f32[32,7552]{1,0:T(8,128)} %inj_hbm.1), custom_call_target="tpu_custom_call" | custom-call | flops 2969567232 | bytes 3866624 | tf_op jit(solution)/shard_map/picks/pallas_call | solution.py:321
  35.0 0.0 copy-start.1
  35.0 0.0 copy-start.2
  35.0 0.0 copy-start.4
  35.1 12.0 %all_to_all.28.got_ref = f32[4,40,768]{2,1,0:T(8,128)S(1)} all-to-all(f32[4,40,768]{2,1,0:T(8,128)} %picks.1), channel_id=1, replica_groups=mesh['line'=64,'bus_x'=4,'bus_z'=2] {'bus_x'}, dimensions={0} | all-to-all | bytes 983040 | tf_op jit(solution)/shard_map/picks/all_to_all | solution.py:339
  47.0 0.0 copy-done
  47.0 0.0 copy-done.3
  47.0 0.4 reply.1
  47.4 0.6 copy.9
  48.0 33.4 %all_to_all.29 = f32[128,1,1152]{2,1,0:T(1,128)S(1)} all-to-all(f32[128,1,1152]{2,1,0:T(1,128)S(1)} %copy.9), channel_id=1, replica_groups=mesh['line'=64,'bus_x'=4,'bus_z'=2] {'bus_z','line'}, dimensions={0} | all-to-all | bytes 1179648 | tf_op jit(solution)/shard_map/reply/all_to_all | solution.py:347
  81.5 0.0 copy-done.1
  81.5 0.0 copy-done.2
  81.5 0.0 copy-done.4
  81.5 1.2 %screen.1 = f32[8,16,64]{2,1,0:T(8,128)} custom-call(f32[128,1152]{1,0:T(8,128)S(1)} %bitcast.15, s32[8,64]{1,0:T(8,128)S(1)} %bitcast.19, s32[1,64]{1,0:T(1,128)S(1)} %bitcast.21, s32[1,64]{1,0:T(1,128)S(1)} %bitcast.23), custom_call_target="tpu_custom_call" | custom-call | tf_op jit(solution)/shard_map/screen/pallas_call | solution.py:349
  (1 shorter events, 0.0 us)
Async XLA Ops:
  25.9 21.1 %copy-start = (f32[64,1,128]{2,1,0:T(1,128)S(1)}, f32[64,1,128]{2,1,0:T(1,128)}, u32[]{:S(2)}) copy-start(f32[64,1,128]{2,1,0:T(1,128)} %all_to_all.27) | copy-start | bytes 98308
  25.9 21.1 %copy-start.3 = (f32[128]{0:T(128)S(1)}, f32[128]{0:T(128)}, u32[]{:S(2)}) copy-start(f32[128]{0:T(128)} %param.9) | copy-start | bytes 1540
  35.0 46.5 %copy-start.1 = (s32[64,8]{0,1:T(8,128)S(1)}, s32[64,8]{0,1:T(8,128)}, u32[]{:S(2)}) copy-start(s32[64,8]{0,1:T(8,128)} %param.10) | copy-start | bytes 6148
  35.0 46.5 %copy-start.2 = (s32[64]{0:T(128)S(1)}, s32[64]{0:T(128)}, u32[]{:S(2)}) copy-start(s32[64]{0:T(128)} %param.12) | copy-start | bytes 772
  35.0 46.5 %copy-start.4 = (s32[64]{0:T(128)S(1)}, s32[64]{0:T(128)}, u32[]{:S(2)}) copy-start(s32[64]{0:T(128)} %param.11) | copy-start | bytes 772

commit v4 on v3

--- a/solution.py
+++ b/solution.py
@@ -12,10 +12,11 @@
 NN = (((1,), (0,)), ((), ()))
 HOURS = 32
 CAP = 12
-CHUNK = 1920
+CHUNK = 2304
 PASS = 2
+TILES = 9
 IN_VMEM = pl.BlockSpec(memory_space=pltpu.VMEM)
-IN_PLACE = pl.BlockSpec(memory_space=pl.ANY)
+IN_HBM = pl.BlockSpec(memory_space=pltpu.HBM)
 
 
 def iota(shape, axis):
@@ -65,7 +66,7 @@
 
 
 def pick_kernel(
-    req_ref, s_hbm, inj_hbm, out_ref, s_ref, inj_ref, from_ref, to_ref, sum_ref, flow_ref, s_sems, inj_sem
+    req_ref, s_hbm, inj_hbm, out_ref, s_ref, inj_ref, from_ref, to_ref, sum_ref, flow_ref, s_sems, inj_sems
 ):
     lines = req_ref.shape[0]
     rows, width = s_ref.shape
@@ -73,17 +74,24 @@
     deep = rows // peers
     whole, rest = width // CHUNK, width % CHUNK
 
-    def copy(at, size, q):
+    def copies(at, size, q):
         cols = pl.ds(at, size)
-        return pltpu.make_async_copy(s_hbm.at[:, cols], s_ref.at[:, cols], s_sems.at[q])
-
-    inj_copy = pltpu.make_async_copy(inj_hbm, inj_ref, inj_sem)
+        return (
+            pltpu.make_async_copy(s_hbm.at[:, cols], s_ref.at[:, cols], s_sems.at[q]),
+            pltpu.make_async_copy(inj_hbm.at[:, cols], inj_ref.at[:, cols], inj_sems.at[q]),
+        )
+
+    def fetch(at, size, q):
+        for copy in copies(at, size, q):
+            copy.start()
+
+    def arrive(at, size, q):
+        for copy in copies(at, size, q):
+            copy.wait()
+
+    fetch(whole * CHUNK, rest, whole)
     for q in range(whole):
-        copy(q * CHUNK, CHUNK, q).start()
-        if q == 0:
-            inj_copy.start()
-    if rest:
-        copy(whole * CHUNK, rest, whole).start()
+        fetch(q * CHUNK, CHUNK, q)
     bus = lax.axis_index("bus_x") * lax.axis_size("bus_z") + lax.axis_index("bus_z")
     base = bus * width + 1
     req = req_ref[...]
@@ -119,18 +127,16 @@
             jnp.concatenate([i_high, i_low], axis=0), both, NT, preferred_element_type=F32
         )
 
-    inj_copy.wait()
+    arrive(whole * CHUNK, rest, whole)
+    step(whole * CHUNK, rest)
 
     def body(q, carry):
         at = pl.multiple_of(q * CHUNK, CHUNK)
-        copy(at, CHUNK, q).wait()
+        arrive(at, CHUNK, q)
         step(at, CHUNK)
         return carry
 
     lax.fori_loop(0, whole, body, 0)
-    if rest:
-        copy(whole * CHUNK, rest, whole).wait()
-        step(whole * CHUNK, rest)
     part = (
         flow_ref[:HOURS, :rows]
         + (flow_ref[:HOURS, rows:] + flow_ref[HOURS:, :rows])
@@ -158,7 +164,7 @@
     peers = got_ref.shape[0]
     lines = req_ref.shape[0]
     rows = rate_ref.shape[1]
-    passes = out_ref.shape[0] // lines
+    passes = out_ref.shape[0] // (lines * TILES)
     sub = (got_ref.shape[1] - 8) // passes
     place = lax.axis_index("bus_x") * passes
     total = got_ref[0]
@@ -193,17 +199,19 @@
     def wide(block):
         return jnp.concatenate([block, jnp.zeros((block.shape[0], 128 - lines), F32)], axis=1)
 
+    def put(p, q, block):
+        out_ref[pl.ds(p * lines * TILES + q, lines, stride=TILES), :] = block
+
     for p in range(passes):
-        at = slice(p * lines, (p + 1) * lines)
         wanted = iota((128, 128), 0) == (place + p) * sub + iota((128, 128), 1) % sub
         spread = lax.dot_general(f_all, jnp.where(wanted, 1.0, 0.0).astype(BF16), NN, preferred_element_type=F32)
         spread = spread[:HOURS] + spread[HOURS : 2 * HOURS] + spread[2 * HOURS :]
         spread = jnp.where(lane // sub == hour % 8, spread, 0.0)
         for t in range(4):
             row = jnp.sum(spread[8 * t : 8 * t + 8], axis=0, keepdims=True)
-            out_ref[at, 128 * t : 128 * t + 128] = jnp.broadcast_to(row, (lines, 128))
+            put(p, t, jnp.broadcast_to(row, (lines, 128)))
         for q in range(3):
-            out_ref[at, 512 + 128 * q : 640 + 128 * q] = lost[q * lines : (q + 1) * lines]
+            put(p, 4 + q, lost[q * lines : (q + 1) * lines])
         rate = rate_scratch[pl.ds(pl.multiple_of((place + p) * sub, sub), sub), :]
         part = sens[p * sub : (p + 1) * sub]
         blocks = [wide(part[:, c * lines : (c + 1) * lines]) for c in range(CAP)]
@@ -211,21 +219,21 @@
         two = jnp.concatenate(
             blocks[8:] + [rest[:, 512:640], rest[:, 640:768], rate, jnp.zeros((32, 128), F32)], axis=0
         )
-        out_ref[at, 896:1024] = jnp.transpose(one)[:lines]
-        out_ref[at, 1024:1152] = jnp.transpose(two)[:lines]
+        put(p, 7, jnp.transpose(one)[:lines])
+        put(p, 8, jnp.transpose(two)[:lines])
 
 
 def screen_kernel(got_ref, mon_ref, off_ref, live_ref, out_ref):
     slots, outages = mon_ref.shape
     sub = out_ref.shape[1]
     passes = lax.axis_size("bus_z")
-    lines = got_ref.shape[0] // passes
+    lines = got_ref.shape[0] // (passes * TILES)
     place = lax.axis_index("bus_x") * passes + lax.axis_index("bus_z")
     pieces = []
-    for t in range(9):
-        block = got_ref[:lines, 128 * t : 128 * t + 128]
+    for t in range(TILES):
+        block = got_ref[pl.ds(t, lines, stride=TILES), :]
         for p in range(1, passes):
-            block = block + got_ref[p * lines : (p + 1) * lines, 128 * t : 128 * t + 128]
+            block = block + got_ref[pl.ds(p * lines * TILES + t, lines, stride=TILES), :]
         high = block.astype(BF16).astype(F32)
         low = (block - high).astype(BF16).astype(F32)
         pieces.append(jnp.transpose(jnp.concatenate([high, low], axis=0)).astype(BF16))
@@ -321,7 +329,7 @@
         partial_sens = call(
             pick_kernel,
             shape((peers, passes * sub_rows + 8, entries), F32),
-            [IN_VMEM, IN_PLACE, IN_PLACE],
+            [IN_VMEM, IN_HBM, IN_HBM],
             scratch=(
                 pltpu.VMEM((block_rows, bus_width), F32),
                 pltpu.VMEM((HOURS, bus_width), F32),
@@ -329,25 +337,26 @@
                 pltpu.VMEM((entries, 128), jnp.int16),
                 pltpu.VMEM((entries, 2 * block_rows), F32),
                 pltpu.VMEM((2 * HOURS, 2 * block_rows), F32),
-                pltpu.SemaphoreType.DMA((-(-bus_width // CHUNK),)),
-                pltpu.SemaphoreType.DMA,
+                pltpu.SemaphoreType.DMA((bus_width // CHUNK + 1,)),
+                pltpu.SemaphoreType.DMA((bus_width // CHUNK + 1,)),
             ),
             flops=4 * entries * block_rows * bus_width,
             moved=4 * block_rows * bus_width,
-            limit=56,
+            limit=53,
         )(asked, shift_factors, injection)
         half_sens = lax.all_to_all(partial_sens, "bus_x", split_axis=0, concat_axis=0, tiled=True)
     with jax.named_scope("reply"):
         reply = call(
             reply_kernel,
-            shape((passes * line_count, 1152), F32),
+            shape((passes * line_count * TILES, 128), F32),
             [IN_VMEM] * 3,
             scratch=(pltpu.VMEM((block_rows, block_rows), F32),),
         )(half_sens, asked, rate_row)
+        reply = reply.reshape(passes * line_count, TILES * 128)
         got = lax.all_to_all(reply, ("bus_z", "line"), split_axis=0, concat_axis=0, tiled=True)
     with jax.named_scope("screen"):
         loading = call(screen_kernel, shape((slot_count, sub_rows, outages), F32), [IN_VMEM] * 4)(
-            got, named, off_row, live_row
+            got.reshape(-1, 128), named, off_row, live_row
         )
     return jnp.transpose(loading, (2, 0, 1))
 

time: 83.1 us -> 80.2 us (0.965)
  Pallas kernels: 12.5 us -> 11 us
    pallas_call x1, Pallas kernels: 9.11 us -> 7.64 us  [local(): call(pick_kernel, shape((peers, passes * sub_rows + 8, entries), F32), [I...]
where the time goes in v4:
time: 80.2 us; the launch traced here: 80 us
  blocking collectives  68.9 us (86%)
  Pallas kernels  11 us (14%)
    all_to_all x1, blocking collectives, local(): lax.all_to_all(reply, ('bus_z', 'line'), split_axis=0, concat_axis=0, til...  32.8 us
    all_to_all x1, blocking collectives, local(): lax.all_to_all(requests, 'line', split_axis=0, concat_axis=0, tiled=True)  24.1 us
    all_to_all x1, blocking collectives, local(): lax.all_to_all(partial_sens, 'bus_x', split_axis=0, concat_axis=0, tiled=...  12 us
    pallas_call x1, Pallas kernels, local(): call(pick_kernel, shape((peers, passes * sub_rows + 8, entries), F32), [I...  7.64 us
    pallas_call x1, Pallas kernels, local(): call(request_kernel, shape((line_count, 128), F32), [IN_VMEM] * 3, limit=56)  1.76 us

profile of v4, /device:TPU:1, one launch (start us, length us, event | category | flops | bytes accessed | tf_op | source)
XLA Modules:
  0.0 80.0 jit_solution(7044681373719805483)
XLA Ops:
  0.0 1.8 %requests.1 = f32[64,128]{1,0:T(8,128)} custom-call(s32[8,64]{1,0:T(8,128)} %bitcast.16, s32[2,64]{1,0:T(2,128)} %bitcast.23, s32[1,64]{1,0:T(1,128)} %bitcast.18), custom_call_target="tpu_custom_call" | custom-call | tf_op jit(solution)/shard_map/requests/pallas_call | solution.py:324
  1.8 24.1 %all_to_all.25 = f32[64,1,128]{2,1,0:T(1,128)S(1)} all-to-all(f32[64,1,128]{2,1,0:T(1,128)} %bitcast.22), channel_id=1, replica_groups=mesh['line'=64,'bus_x'=4,'bus_z'=2] {'line'}, dimensions={0} | all-to-all | bytes 65536 | tf_op jit(solution)/shard_map/requests/all_to_all | solution.py:327
  25.9 0.0 copy-start.2
  25.9 0.0 copy-start
  25.9 0.0 copy-start.1
  25.9 0.0 copy-start.3
  25.9 7.6 %picks.1 = f32[4,40,768]{2,1,0:T(8,128)S(1)} custom-call(f32[64,128]{1,0:T(8,128)S(1)} %bitcast.14, f32[128,7552]{1,0:T(8,128)} %s_hbm.1, f32[32,7552]{1,0:T(8,128)} %inj_hbm.1), custom_call_target="tpu_custom_call" | custom-call | flops 2969567232 | bytes 3866624 | tf_op jit(solution)/shard_map/picks/pallas_call | solution.py:329
  33.6 12.0 %all_to_all.26.got_ref = f32[4,40,768]{2,1,0:T(8,128)S(1)} all-to-all(f32[4,40,768]{2,1,0:T(8,128)S(1)} %picks.1), channel_id=1, replica_groups=mesh['line'=64,'bus_x'=4,'bus_z'=2] {'bus_x'}, dimensions={0} | all-to-all | bytes 983040 | tf_op jit(solution)/shard_map/picks/all_to_all | solution.py:347
  45.6 0.0 copy-done.2
  45.6 0.4 reply.1
  46.0 32.8 %all_to_all.27 = f32[128,1,1152]{2,1,0:T(1,128)S(1)} all-to-all(f32[128,1,1152]{2,1,0:T(1,128)S(1)} %bitcast.12), channel_id=1, replica_groups=mesh['line'=64,'bus_x'=4,'bus_z'=2] {'bus_z','line'}, dimensions={0} | all-to-all | bytes 1179648 | tf_op jit(solution)/shard_map/reply/all_to_all | solution.py:356
  78.7 0.0 copy-done
  78.7 0.0 copy-done.1
  78.8 0.0 copy-done.3
  78.8 1.2 %screen.1 = f32[8,16,64]{2,1,0:T(8,128)} custom-call(f32[1152,128]{1,0:T(8,128)S(1)} %bitcast.13, s32[8,64]{1,0:T(8,128)S(1)} %bitcast.17, s32[1,64]{1,0:T(1,128)S(1)} %bitcast.19, s32[1,64]{1,0:T(1,128)S(1)} %bitcast.21), custom_call_target="tpu_custom_call" | custom-call | tf_op jit(solution)/shard_map/screen/pallas_call | solution.py:358
Async XLA Ops:
  25.9 19.7 %copy-start.2 = (f32[128]{0:T(128)S(1)}, f32[128]{0:T(128)}, u32[]{:S(2)}) copy-start(f32[128]{0:T(128)} %param.9) | copy-start | bytes 1540
  25.9 52.8 %copy-start = (s32[64,8]{0,1:T(8,128)S(1)}, s32[64,8]{0,1:T(8,128)}, u32[]{:S(2)}) copy-start(s32[64,8]{0,1:T(8,128)} %param.10) | copy-start | bytes 6148
  25.9 52.8 %copy-start.1 = (s32[64]{0:T(128)S(1)}, s32[64]{0:T(128)}, u32[]{:S(2)}) copy-start(s32[64]{0:T(128)} %param.12) | copy-start | bytes 772
  25.9 52.8 %copy-start.3 = (s32[64]{0:T(128)S(1)}, s32[64]{0:T(128)}, u32[]{:S(2)}) copy-start(s32[64]{0:T(128)} %param.11) | copy-start | bytes 772

commit v5 on v4

--- a/solution.py
+++ b/solution.py
@@ -15,6 +15,7 @@
 CHUNK = 2304
 PASS = 2
 TILES = 9
+PACKED = 256
 IN_VMEM = pl.BlockSpec(memory_space=pltpu.VMEM)
 IN_HBM = pl.BlockSpec(memory_space=pltpu.HBM)
 
@@ -28,7 +29,7 @@
     return high, (value - high.astype(F32)).astype(BF16)
 
 
-def request_kernel(mon_ref, ends_ref, off_ref, out_ref):
+def request_kernel(mon_ref, ends_ref, off_ref, live_ref, out_ref):
     slots, outages = mon_ref.shape
     lines = out_ref.shape[0]
 
@@ -37,14 +38,18 @@
 
     named = twice(mon_ref[...])
     line_row = iota((lines, 128), 0)
+    live = twice(live_ref[...])
     names = jnp.zeros((lines, 128), F32)
+    asks = jnp.zeros((lines, 128), F32)
     for s in range(slots):
-        names = jnp.where(named[s : s + 1] == line_row, 1.0, names)
+        same = named[s : s + 1] == line_row
+        names = jnp.where(same, 1.0, names)
+        asks = jnp.where(same & (s < live), 1.0, asks)
     earlier = iota((128, 128), 0) < iota((128, 128), 1) % outages
     rank = lax.dot_general(
         names.astype(BF16), jnp.where(earlier, 1.0, 0.0).astype(BF16), NN, preferred_element_type=F32
     )
-    rank = jnp.where(names > 0.0, rank, -1.0)
+    rank = jnp.where(asks > 0.0, rank, -1.0)
     start = twice(ends_ref[0:1, :]) + 1
     end = twice(ends_ref[1:2, :]) + 1
     place = twice(off_ref[...]) + 1
@@ -66,11 +71,27 @@
 
 
 def pick_kernel(
-    req_ref, s_hbm, inj_hbm, out_ref, s_ref, inj_ref, from_ref, to_ref, sum_ref, flow_ref, s_sems, inj_sems
+    req_ref,
+    s_hbm,
+    inj_hbm,
+    out_ref,
+    s_ref,
+    inj_ref,
+    split_ref,
+    turn_ref,
+    perm_ref,
+    from_ref,
+    to_ref,
+    sum_ref,
+    flow_ref,
+    total_ref,
+    s_sems,
+    inj_sems,
 ):
     lines = req_ref.shape[0]
     rows, width = s_ref.shape
     peers, _, entries = out_ref.shape
+    packed = from_ref.shape[0]
     deep = rows // peers
     whole, rest = width // CHUNK, width % CHUNK
 
@@ -93,70 +114,128 @@
     for q in range(whole):
         fetch(q * CHUNK, CHUNK, q)
     bus = lax.axis_index("bus_x") * lax.axis_size("bus_z") + lax.axis_index("bus_z")
-    base = bus * width + 1
+    base = (bus * width + 1).astype(F32)
     req = req_ref[...]
     lane = iota((lines, 128), 1)
-    for c in range(CAP):
-        first = req[:, c : c + 1].astype(jnp.int32) - base
-        second = req[:, 16 + c : 17 + c].astype(jnp.int32) - base
-        same = first == second
-        first = jnp.where(same | (first < 0) | (first >= width), -1, first)
-        second = jnp.where(same | (second < 0) | (second >= width), -1, second)
-        from_ref[c * lines : (c + 1) * lines, :] = jnp.broadcast_to(first, (lines, 128)).astype(jnp.int16)
-        to_ref[c * lines : (c + 1) * lines, :] = jnp.broadcast_to(second, (lines, 128)).astype(jnp.int16)
-    sum_ref[...] = jnp.zeros_like(sum_ref)
+    first = req - base
+    second = pltpu.roll(req, 112, 1) - base
+    has_first = (first >= 0.0) & (first < float(width))
+    has_second = (second >= 0.0) & (second < float(width))
+    used = (has_first | has_second) & (first != second) & (lane < CAP)
+    mask = jnp.where(used, 1.0, 0.0)
+    hits = mask.astype(BF16)
+    above = jnp.where(iota((lines, lines), 1) < iota((lines, lines), 0), 1.0, 0.0).astype(BF16)
+    ahead = jnp.where(iota((128, 128), 0) < iota((128, 128), 1), 1.0, 0.0).astype(BF16)
+    ones = jnp.ones((lines, lines), BF16)
+    in_lane = lax.dot_general(ones, hits, NN, preferred_element_type=F32)
+    rank = lax.dot_general(above, hits, NN, preferred_element_type=F32) + lax.dot_general(
+        in_lane.astype(BF16), ahead, NN, preferred_element_type=F32
+    )
+    rank = jnp.where(used, rank, -1.0)
+    count = jnp.sum(mask).astype(jnp.int32)
+    blocks = (count + (packed - 1)) // packed
+    first = jnp.where(has_first & used, first + 1.0, 0.0)
+    second = jnp.where(has_second & used, second + 1.0, 0.0)
+    first_high = jnp.floor(first * (1.0 / 128.0))
+    second_high = jnp.floor(second * (1.0 / 128.0))
+    fields = (first_high, first - 128.0 * first_high, second_high, second - 128.0 * second_high, rank)
+    mixed = pltpu.roll(req, 48, 1)
+    for q in reversed(range(5)):
+        field = pltpu.roll(fields[q], 16 * q, 1) if q else fields[q]
+        mixed = jnp.where(lane < 16 * (q + 1), field, mixed) if q < 4 else jnp.where(lane < 80, field, mixed)
+    turn_ref[...] = jnp.transpose(jnp.concatenate([mixed, jnp.zeros((128 - lines, 128), F32)], axis=0))
+    pairs = []
+    lane_row = iota((8, 128), 1)
+    for t in range(CAP // 2):
+        even = turn_ref[pl.ds(2 * t, 8, stride=16), :]
+        odd = turn_ref[pl.ds(2 * t + 1, 8, stride=16), :]
+        pairs.append(jnp.where(lane_row < lines, even, pltpu.roll(odd, lines, 1)))
+    table = jnp.concatenate(pairs, axis=1)
+    ranks = table[4:5].astype(jnp.int32)
+    offs = table[5:6].astype(jnp.int32) - 1
+    table_low = table.astype(BF16)
+    one, minus, zero = jnp.asarray(1, BF16), jnp.asarray(-1, BF16), jnp.asarray(0, BF16)
     flow_ref[...] = jnp.zeros_like(flow_ref)
-    one, minus, zero = jnp.asarray(1, BF16), jnp.asarray(-1, BF16), jnp.asarray(0, BF16)
-
-    def step(at, size):
+    total_ref[...] = jnp.zeros_like(total_ref)
+
+    def open_block(block):
+        perm = jnp.where(iota((packed, entries), 0) + block * packed == ranks, 1.0, 0.0).astype(BF16)
+        perm_ref[...] = perm
+        ends = lax.dot_general(perm, table_low, NT, preferred_element_type=F32)
+        start = (128.0 * ends[:, 0:1] + ends[:, 1:2] - 1.0).astype(jnp.int32)
+        end = (128.0 * ends[:, 2:3] + ends[:, 3:4] - 1.0).astype(jnp.int32)
+        from_ref[...] = jnp.broadcast_to(start, (packed, 128)).astype(jnp.int16)
+        to_ref[...] = jnp.broadcast_to(end, (packed, 128)).astype(jnp.int16)
+        sum_ref[...] = jnp.zeros_like(sum_ref)
+
+    def pick(at, size):
         columns = []
         for t in range(size // 128):
             spot = (iota((16, 128), 1) + (at + t * 128)).astype(jnp.int16)
-            spot = jnp.broadcast_to(spot[None], (entries // 16, 16, 128)).reshape(entries, 128)
+            spot = jnp.broadcast_to(spot[None], (packed // 16, 16, 128)).reshape(packed, 128)
             columns.append(
                 jnp.where(from_ref[...] == spot, one, jnp.where(to_ref[...] == spot, minus, zero))
             )
+        sum_ref[...] += lax.dot_general(
+            jnp.concatenate(columns, axis=1), split_ref[:, pl.ds(at, size)], NT, preferred_element_type=F32
+        )
+
+    def close_block():
+        turned = jnp.transpose(sum_ref[:, :rows] + sum_ref[:, rows:])
+        both = lax.dot_general(
+            jnp.concatenate(split2(turned), axis=0), perm_ref[...], NN, preferred_element_type=F32
+        )
+        total_ref[...] += both[:rows] + both[rows:]
+
+    def step(at, size):
         cols = pl.ds(at, size)
-        s_high, s_low = split2(s_ref[:, cols])
-        both = jnp.concatenate([s_high, s_low], axis=0)
-        i_high, i_low = split2(inj_ref[:, cols])
-        sum_ref[...] += lax.dot_general(
-            jnp.concatenate(columns, axis=1), both, NT, preferred_element_type=F32
-        )
+        both = jnp.concatenate(split2(s_ref[:, cols]), axis=0)
+        split_ref[:, cols] = both
         flow_ref[...] += lax.dot_general(
-            jnp.concatenate([i_high, i_low], axis=0), both, NT, preferred_element_type=F32
-        )
-
+            jnp.concatenate(split2(inj_ref[:, cols]), axis=0), both, NT, preferred_element_type=F32
+        )
+        pick(at, size)
+
+    open_block(0)
     arrive(whole * CHUNK, rest, whole)
     step(whole * CHUNK, rest)
 
-    def body(q, carry):
+    def first_block(q, carry):
         at = pl.multiple_of(q * CHUNK, CHUNK)
         arrive(at, CHUNK, q)
         step(at, CHUNK)
         return carry
 
-    lax.fori_loop(0, whole, body, 0)
+    lax.fori_loop(0, whole, first_block, 0)
+    close_block()
+
+    def other_block(block, carry):
+        open_block(block)
+        pick(whole * CHUNK, rest)
+
+        def piece(q, carry):
+            pick(pl.multiple_of(q * CHUNK, CHUNK), CHUNK)
+            return carry
+
+        lax.fori_loop(0, whole, piece, 0)
+        close_block()
+        return carry
+
+    lax.fori_loop(1, blocks, other_block, 0)
     part = (
         flow_ref[:HOURS, :rows]
         + (flow_ref[:HOURS, rows:] + flow_ref[HOURS:, :rows])
         + flow_ref[HOURS:, rows:]
     )
-    picked = sum_ref[:, :rows] + sum_ref[:, rows:]
-    own = jnp.zeros((lines, 128), F32)
-    for c in range(CAP):
-        off = req[:, 32 + c : 33 + c].astype(jnp.int32) - 1
-        value = jnp.sum(
-            jnp.where(lane == off, picked[c * lines : (c + 1) * lines], 0.0), axis=1, keepdims=True
-        )
-        own = jnp.where(lane == c, value, own)
-    turned = jnp.transpose(picked)
-    own_turned = jnp.transpose(jnp.concatenate([own, jnp.zeros((128 - lines, 128), F32)], axis=0))
+    total = total_ref[...]
+    own = jnp.sum(jnp.where(iota((rows, entries), 0) == offs, total, 0.0), axis=0, keepdims=True)
+    own = [own[:, 128 * t : 128 * t + 128] for t in range(CAP // 2)] + [jnp.zeros((2, 128), F32)]
     extra = jnp.concatenate(
-        [part[8 * t : 8 * t + 8] for t in range(4)] + [own_turned[0:8], own_turned[8:16]], axis=1
+        [part[8 * t : 8 * t + 8] for t in range(4)] + [jnp.concatenate(own, axis=0), jnp.zeros((8, 128), F32)],
+        axis=1,
     )
     for b in range(peers):
-        out_ref[b, :deep, :] = turned[b * deep : (b + 1) * deep]
+        out_ref[b, :deep, :] = total[b * deep : (b + 1) * deep]
         out_ref[b, deep:, :] = extra
 
 
@@ -217,7 +296,9 @@
         blocks = [wide(part[:, c * lines : (c + 1) * lines]) for c in range(CAP)]
         one = jnp.concatenate(blocks[:8], axis=0)
         two = jnp.concatenate(
-            blocks[8:] + [rest[:, 512:640], rest[:, 640:768], rate, jnp.zeros((32, 128), F32)], axis=0
+            blocks[8:]
+            + [rest[:, 512:640], pltpu.roll(rest[:, 512:640], lines, 1), rate, jnp.zeros((32, 128), F32)],
+            axis=0,
         )
         put(p, 7, jnp.transpose(one)[:lines])
         put(p, 8, jnp.transpose(two)[:lines])
@@ -268,7 +349,8 @@
     for c in range(CAP):
         mine = turn_own == float(c)
         lost = jnp.where(mine, got_own[HOURS * c : HOURS * c + HOURS], lost)
-        self_sens = jnp.where(mine, got_own[448 + c : 449 + c], self_sens)
+        at = 448 + 8 * (c % 2) + c // 2
+        self_sens = jnp.where(mine, got_own[at : at + 1], self_sens)
     divisor = jnp.maximum(1.0 - self_sens, floor_value)
     off = jnp.concatenate([off_ref[...], off_ref[...]], axis=1)
     live = jnp.concatenate([live_ref[...], live_ref[...]], axis=1)
@@ -321,8 +403,8 @@
     rate_row = rating.reshape(1, block_rows)
     named = monitored.T
     with jax.named_scope("requests"):
-        requests = call(request_kernel, shape((line_count, 128), F32), [IN_VMEM] * 3, limit=56)(
-            named, outage_ends.T, off_row
+        requests = call(request_kernel, shape((line_count, 128), F32), [IN_VMEM] * 4, limit=56)(
+            named, outage_ends.T, off_row, live_row
         )
         asked = lax.all_to_all(requests, "line", split_axis=0, concat_axis=0, tiled=True)
     with jax.named_scope("picks"):
@@ -333,10 +415,14 @@
             scratch=(
                 pltpu.VMEM((block_rows, bus_width), F32),
                 pltpu.VMEM((HOURS, bus_width), F32),
-                pltpu.VMEM((entries, 128), jnp.int16),
-                pltpu.VMEM((entries, 128), jnp.int16),
-                pltpu.VMEM((entries, 2 * block_rows), F32),
+                pltpu.VMEM((2 * block_rows, bus_width), BF16),
+                pltpu.VMEM((128, 128), F32),
+                pltpu.VMEM((PACKED, entries), BF16),
+                pltpu.VMEM((PACKED, 128), jnp.int16),
+                pltpu.VMEM((PACKED, 128), jnp.int16),
+                pltpu.VMEM((PACKED, 2 * block_rows), F32),
                 pltpu.VMEM((2 * HOURS, 2 * block_rows), F32),
+                pltpu.VMEM((block_rows, entries), F32),
                 pltpu.SemaphoreType.DMA((bus_width // CHUNK + 1,)),
                 pltpu.SemaphoreType.DMA((bus_width // CHUNK + 1,)),
             ),

time: 80.2 us -> 77.5 us (0.966)
  Pallas kernels: 11 us -> 8.3 us
    pallas_call x1, Pallas kernels: 7.64 us -> 4.86 us  [local(): call(pick_kernel, shape((peers, passes * sub_rows + 8, entries), F32), [I...]
where the time goes in v5:
time: 77.5 us; the launch traced here: 77.3 us
  blocking collectives  68.9 us (89%)
  Pallas kernels  8.3 us (11%)
    all_to_all x1, blocking collectives, local(): lax.all_to_all(reply, ('bus_z', 'line'), split_axis=0, concat_axis=0, til...  32.8 us
    all_to_all x1, blocking collectives, local(): lax.all_to_all(requests, 'line', split_axis=0, concat_axis=0, tiled=True)  24.1 us
    all_to_all x1, blocking collectives, local(): lax.all_to_all(partial_sens, 'bus_x', split_axis=0, concat_axis=0, tiled=...  12 us
    pallas_call x1, Pallas kernels, local(): call(pick_kernel, shape((peers, passes * sub_rows + 8, entries), F32), [I...  4.86 us
    pallas_call x1, Pallas kernels, local(): call(request_kernel, shape((line_count, 128), F32), [IN_VMEM] * 4, limit=56)  1.82 us

profile of v5, /device:TPU:1, one launch (start us, length us, event | category | flops | bytes accessed | tf_op | source)
XLA Modules:
  0.0 77.3 jit_solution(988472368682212670)
XLA Ops:
  0.0 1.8 %requests.1 = f32[64,128]{1,0:T(8,128)} custom-call(s32[8,64]{1,0:T(8,128)} %bitcast.16, s32[2,64]{1,0:T(2,128)} %bitcast.24, s32[1,64]{1,0:T(1,128)} %bitcast.18, s32[1,64]{1,0:T(1,128)} %bitcast.20), custom_call_target="tpu_custom_call" | custom-call | tf_op jit(solution)/shard_map/requests/pallas_call | solution.py:406
  1.8 24.1 %all_to_all.25 = f32[64,1,128]{2,1,0:T(1,128)S(1)} all-to-all(f32[64,1,128]{2,1,0:T(1,128)} %bitcast.23), channel_id=1, replica_groups=mesh['line'=64,'bus_x'=4,'bus_z'=2] {'line'}, dimensions={0} | all-to-all | bytes 65536 | tf_op jit(solution)/shard_map/requests/all_to_all | solution.py:409
  26.0 0.0 copy-start.3
  26.0 0.0 copy-start
  26.0 0.0 copy-start.1
  26.0 0.0 copy-start.2
  26.0 4.9 %picks.1 = f32[4,40,768]{2,1,0:T(8,128)S(1)} custom-call(f32[64,128]{1,0:T(8,128)S(1)} %bitcast.14, f32[128,7552]{1,0:T(8,128)} %s_hbm.1, f32[32,7552]{1,0:T(8,128)} %inj_hbm.1), custom_call_target="tpu_custom_call" | custom-call | flops 2969567232 | bytes 3866624 | tf_op jit(solution)/shard_map/picks/pallas_call | solution.py:411
  30.8 12.0 %all_to_all.26.got_ref = f32[4,40,768]{2,1,0:T(8,128)S(1)} all-to-all(f32[4,40,768]{2,1,0:T(8,128)S(1)} %picks.1), channel_id=1, replica_groups=mesh['line'=64,'bus_x'=4,'bus_z'=2] {'bus_x'}, dimensions={0} | all-to-all | bytes 983040 | tf_op jit(solution)/shard_map/picks/all_to_all | solution.py:433
  42.9 0.0 copy-done.3
  42.9 0.4 reply.1
  43.3 32.8 %all_to_all.27 = f32[128,1,1152]{2,1,0:T(1,128)S(1)} all-to-all(f32[128,1,1152]{2,1,0:T(1,128)S(1)} %bitcast.12), channel_id=1, replica_groups=mesh['line'=64,'bus_x'=4,'bus_z'=2] {'bus_z','line'}, dimensions={0} | all-to-all | bytes 1179648 | tf_op jit(solution)/shard_map/reply/all_to_all | solution.py:442
  76.0 0.0 copy-done
  76.0 0.0 copy-done.1
  76.0 0.0 copy-done.2
  76.0 1.2 %screen.1 = f32[8,16,64]{2,1,0:T(8,128)} custom-call(f32[1152,128]{1,0:T(8,128)S(1)} %bitcast.13, s32[8,64]{1,0:T(8,128)S(1)} %bitcast.17, s32[1,64]{1,0:T(1,128)S(1)} %bitcast.19, s32[1,64]{1,0:T(1,128)S(1)} %bitcast.21), custom_call_target="tpu_custom_call" | custom-call | tf_op jit(solution)/shard_map/screen/pallas_call | solution.py:444
Async XLA Ops:
  26.0 16.9 %copy-start.3 = (f32[128]{0:T(128)S(1)}, f32[128]{0:T(128)}, u32[]{:S(2)}) copy-start(f32[128]{0:T(128)} %param.9) | copy-start | bytes 1540
  26.0 50.1 %copy-start = (s32[64,8]{0,1:T(8,128)S(1)}, s32[64,8]{0,1:T(8,128)}, u32[]{:S(2)}) copy-start(s32[64,8]{0,1:T(8,128)} %param.10) | copy-start | bytes 6148
  26.0 50.1 %copy-start.1 = (s32[64]{0:T(128)S(1)}, s32[64]{0:T(128)}, u32[]{:S(2)}) copy-start(s32[64]{0:T(128)} %param.12) | copy-start | bytes 772
  26.0 50.1 %copy-start.2 = (s32[64]{0:T(128)S(1)}, s32[64]{0:T(128)}, u32[]{:S(2)}) copy-start(s32[64]{0:T(128)} %param.11) | copy-start | bytes 772

commit v6 on v5

--- a/solution.py
+++ b/solution.py
@@ -14,7 +14,7 @@
 CAP = 12
 CHUNK = 2304
 PASS = 2
-TILES = 9
+TILES = 6
 PACKED = 256
 IN_VMEM = pl.BlockSpec(memory_space=pltpu.VMEM)
 IN_HBM = pl.BlockSpec(memory_space=pltpu.HBM)
@@ -70,23 +70,63 @@
     out_ref[...] = 256.0 * high + low
 
 
+def flow_kernel(s_hbm, inj_hbm, part_ref, s_ref, inj_ref, flow_ref, s_sems, inj_sems):
+    rows, width = s_ref.shape
+    whole, rest = width // CHUNK, width % CHUNK
+
+    def copies(at, size, q):
+        cols = pl.ds(at, size)
+        return (
+            pltpu.make_async_copy(s_hbm.at[:, cols], s_ref.at[:, cols], s_sems.at[q]),
+            pltpu.make_async_copy(inj_hbm.at[:, cols], inj_ref.at[:, cols], inj_sems.at[q]),
+        )
+
+    def fetch(at, size, q):
+        for copy in copies(at, size, q):
+            copy.start()
+
+    def step(at, size, q):
+        for copy in copies(at, size, q):
+            copy.wait()
+        cols = pl.ds(at, size)
+        flow_ref[...] += lax.dot_general(
+            jnp.concatenate(split2(inj_ref[:, cols]), axis=0),
+            jnp.concatenate(split2(s_ref[:, cols]), axis=0),
+            NT,
+            preferred_element_type=F32,
+        )
+
+    for q in range(whole):
+        fetch(q * CHUNK, CHUNK, q)
+    fetch(whole * CHUNK, rest, whole)
+    flow_ref[...] = jnp.zeros_like(flow_ref)
+
+    def body(q, carry):
+        step(pl.multiple_of(q * CHUNK, CHUNK), CHUNK, q)
+        return carry
+
+    lax.fori_loop(0, whole, body, 0)
+    step(whole * CHUNK, rest, whole)
+    part_ref[...] = (
+        flow_ref[:HOURS, :rows]
+        + (flow_ref[:HOURS, rows:] + flow_ref[HOURS:, :rows])
+        + flow_ref[HOURS:, rows:]
+    )
+
+
 def pick_kernel(
     req_ref,
     s_hbm,
-    inj_hbm,
     out_ref,
     s_ref,
-    inj_ref,
     split_ref,
     turn_ref,
     perm_ref,
     from_ref,
     to_ref,
     sum_ref,
-    flow_ref,
     total_ref,
     s_sems,
-    inj_sems,
 ):
     lines = req_ref.shape[0]
     rows, width = s_ref.shape
@@ -95,24 +135,13 @@
     deep = rows // peers
     whole, rest = width // CHUNK, width % CHUNK
 
-    def copies(at, size, q):
+    def copy(at, size, q):
         cols = pl.ds(at, size)
-        return (
-            pltpu.make_async_copy(s_hbm.at[:, cols], s_ref.at[:, cols], s_sems.at[q]),
-            pltpu.make_async_copy(inj_hbm.at[:, cols], inj_ref.at[:, cols], inj_sems.at[q]),
-        )
-
-    def fetch(at, size, q):
-        for copy in copies(at, size, q):
-            copy.start()
-
-    def arrive(at, size, q):
-        for copy in copies(at, size, q):
-            copy.wait()
-
-    fetch(whole * CHUNK, rest, whole)
+        return pltpu.make_async_copy(s_hbm.at[:, cols], s_ref.at[:, cols], s_sems.at[q])
+
+    copy(whole * CHUNK, rest, whole).start()
     for q in range(whole):
-        fetch(q * CHUNK, CHUNK, q)
+        copy(q * CHUNK, CHUNK, q).start()
     bus = lax.axis_index("bus_x") * lax.axis_size("bus_z") + lax.axis_index("bus_z")
     base = (bus * width + 1).astype(F32)
     req = req_ref[...]
@@ -155,7 +184,6 @@
     offs = table[5:6].astype(jnp.int32) - 1
     table_low = table.astype(BF16)
     one, minus, zero = jnp.asarray(1, BF16), jnp.asarray(-1, BF16), jnp.asarray(0, BF16)
-    flow_ref[...] = jnp.zeros_like(flow_ref)
     total_ref[...] = jnp.zeros_like(total_ref)
 
     def open_block(block):
@@ -191,18 +219,15 @@
         cols = pl.ds(at, size)
         both = jnp.concatenate(split2(s_ref[:, cols]), axis=0)
         split_ref[:, cols] = both
-        flow_ref[...] += lax.dot_general(
-            jnp.concatenate(split2(inj_ref[:, cols]), axis=0), both, NT, preferred_element_type=F32
-        )
         pick(at, size)
 
     open_block(0)
-    arrive(whole * CHUNK, rest, whole)
+    copy(whole * CHUNK, rest, whole).wait()
     step(whole * CHUNK, rest)
 
     def first_block(q, carry):
         at = pl.multiple_of(q * CHUNK, CHUNK)
-        arrive(at, CHUNK, q)
+        copy(at, CHUNK, q).wait()
         step(at, CHUNK)
         return carry
 
@@ -222,21 +247,25 @@
         return carry
 
     lax.fori_loop(1, blocks, other_block, 0)
-    part = (
-        flow_ref[:HOURS, :rows]
-        + (flow_ref[:HOURS, rows:] + flow_ref[HOURS:, :rows])
-        + flow_ref[HOURS:, rows:]
-    )
     total = total_ref[...]
     own = jnp.sum(jnp.where(iota((rows, entries), 0) == offs, total, 0.0), axis=0, keepdims=True)
     own = [own[:, 128 * t : 128 * t + 128] for t in range(CAP // 2)] + [jnp.zeros((2, 128), F32)]
-    extra = jnp.concatenate(
-        [part[8 * t : 8 * t + 8] for t in range(4)] + [jnp.concatenate(own, axis=0), jnp.zeros((8, 128), F32)],
-        axis=1,
-    )
+    own = jnp.concatenate(own, axis=0)
     for b in range(peers):
         out_ref[b, :deep, :] = total[b * deep : (b + 1) * deep]
-        out_ref[b, deep:, :] = extra
+        out_ref[b, deep:, :512] = jnp.zeros((8, 512), F32)
+        out_ref[b, deep:, 512:640] = own
+        out_ref[b, deep:, 640:] = jnp.zeros((8, 128), F32)
+
+
+def merge_kernel(message_ref, mine_ref, other_ref, out_ref):
+    flows = mine_ref[...] + other_ref[...]
+    flows = jnp.concatenate([flows[8 * t : 8 * t + 8] for t in range(4)], axis=1)
+    deep = out_ref.shape[1] - 8
+    for b in range(out_ref.shape[0]):
+        out_ref[b, :deep, :] = message_ref[b, :deep, :]
+        out_ref[b, deep:, :512] = flows
+        out_ref[b, deep:, 512:] = message_ref[b, deep:, 512:]
 
 
 def reply_kernel(got_ref, req_ref, rate_ref, out_ref, rate_scratch):
@@ -245,14 +274,19 @@
     rows = rate_ref.shape[1]
     passes = out_ref.shape[0] // (lines * TILES)
     sub = (got_ref.shape[1] - 8) // passes
+    half = HOURS // passes
     place = lax.axis_index("bus_x") * passes
     total = got_ref[0]
     for b in range(1, peers):
         total = total + got_ref[b]
     sens, rest = total[: passes * sub], total[passes * sub :]
-    flows = jnp.concatenate([rest[:, 128 * t : 128 * t + 128] for t in range(4)], axis=0)
-    lane = iota((HOURS, 128), 1)
-    hour = iota((HOURS, 128), 0)
+    flows = jnp.where(
+        lax.axis_index("bus_z") == 0,
+        jnp.concatenate([rest[:, 0:128], rest[:, 128:256]], axis=0),
+        jnp.concatenate([rest[:, 256:384], rest[:, 384:512]], axis=0),
+    )
+    lane = iota((half, 128), 1)
+    hour = iota((half, 128), 0)
     f_high, f_low = split2(flows)
     f_rest = (flows - f_high.astype(F32) - f_low.astype(F32)).astype(BF16)
     f_all = jnp.concatenate([f_high, f_low, f_rest], axis=0)
@@ -261,13 +295,13 @@
     hots = [
         jnp.where(lane_line == req[:, 32 + c : 33 + c].astype(jnp.int32) - 1, 1.0, 0.0).astype(BF16)
         for c in range(CAP)
-    ]
-    left = jnp.concatenate([jnp.concatenate(hots[4 * q : 4 * q + 4], axis=1) for q in range(3)], axis=0)
+    ] + [jnp.zeros((lines, 128), BF16)] * 4
+    left = jnp.concatenate([jnp.concatenate(hots[8 * q : 8 * q + 8], axis=1) for q in range(2)], axis=0)
 
     def diagonal(block):
         blank = jnp.zeros_like(block)
         return jnp.concatenate(
-            [jnp.concatenate([block if v == u else blank for v in range(4)], axis=1) for u in range(4)], axis=0
+            [jnp.concatenate([block if v == u else blank for v in range(8)], axis=1) for u in range(8)], axis=0
         )
 
     lost = lax.dot_general(
@@ -284,24 +318,23 @@
     for p in range(passes):
         wanted = iota((128, 128), 0) == (place + p) * sub + iota((128, 128), 1) % sub
         spread = lax.dot_general(f_all, jnp.where(wanted, 1.0, 0.0).astype(BF16), NN, preferred_element_type=F32)
-        spread = spread[:HOURS] + spread[HOURS : 2 * HOURS] + spread[2 * HOURS :]
+        spread = spread[:half] + spread[half : 2 * half] + spread[2 * half :]
         spread = jnp.where(lane // sub == hour % 8, spread, 0.0)
-        for t in range(4):
+        for t in range(2):
             row = jnp.sum(spread[8 * t : 8 * t + 8], axis=0, keepdims=True)
             put(p, t, jnp.broadcast_to(row, (lines, 128)))
-        for q in range(3):
-            put(p, 4 + q, lost[q * lines : (q + 1) * lines])
         rate = rate_scratch[pl.ds(pl.multiple_of((place + p) * sub, sub), sub), :]
         part = sens[p * sub : (p + 1) * sub]
         blocks = [wide(part[:, c * lines : (c + 1) * lines]) for c in range(CAP)]
         one = jnp.concatenate(blocks[:8], axis=0)
-        two = jnp.concatenate(
-            blocks[8:]
-            + [rest[:, 512:640], pltpu.roll(rest[:, 512:640], lines, 1), rate, jnp.zeros((32, 128), F32)],
-            axis=0,
-        )
-        put(p, 7, jnp.transpose(one)[:lines])
-        put(p, 8, jnp.transpose(two)[:lines])
+        two = jnp.concatenate([jnp.zeros((64, 128), F32)] + blocks[8:], axis=0)
+        three = jnp.concatenate(
+            [rest[:, 512:640], pltpu.roll(rest[:, 512:640], lines, 1), rate, jnp.zeros((96, 128), F32)], axis=0
+        )
+        put(p, 2, lost[:lines])
+        put(p, 3, jnp.where(lane_line < 64, lost[lines:], jnp.transpose(two)[:lines]))
+        put(p, 4, jnp.transpose(one)[:lines])
+        put(p, 5, jnp.transpose(three)[:lines])
 
 
 def screen_kernel(got_ref, mon_ref, off_ref, live_ref, out_ref):
@@ -310,16 +343,19 @@
     passes = lax.axis_size("bus_z")
     lines = got_ref.shape[0] // (passes * TILES)
     place = lax.axis_index("bus_x") * passes + lax.axis_index("bus_z")
-    pieces = []
-    for t in range(TILES):
-        block = got_ref[pl.ds(t, lines, stride=TILES), :]
-        for p in range(1, passes):
-            block = block + got_ref[pl.ds(p * lines * TILES + t, lines, stride=TILES), :]
+    half = HOURS // passes
+
+    def tile(p, t):
+        return got_ref[pl.ds(p * lines * TILES + t, lines, stride=TILES), :]
+
+    def piece(block):
         high = block.astype(BF16).astype(F32)
         low = (block - high).astype(BF16).astype(F32)
-        pieces.append(jnp.transpose(jnp.concatenate([high, low], axis=0)).astype(BF16))
-    shared = jnp.concatenate(pieces[:4] + pieces[7:], axis=0)
-    own = jnp.concatenate(pieces[4:7] + pieces[8:], axis=0)
+        return jnp.transpose(jnp.concatenate([high, low], axis=0)).astype(BF16)
+
+    sums = [piece(tile(0, t) + tile(1, t)) for t in (4, 3, 5)]
+    shared = jnp.concatenate([piece(tile(p, t)) for p in range(passes) for t in range(2)] + sums, axis=0)
+    own = jnp.concatenate([piece(tile(p, t)) for p in range(passes) for t in range(2, 4)] + sums[2:], axis=0)
     named = jnp.concatenate([mon_ref[...], mon_ref[...]], axis=1)
     line_row = iota((lines, 128), 0)
     lane = iota((1, 128), 1)
@@ -344,17 +380,19 @@
     plain = (((1,), (0,)), ((), ()))
     hot_own, turn_own = hot_of(named[0:1])
     got_own = lax.dot_general(own, hot_own, plain, preferred_element_type=F32)
-    lost = jnp.zeros((HOURS, 128), F32)
+    lost = [jnp.zeros((half, 128), F32)] * passes
     self_sens = jnp.zeros((1, 128), F32)
     for c in range(CAP):
         mine = turn_own == float(c)
-        lost = jnp.where(mine, got_own[HOURS * c : HOURS * c + HOURS], lost)
-        at = 448 + 8 * (c % 2) + c // 2
+        for p in range(passes):
+            at = 256 * p + half * c
+            lost[p] = jnp.where(mine, got_own[at : at + half], lost[p])
+        at = 512 + 8 * (c % 2) + c // 2
         self_sens = jnp.where(mine, got_own[at : at + 1], self_sens)
+    lost = jnp.concatenate(lost, axis=0)
     divisor = jnp.maximum(1.0 - self_sens, floor_value)
     off = jnp.concatenate([off_ref[...], off_ref[...]], axis=1)
     live = jnp.concatenate([live_ref[...], live_ref[...]], axis=1)
-    lost_scaled = lost
     row = iota((sub, 128), 0)
     for t in range(slots // 2):
         target = jnp.where(lane < outages, named[2 * t : 2 * t + 1], named[2 * t + 1 : 2 * t + 2])
@@ -362,12 +400,13 @@
         got = lax.dot_general(shared, hot, plain, preferred_element_type=F32)
         sens = jnp.zeros((sub, 128), F32)
         for c in range(CAP):
-            sens = jnp.where(turn == float(c), got[512 + sub * c : 512 + sub * c + sub], sens)
+            at = 512 + sub * c + (64 if c >= 8 else 0)
+            sens = jnp.where(turn == float(c), got[at : at + sub], sens)
         factor = sens / divisor
         worst = jnp.zeros((sub, 128), F32)
         for h in range(HOURS):
-            worst = jnp.maximum(worst, jnp.abs(got[sub * h : sub * h + sub] + factor * lost_scaled[h : h + 1]))
-        result = worst / got[720:736]
+            worst = jnp.maximum(worst, jnp.abs(got[sub * h : sub * h + sub] + factor * lost[h : h + 1]))
+        result = worst / got[784:800]
         slot = 2 * t + jnp.where(lane < outages, 0, 1)
         keep = slot < live
         if t == 0:
@@ -407,29 +446,47 @@
             named, outage_ends.T, off_row, live_row
         )
         asked = lax.all_to_all(requests, "line", split_axis=0, concat_axis=0, tiled=True)
+    pieces = bus_width // CHUNK + 1
+    with jax.named_scope("flows"):
+        mine = call(
+            flow_kernel,
+            shape((HOURS, block_rows), F32),
+            [IN_HBM, IN_HBM],
+            scratch=(
+                pltpu.VMEM((block_rows, bus_width), F32),
+                pltpu.VMEM((HOURS, bus_width), F32),
+                pltpu.VMEM((2 * HOURS, 2 * block_rows), F32),
+                pltpu.SemaphoreType.DMA((pieces,)),
+                pltpu.SemaphoreType.DMA((pieces,)),
+            ),
+            flops=8 * HOURS * block_rows * bus_width,
+            moved=4 * block_rows * bus_width,
+            limit=54,
+        )(shift_factors, injection)
+        other = lax.ppermute(mine, "bus_z", [(p, (p + 1) % passes) for p in range(passes)])
     with jax.named_scope("picks"):
         partial_sens = call(
             pick_kernel,
             shape((peers, passes * sub_rows + 8, entries), F32),
-            [IN_VMEM, IN_HBM, IN_HBM],
+            [IN_VMEM, IN_HBM],
             scratch=(
                 pltpu.VMEM((block_rows, bus_width), F32),
-                pltpu.VMEM((HOURS, bus_width), F32),
                 pltpu.VMEM((2 * block_rows, bus_width), BF16),
                 pltpu.VMEM((128, 128), F32),
                 pltpu.VMEM((PACKED, entries), BF16),
                 pltpu.VMEM((PACKED, 128), jnp.int16),
                 pltpu.VMEM((PACKED, 128), jnp.int16),
                 pltpu.VMEM((PACKED, 2 * block_rows), F32),
-                pltpu.VMEM((2 * HOURS, 2 * block_rows), F32),
                 pltpu.VMEM((block_rows, entries), F32),
-                pltpu.SemaphoreType.DMA((bus_width // CHUNK + 1,)),
-                pltpu.SemaphoreType.DMA((bus_width // CHUNK + 1,)),
+                pltpu.SemaphoreType.DMA((pieces,)),
             ),
             flops=4 * entries * block_rows * bus_width,
             moved=4 * block_rows * bus_width,
             limit=53,
-        )(asked, shift_factors, injection)
+        )(asked, shift_factors)
+        partial_sens = call(merge_kernel, shape((peers, passes * sub_rows + 8, entries), F32), [IN_VMEM] * 3)(
+            partial_sens, mine, other
+        )
         half_sens = lax.all_to_all(partial_sens, "bus_x", split_axis=0, concat_axis=0, tiled=True)
     with jax.named_scope("reply"):
         reply = call(

time: 77.5 us -> 76.6 us (0.988)
  blocking collectives: 68.9 us -> 42.5 us
  starting transfers between devices: 0 us -> 22.5 us
  Pallas kernels: 8.3 us -> 11.2 us
    all_to_all x1 -> x0, blocking collectives: 24.1 us -> none  [local(): lax.all_to_all(requests, 'line', split_axis=0, concat_axis=0, tiled=True)]
    all_to_all x0 -> x1, starting transfers between devices: none -> 14.6 us  [local(): lax.all_to_all(requests, 'line', split_axis=0, concat_axis=0, tiled=True)]
    ppermute x0 -> x1, starting transfers between devices: none -> 7.94 us  [local(): lax.ppermute(mine, 'bus_z', [(p, (p + 1) % passes) for p in range(passes)])]
    pallas_call x0 -> x2, Pallas kernels: none -> 3.79 us  [the longest x1 3.76 us: local(): call(flow_kernel, shape((HOURS, block_rows), F32), [IN_HBM, IN_HBM], scra...]
    all_to_all x1, blocking collectives: 32.8 us -> 30.5 us  [local(): lax.all_to_all(reply, ('bus_z', 'line'), split_axis=0, concat_axis=0, til...]
    pallas_call x1, Pallas kernels: 4.86 us -> 3.94 us  [local(): call(pick_kernel, shape((peers, passes * sub_rows + 8, entries), F32), [I...]
  transfers between devices with their start and end apart: 0 -> 2, of which waited for: 0 -> 0; matrix products, arithmetic and copies ran while one was open for 0% -> 0% of each run, Pallas kernels for 0% -> 10%
where the time goes in v6:
time: 76.6 us; the launch traced here: 76.4 us
  blocking collectives  42.5 us (55%)
  starting transfers between devices  22.5 us (29%)
  Pallas kernels  11.2 us (15%)
    all_to_all x1, blocking collectives, local(): lax.all_to_all(reply, ('bus_z', 'line'), split_axis=0, concat_axis=0, til...  30.5 us
    all_to_all x1, starting transfers between devices, local(): lax.all_to_all(requests, 'line', split_axis=0, concat_axis=0, tiled=True)  14.6 us
    all_to_all x1, blocking collectives, local(): lax.all_to_all(partial_sens, 'bus_x', split_axis=0, concat_axis=0, tiled=...  12 us
    ppermute x1, starting transfers between devices, local(): lax.ppermute(mine, 'bus_z', [(p, (p + 1) % passes) for p in range(passes)])  7.94 us
    pallas_call x1, Pallas kernels, local(): call(pick_kernel, shape((peers, passes * sub_rows + 8, entries), F32), [I...  3.94 us
    pallas_call x1, Pallas kernels, local(): call(flow_kernel, shape((HOURS, block_rows), F32), [IN_HBM, IN_HBM], scra...  3.76 us
    pallas_call x1, Pallas kernels, local(): call(request_kernel, shape((line_count, 128), F32), [IN_VMEM] * 4, limit=56)  1.82 us
  transfers between devices with their start and end apart: 2, of which 0 were waited for; matrix products, arithmetic and copies ran while one was open for 0% of the time, Pallas kernels for 10%

profile of v6, /device:TPU:1, one launch (start us, length us, event | category | flops | bytes accessed | tf_op | source)
XLA Modules:
  0.0 76.4 jit_solution(6496583587359300070)
XLA Ops:
  0.0 1.8 %requests.1 = f32[64,128]{1,0:T(8,128)} custom-call(s32[8,64]{1,0:T(8,128)} %bitcast.16, s32[2,64]{1,0:T(2,128)} %bitcast.24, s32[1,64]{1,0:T(1,128)} %bitcast.18, s32[1,64]{1,0:T(1,128)} %bitcast.20), custom_call_target="tpu_custom_call" | custom-call | tf_op jit(solution)/shard_map/requests/pallas_call | solution.py:445
  1.8 14.6 %all-to-all-start = ((f32[64,1,128]{2,1,0:T(1,128)}), f32[64,1,128]{2,1,0:T(1,128)S(1)}, u32[]{:S(2)}, u32[]{:S(2)}) async-start(f32[64,1,128]{2,1,0:T(1,128)} %bitcast.23), calls=%async_computation | async-start | bytes 65536 | tf_op jit(solution)/shard_map/requests/all_to_all | solution.py:448
  16.4 3.8 %flows.1.mine_ref = f32[32,128]{1,0:T(8,128)} custom-call(f32[128,7552]{1,0:T(8,128)} %s_hbm.3, f32[32,7552]{1,0:T(8,128)} %inj_hbm.1), custom_call_target="tpu_custom_call" | custom-call | flops 247463936 | bytes 3866624 | tf_op jit(solution)/shard_map/flows/pallas_call | solution.py:451
  20.2 7.9 %collective-permute-start = (f32[32,128]{1,0:T(8,128)}, f32[32,128]{1,0:T(8,128)S(1)}, u32[]{:S(2)}, u32[]{:S(2)}) collective-permute-start(f32[32,128]{1,0:T(8,128)} %flows.1.mine_ref), channel_id=1, source_target_pairs={{0,1},{1,0},{2,3},{3,2},{4,5},{5,4},{6,7},{7,6},{8,9},{9,8},{10,11... | collective-permute-start | bytes 49160 | tf_op jit(solution)/shard_map/flows/ppermute | solution.py:466
  28.1 0.0 all-to-all-done
  28.1 0.0 copy-start
  28.1 0.0 copy-start.4
  28.2 0.0 copy-start.1
  28.2 0.0 copy-start.2
  28.2 0.0 copy-start.3
  28.2 3.9 %picks.2.message_ref = f32[4,40,768]{2,1,0:T(8,128)S(1)} custom-call(f32[64,128]{1,0:T(8,128)S(1)} %bitcast.14, f32[128,7552]{1,0:T(8,128)} %s_hbm.3), custom_call_target="tpu_custom_call" | custom-call | flops 2969567232 | bytes 3866624 | tf_op jit(solution)/shard_map/picks/pallas_call | solution.py:468
  32.1 0.0 collective-permute-done.other_ref
  32.2 0.0 copy-done
  32.2 12.0 %all_to_all.25.got_ref = f32[4,40,768]{2,1,0:T(8,128)S(1)} all-to-all(f32[4,40,768]{2,1,0:T(8,128)S(1)} %picks.3), channel_id=1, replica_groups=mesh['line'=64,'bus_x'=4,'bus_z'=2] {'bus_x'}, dimensions={0} | all-to-all | bytes 983040 | tf_op jit(solution)/shard_map/picks/all_to_all | solution.py:490
  44.2 0.0 copy-done.4
  44.2 0.4 reply.1
  44.6 30.5 %all_to_all.26 = f32[128,1,768]{2,1,0:T(1,128)S(1)} all-to-all(f32[128,1,768]{2,1,0:T(1,128)S(1)} %bitcast.12), channel_id=1, replica_groups=mesh['line'=64,'bus_x'=4,'bus_z'=2] {'bus_z','line'}, dimensions={0} | all-to-all | bytes 786432 | tf_op jit(solution)/shard_map/reply/all_to_all | solution.py:499
  75.1 0.0 copy-done.1
  75.1 0.0 copy-done.2
  75.1 0.0 copy-done.3
  75.1 1.3 %screen.1 = f32[8,16,64]{2,1,0:T(8,128)} custom-call(f32[768,128]{1,0:T(8,128)S(1)} %bitcast.13, s32[8,64]{1,0:T(8,128)S(1)} %bitcast.17, s32[1,64]{1,0:T(1,128)S(1)} %bitcast.19, s32[1,64]{1,0:T(1,128)S(1)} %bitcast.21), custom_call_target="tpu_custom_call" | custom-call | tf_op jit(solution)/shard_map/screen/pallas_call | solution.py:501
  (1 shorter events, 0.0 us)
Async XLA Ops:
  1.8 26.3 %all-to-all-start = ((f32[64,1,128]{2,1,0:T(1,128)}), f32[64,1,128]{2,1,0:T(1,128)S(1)}, u32[]{:S(2)}, u32[]{:S(2)}) async-start(f32[64,1,128]{2,1,0:T(1,128)} %bitcast.23), calls=%async_computation | async-start | bytes 65536 | tf_op jit(solution)/shard_map/requests/all_to_all | solution.py:448
  20.2 12.0 %collective-permute-start = (f32[32,128]{1,0:T(8,128)}, f32[32,128]{1,0:T(8,128)S(1)}, u32[]{:S(2)}, u32[]{:S(2)}) collective-permute-start(f32[32,128]{1,0:T(8,128)} %flows.1.mine_ref), channel_id=1, source_target_pairs={{0,1},{1,0},{2,3},{3,2},{4,5},{5,4},{6,7},{7,6},{8,9},{9,8},{10,11... | collective-permute-start | bytes 49160 | tf_op jit(solution)/shard_map/flows/ppermute | solution.py:466
  28.1 4.0 %copy-start = (f32[32,128]{1,0:T(8,128)S(1)}, f32[32,128]{1,0:T(8,128)}, u32[]{:S(2)}) copy-start(f32[32,128]{1,0:T(8,128)} %flows.1.mine_ref) | copy-start | bytes 49156
  28.1 16.0 %copy-start.4 = (f32[128]{0:T(128)S(1)}, f32[128]{0:T(128)}, u32[]{:S(2)}) copy-start(f32[128]{0:T(128)} %param.9) | copy-start | bytes 1540
  28.2 46.9 %copy-start.1 = (s32[64,8]{0,1:T(8,128)S(1)}, s32[64,8]{0,1:T(8,128)}, u32[]{:S(2)}) copy-start(s32[64,8]{0,1:T(8,128)} %param.10) | copy-start | bytes 6148
  28.2 46.9 %copy-start.2 = (s32[64]{0:T(128)S(1)}, s32[64]{0:T(128)}, u32[]{:S(2)}) copy-start(s32[64]{0:T(128)} %param.12) | copy-start | bytes 772
  28.2 46.9 %copy-start.3 = (s32[64]{0:T(128)S(1)}, s32[64]{0:T(128)}, u32[]{:S(2)}) copy-start(s32[64]{0:T(128)} %param.11) | copy-start | bytes 772

commit v7 on v5

--- a/solution.py
+++ b/solution.py
@@ -17,7 +17,6 @@
 TILES = 9
 PACKED = 256
 IN_VMEM = pl.BlockSpec(memory_space=pltpu.VMEM)
-IN_HBM = pl.BlockSpec(memory_space=pltpu.HBM)
 
 
 def iota(shape, axis):
@@ -29,16 +28,15 @@
     return high, (value - high.astype(F32)).astype(BF16)
 
 
-def request_kernel(mon_ref, ends_ref, off_ref, live_ref, out_ref):
-    slots, outages = mon_ref.shape
+def request_kernel(table_ref, out_ref):
+    outages = table_ref.shape[1]
+    slots = table_ref.shape[0] - 4
     lines = out_ref.shape[0]
-
-    def twice(row):
-        return jnp.concatenate([row, row], axis=1)
-
-    named = twice(mon_ref[...])
+    table = table_ref[...]
+    table = jnp.concatenate([table, table], axis=1)
+    named = table[:slots]
     line_row = iota((lines, 128), 0)
-    live = twice(live_ref[...])
+    live = table[slots + 3 : slots + 4]
     names = jnp.zeros((lines, 128), F32)
     asks = jnp.zeros((lines, 128), F32)
     for s in range(slots):
@@ -50,9 +48,9 @@
         names.astype(BF16), jnp.where(earlier, 1.0, 0.0).astype(BF16), NN, preferred_element_type=F32
     )
     rank = jnp.where(asks > 0.0, rank, -1.0)
-    start = twice(ends_ref[0:1, :]) + 1
-    end = twice(ends_ref[1:2, :]) + 1
-    place = twice(off_ref[...]) + 1
+    start = table[slots : slots + 1] + 1
+    end = table[slots + 1 : slots + 2] + 1
+    place = table[slots + 2 : slots + 3] + 1
     second = iota((1, 128), 1) // outages
     spot = iota((128, 128), 0)
     chosen, high, low = [], [], []
@@ -72,11 +70,9 @@
 
 def pick_kernel(
     req_ref,
-    s_hbm,
-    inj_hbm,
-    out_ref,
     s_ref,
     inj_ref,
+    out_ref,
     split_ref,
     turn_ref,
     perm_ref,
@@ -85,8 +81,6 @@
     sum_ref,
     flow_ref,
     total_ref,
-    s_sems,
-    inj_sems,
 ):
     lines = req_ref.shape[0]
     rows, width = s_ref.shape
@@ -95,24 +89,6 @@
     deep = rows // peers
     whole, rest = width // CHUNK, width % CHUNK
 
-    def copies(at, size, q):
-        cols = pl.ds(at, size)
-        return (
-            pltpu.make_async_copy(s_hbm.at[:, cols], s_ref.at[:, cols], s_sems.at[q]),
-            pltpu.make_async_copy(inj_hbm.at[:, cols], inj_ref.at[:, cols], inj_sems.at[q]),
-        )
-
-    def fetch(at, size, q):
-        for copy in copies(at, size, q):
-            copy.start()
-
-    def arrive(at, size, q):
-        for copy in copies(at, size, q):
-            copy.wait()
-
-    fetch(whole * CHUNK, rest, whole)
-    for q in range(whole):
-        fetch(q * CHUNK, CHUNK, q)
     bus = lax.axis_index("bus_x") * lax.axis_size("bus_z") + lax.axis_index("bus_z")
     base = (bus * width + 1).astype(F32)
     req = req_ref[...]
@@ -197,12 +173,10 @@
         pick(at, size)
 
     open_block(0)
-    arrive(whole * CHUNK, rest, whole)
     step(whole * CHUNK, rest)
 
     def first_block(q, carry):
         at = pl.multiple_of(q * CHUNK, CHUNK)
-        arrive(at, CHUNK, q)
         step(at, CHUNK)
         return carry
 
@@ -279,7 +253,7 @@
         return jnp.concatenate([block, jnp.zeros((block.shape[0], 128 - lines), F32)], axis=1)
 
     def put(p, q, block):
-        out_ref[pl.ds(p * lines * TILES + q, lines, stride=TILES), :] = block
+        out_ref[pl.ds(p * TILES + q, lines, stride=passes * TILES), :] = block
 
     for p in range(passes):
         wanted = iota((128, 128), 0) == (place + p) * sub + iota((128, 128), 1) % sub
@@ -304,23 +278,23 @@
         put(p, 8, jnp.transpose(two)[:lines])
 
 
-def screen_kernel(got_ref, mon_ref, off_ref, live_ref, out_ref):
-    slots, outages = mon_ref.shape
-    sub = out_ref.shape[1]
+def screen_kernel(got_ref, table_ref, out_ref):
+    slots, sub, outages = out_ref.shape
     passes = lax.axis_size("bus_z")
     lines = got_ref.shape[0] // (passes * TILES)
     place = lax.axis_index("bus_x") * passes + lax.axis_index("bus_z")
     pieces = []
     for t in range(TILES):
-        block = got_ref[pl.ds(t, lines, stride=TILES), :]
+        block = got_ref[pl.ds(t, lines, stride=passes * TILES), :]
         for p in range(1, passes):
-            block = block + got_ref[pl.ds(p * lines * TILES + t, lines, stride=TILES), :]
+            block = block + got_ref[pl.ds(p * TILES + t, lines, stride=passes * TILES), :]
         high = block.astype(BF16).astype(F32)
         low = (block - high).astype(BF16).astype(F32)
         pieces.append(jnp.transpose(jnp.concatenate([high, low], axis=0)).astype(BF16))
     shared = jnp.concatenate(pieces[:4] + pieces[7:], axis=0)
     own = jnp.concatenate(pieces[4:7] + pieces[8:], axis=0)
-    named = jnp.concatenate([mon_ref[...], mon_ref[...]], axis=1)
+    table = jnp.concatenate([table_ref[...], table_ref[...]], axis=1)
+    named = table[:slots]
     line_row = iota((lines, 128), 0)
     lane = iota((1, 128), 1)
     outage = lane % outages
@@ -352,8 +326,8 @@
         at = 448 + 8 * (c % 2) + c // 2
         self_sens = jnp.where(mine, got_own[at : at + 1], self_sens)
     divisor = jnp.maximum(1.0 - self_sens, floor_value)
-    off = jnp.concatenate([off_ref[...], off_ref[...]], axis=1)
-    live = jnp.concatenate([live_ref[...], live_ref[...]], axis=1)
+    off = table[slots + 2 : slots + 3]
+    live = table[slots + 3 : slots + 4]
     lost_scaled = lost
     row = iota((sub, 128), 0)
     for t in range(slots // 2):
@@ -398,23 +372,21 @@
     outages, slot_count = monitored.shape
     entries = CAP * line_count
     shape = jax.ShapeDtypeStruct
-    off_row = outage_offset.reshape(1, outages)
-    live_row = live_count.reshape(1, outages)
     rate_row = rating.reshape(1, block_rows)
-    named = monitored.T
+    table = jnp.concatenate(
+        [monitored.T, outage_ends.T, outage_offset.reshape(1, outages), live_count.reshape(1, outages)], axis=0
+    )
     with jax.named_scope("requests"):
-        requests = call(request_kernel, shape((line_count, 128), F32), [IN_VMEM] * 4, limit=56)(
-            named, outage_ends.T, off_row, live_row
+        requests = call(request_kernel, shape((line_count, 128), F32), [IN_VMEM], flops=10**10, moved=10**7)(
+            table
         )
         asked = lax.all_to_all(requests, "line", split_axis=0, concat_axis=0, tiled=True)
     with jax.named_scope("picks"):
         partial_sens = call(
             pick_kernel,
             shape((peers, passes * sub_rows + 8, entries), F32),
-            [IN_VMEM, IN_HBM, IN_HBM],
+            [IN_VMEM] * 3,
             scratch=(
-                pltpu.VMEM((block_rows, bus_width), F32),
-                pltpu.VMEM((HOURS, bus_width), F32),
                 pltpu.VMEM((2 * block_rows, bus_width), BF16),
                 pltpu.VMEM((128, 128), F32),
                 pltpu.VMEM((PACKED, entries), BF16),
@@ -423,12 +395,10 @@
                 pltpu.VMEM((PACKED, 2 * block_rows), F32),
                 pltpu.VMEM((2 * HOURS, 2 * block_rows), F32),
                 pltpu.VMEM((block_rows, entries), F32),
-                pltpu.SemaphoreType.DMA((bus_width // CHUNK + 1,)),
-                pltpu.SemaphoreType.DMA((bus_width // CHUNK + 1,)),
             ),
             flops=4 * entries * block_rows * bus_width,
             moved=4 * block_rows * bus_width,
-            limit=53,
+            limit=24,
         )(asked, shift_factors, injection)
         half_sens = lax.all_to_all(partial_sens, "bus_x", split_axis=0, concat_axis=0, tiled=True)
     with jax.named_scope("reply"):
@@ -439,10 +409,10 @@
             scratch=(pltpu.VMEM((block_rows, block_rows), F32),),
         )(half_sens, asked, rate_row)
         reply = reply.reshape(passes * line_count, TILES * 128)
-        got = lax.all_to_all(reply, ("bus_z", "line"), split_axis=0, concat_axis=0, tiled=True)
+        got = lax.all_to_all(reply, ("line", "bus_z"), split_axis=0, concat_axis=0, tiled=True)
     with jax.named_scope("screen"):
-        loading = call(screen_kernel, shape((slot_count, sub_rows, outages), F32), [IN_VMEM] * 4)(
-            got.reshape(-1, 128), named, off_row, live_row
+        loading = call(screen_kernel, shape((slot_count, sub_rows, outages), F32), [IN_VMEM] * 2)(
+            got.reshape(-1, 128), table
         )
     return jnp.transpose(loading, (2, 0, 1))
 

time: 77.5 us -> 75.7 us (0.977)
  Pallas kernels: 8.3 us -> 6.36 us
    pallas_call x1, Pallas kernels: 1.82 us -> 0.49 us  [local(): call(request_kernel, shape((line_count, 128), F32), [IN_VMEM], flops=10 *...]
where the time goes in v7:
time: 75.7 us; the launch traced here: 75.5 us
  blocking collectives  68.4 us (90%)
  Pallas kernels  6.36 us (8%)
    all_to_all x1, blocking collectives, local(): lax.all_to_all(reply, ('line', 'bus_z'), split_axis=0, concat_axis=0, til...  32.1 us
    all_to_all x1, blocking collectives, local(): lax.all_to_all(requests, 'line', split_axis=0, concat_axis=0, tiled=True)  24.3 us
    all_to_all x1, blocking collectives, local(): lax.all_to_all(partial_sens, 'bus_x', split_axis=0, concat_axis=0, tiled=...  12 us
    pallas_call x1, Pallas kernels, local(): call(pick_kernel, shape((peers, passes * sub_rows + 8, entries), F32), [I...  4.26 us

profile of v7, /device:TPU:1, one launch (start us, length us, event | category | flops | bytes accessed | tf_op | source)
XLA Modules:
  0.0 75.5 jit_solution(8443116217139892857)
XLA Ops:
  0.0 0.7 pad_add_fusion.table_ref
  0.7 0.0 copy-start.1
  0.8 0.0 copy-start.2
  0.8 0.5 requests.1
  1.3 24.3 %all_to_all.25 = f32[64,1,128]{2,1,0:T(1,128)S(1)} all-to-all(f32[64,1,128]{2,1,0:T(1,128)S(1)} %bitcast.16), channel_id=1, replica_groups=mesh['line'=64,'bus_x'=4,'bus_z'=2] {'line'}, dimensions={0} | all-to-all | bytes 65536 | tf_op jit(solution)/shard_map/requests/all_to_all | solution.py:383
  25.5 0.0 copy-done.1
  25.5 0.0 copy-done.2
  25.5 0.0 copy-start
  25.6 4.3 %picks.1 = f32[4,40,768]{2,1,0:T(8,128)S(1)} custom-call(f32[64,128]{1,0:T(8,128)S(1)} %bitcast.14, f32[128,7552]{1,0:T(8,128)S(1)} %copy-done.1, f32[32,7552]{1,0:T(8,128)S(1)} %copy-done.2), custom_call_target="tpu_custom_call" | custom-call | flops 2969567232 | bytes 3866624 | tf_op jit(solution)/shard_map/picks/pallas_call | solution.py:385
  29.8 12.0 %all_to_all.26.got_ref = f32[4,40,768]{2,1,0:T(8,128)S(1)} all-to-all(f32[4,40,768]{2,1,0:T(8,128)S(1)} %picks.1), channel_id=1, replica_groups=mesh['line'=64,'bus_x'=4,'bus_z'=2] {'bus_x'}, dimensions={0} | all-to-all | bytes 983040 | tf_op jit(solution)/shard_map/picks/all_to_all | solution.py:403
  41.9 0.0 copy-done
  41.9 0.4 reply.1
  42.3 32.1 %all_to_all.27 = f32[128,1,1152]{2,1,0:T(1,128)S(1)} all-to-all(f32[128,1,1152]{2,1,0:T(1,128)S(1)} %bitcast.12), channel_id=1, replica_groups=mesh['line'=64,'bus_x'=4,'bus_z'=2] {'line','bus_z'}, dimensions={0} | all-to-all | bytes 1179648 | tf_op jit(solution)/shard_map/reply/all_to_all | solution.py:412
  74.3 1.2 %screen.1 = f32[8,16,64]{2,1,0:T(8,128)} custom-call(f32[1152,128]{1,0:T(8,128)S(1)} %bitcast.13, s32[12,64]{1,0:T(8,128)S(1)} %pad_add_fusion.table_ref), custom_call_target="tpu_custom_call" | custom-call | tf_op jit(solution)/shard_map/screen/pallas_call | solution.py:414
Async XLA Ops:
  0.7 24.8 %copy-start.1 = (f32[128,7552]{1,0:T(8,128)S(1)}, f32[128,7552]{1,0:T(8,128)}, u32[]{:S(2)}) copy-start(f32[128,7552]{1,0:T(8,128)} %s_ref.1) | copy-start | bytes 11599876
  0.8 24.8 %copy-start.2 = (f32[32,7552]{1,0:T(8,128)S(1)}, f32[32,7552]{1,0:T(8,128)}, u32[]{:S(2)}) copy-start(f32[32,7552]{1,0:T(8,128)} %inj_ref.1) | copy-start | bytes 2899972
  25.5 16.3 %copy-start = (f32[128]{0:T(128)S(1)}, f32[128]{0:T(128)}, u32[]{:S(2)}) copy-start(f32[128]{0:T(128)} %param.9) | copy-start | bytes 1540

commit v8 on v7

--- a/solution.py
+++ b/solution.py
@@ -15,7 +15,7 @@
 CHUNK = 2304
 PASS = 2
 TILES = 9
-PACKED = 256
+PACKED = 160
 IN_VMEM = pl.BlockSpec(memory_space=pltpu.VMEM)
 
 
@@ -73,13 +73,11 @@
     s_ref,
     inj_ref,
     out_ref,
-    split_ref,
     turn_ref,
     perm_ref,
     from_ref,
     to_ref,
     sum_ref,
-    flow_ref,
     total_ref,
 ):
     lines = req_ref.shape[0]
@@ -131,7 +129,6 @@
     offs = table[5:6].astype(jnp.int32) - 1
     table_low = table.astype(BF16)
     one, minus, zero = jnp.asarray(1, BF16), jnp.asarray(-1, BF16), jnp.asarray(0, BF16)
-    flow_ref[...] = jnp.zeros_like(flow_ref)
     total_ref[...] = jnp.zeros_like(total_ref)
 
     def open_block(block):
@@ -144,7 +141,7 @@
         to_ref[...] = jnp.broadcast_to(end, (packed, 128)).astype(jnp.int16)
         sum_ref[...] = jnp.zeros_like(sum_ref)
 
-    def pick(at, size):
+    def hot(at, size):
         columns = []
         for t in range(size // 128):
             spot = (iota((16, 128), 1) + (at + t * 128)).astype(jnp.int16)
@@ -152,25 +149,25 @@
             columns.append(
                 jnp.where(from_ref[...] == spot, one, jnp.where(to_ref[...] == spot, minus, zero))
             )
-        sum_ref[...] += lax.dot_general(
-            jnp.concatenate(columns, axis=1), split_ref[:, pl.ds(at, size)], NT, preferred_element_type=F32
-        )
+        return jnp.concatenate(columns, axis=1)
+
+    def multiply(left, at, size):
+        both = jnp.concatenate(split2(s_ref[:, pl.ds(at, size)]), axis=0)
+        return lax.dot_general(left, both, NT, preferred_element_type=F32)
 
     def close_block():
-        turned = jnp.transpose(sum_ref[:, :rows] + sum_ref[:, rows:])
+        turned = jnp.transpose(sum_ref[:packed, :rows] + sum_ref[:packed, rows:])
         both = lax.dot_general(
             jnp.concatenate(split2(turned), axis=0), perm_ref[...], NN, preferred_element_type=F32
         )
         total_ref[...] += both[:rows] + both[rows:]
 
     def step(at, size):
-        cols = pl.ds(at, size)
-        both = jnp.concatenate(split2(s_ref[:, cols]), axis=0)
-        split_ref[:, cols] = both
-        flow_ref[...] += lax.dot_general(
-            jnp.concatenate(split2(inj_ref[:, cols]), axis=0), both, NT, preferred_element_type=F32
-        )
-        pick(at, size)
+        left = jnp.concatenate((hot(at, size),) + split2(inj_ref[:, pl.ds(at, size)]), axis=0)
+        sum_ref[...] += multiply(left, at, size)
+
+    def pick(at, size):
+        sum_ref[:packed] += multiply(hot(at, size), at, size)
 
     open_block(0)
     step(whole * CHUNK, rest)
@@ -181,6 +178,10 @@
         return carry
 
     lax.fori_loop(0, whole, first_block, 0)
+    flows = sum_ref[packed:]
+    part = (
+        flows[:HOURS, :rows] + (flows[:HOURS, rows:] + flows[HOURS:, :rows]) + flows[HOURS:, rows:]
+    )
     close_block()
 
     def other_block(block, carry):
@@ -196,11 +197,6 @@
         return carry
 
     lax.fori_loop(1, blocks, other_block, 0)
-    part = (
-        flow_ref[:HOURS, :rows]
-        + (flow_ref[:HOURS, rows:] + flow_ref[HOURS:, :rows])
-        + flow_ref[HOURS:, rows:]
-    )
     total = total_ref[...]
     own = jnp.sum(jnp.where(iota((rows, entries), 0) == offs, total, 0.0), axis=0, keepdims=True)
     own = [own[:, 128 * t : 128 * t + 128] for t in range(CAP // 2)] + [jnp.zeros((2, 128), F32)]
@@ -387,13 +383,11 @@
             shape((peers, passes * sub_rows + 8, entries), F32),
             [IN_VMEM] * 3,
             scratch=(
-                pltpu.VMEM((2 * block_rows, bus_width), BF16),
                 pltpu.VMEM((128, 128), F32),
                 pltpu.VMEM((PACKED, entries), BF16),
                 pltpu.VMEM((PACKED, 128), jnp.int16),
                 pltpu.VMEM((PACKED, 128), jnp.int16),
-                pltpu.VMEM((PACKED, 2 * block_rows), F32),
-                pltpu.VMEM((2 * HOURS, 2 * block_rows), F32),
+                pltpu.VMEM((PACKED + 2 * HOURS, 2 * block_rows), F32),
                 pltpu.VMEM((block_rows, entries), F32),
             ),
             flops=4 * entries * block_rows * bus_width,

time: 75.7 us -> 74.9 us (0.989)
  Pallas kernels: 6.36 us -> 5.51 us
    pallas_call x1, Pallas kernels: 4.26 us -> 3.41 us  [local(): call(pick_kernel, shape((peers, passes * sub_rows + 8, entries), F32), [I...]
where the time goes in v8:
time: 74.9 us; the launch traced here: 74.7 us
  blocking collectives  68.4 us (91%)
  Pallas kernels  5.51 us (7%)
    all_to_all x1, blocking collectives, local(): lax.all_to_all(reply, ('line', 'bus_z'), split_axis=0, concat_axis=0, til...  32.1 us
    all_to_all x1, blocking collectives, local(): lax.all_to_all(requests, 'line', split_axis=0, concat_axis=0, tiled=True)  24.3 us
    all_to_all x1, blocking collectives, local(): lax.all_to_all(partial_sens, 'bus_x', split_axis=0, concat_axis=0, tiled=...  12 us
    pallas_call x1, Pallas kernels, local(): call(pick_kernel, shape((peers, passes * sub_rows + 8, entries), F32), [I...  3.41 us

profile of v8, /device:TPU:1, one launch (start us, length us, event | category | flops | bytes accessed | tf_op | source)
XLA Modules:
  0.0 74.7 jit_solution(5563531295666690637)
XLA Ops:
  0.0 0.7 pad_add_fusion.table_ref
  0.7 0.0 copy-start.1
  0.8 0.0 copy-start.2
  0.8 0.5 requests.1
  1.3 24.3 %all_to_all.25 = f32[64,1,128]{2,1,0:T(1,128)S(1)} all-to-all(f32[64,1,128]{2,1,0:T(1,128)S(1)} %bitcast.16), channel_id=1, replica_groups=mesh['line'=64,'bus_x'=4,'bus_z'=2] {'line'}, dimensions={0} | all-to-all | bytes 65536 | tf_op jit(solution)/shard_map/requests/all_to_all | solution.py:379
  25.5 0.0 copy-done.1
  25.5 0.0 copy-done.2
  25.5 0.0 copy-start
  25.6 3.4 %picks.1 = f32[4,40,768]{2,1,0:T(8,128)S(1)} custom-call(f32[64,128]{1,0:T(8,128)S(1)} %bitcast.14, f32[128,7552]{1,0:T(8,128)S(1)} %copy-done.1, f32[32,7552]{1,0:T(8,128)S(1)} %copy-done.2), custom_call_target="tpu_custom_call" | custom-call | flops 2969567232 | bytes 3866624 | tf_op jit(solution)/shard_map/picks/pallas_call | solution.py:381
  29.0 12.0 %all_to_all.26.got_ref = f32[4,40,768]{2,1,0:T(8,128)S(1)} all-to-all(f32[4,40,768]{2,1,0:T(8,128)S(1)} %picks.1), channel_id=1, replica_groups=mesh['line'=64,'bus_x'=4,'bus_z'=2] {'bus_x'}, dimensions={0} | all-to-all | bytes 983040 | tf_op jit(solution)/shard_map/picks/all_to_all | solution.py:397
  41.0 0.0 copy-done
  41.0 0.4 reply.1
  41.4 32.1 %all_to_all.27 = f32[128,1,1152]{2,1,0:T(1,128)S(1)} all-to-all(f32[128,1,1152]{2,1,0:T(1,128)S(1)} %bitcast.12), channel_id=1, replica_groups=mesh['line'=64,'bus_x'=4,'bus_z'=2] {'line','bus_z'}, dimensions={0} | all-to-all | bytes 1179648 | tf_op jit(solution)/shard_map/reply/all_to_all | solution.py:406
  73.4 1.2 %screen.1 = f32[8,16,64]{2,1,0:T(8,128)} custom-call(f32[1152,128]{1,0:T(8,128)S(1)} %bitcast.13, s32[12,64]{1,0:T(8,128)S(1)} %pad_add_fusion.table_ref), custom_call_target="tpu_custom_call" | custom-call | tf_op jit(solution)/shard_map/screen/pallas_call | solution.py:408
Async XLA Ops:
  0.7 24.8 %copy-start.1 = (f32[128,7552]{1,0:T(8,128)S(1)}, f32[128,7552]{1,0:T(8,128)}, u32[]{:S(2)}) copy-start(f32[128,7552]{1,0:T(8,128)} %s_ref.1) | copy-start | bytes 11599876
  0.8 24.8 %copy-start.2 = (f32[32,7552]{1,0:T(8,128)S(1)}, f32[32,7552]{1,0:T(8,128)}, u32[]{:S(2)}) copy-start(f32[32,7552]{1,0:T(8,128)} %inj_ref.1) | copy-start | bytes 2899972
  25.5 15.4 %copy-start = (f32[128]{0:T(128)S(1)}, f32[128]{0:T(128)}, u32[]{:S(2)}) copy-start(f32[128]{0:T(128)} %param.9) | copy-start | bytes 1540

commit v9 on v8

--- a/solution.py
+++ b/solution.py
@@ -12,7 +12,7 @@
 NN = (((1,), (0,)), ((), ()))
 HOURS = 32
 CAP = 12
-CHUNK = 2304
+CHUNK = 3072
 PASS = 2
 TILES = 9
 PACKED = 160

time: 74.9 us -> 74.6 us (level)
  no operation moved by 1% of the time
where the time goes in v9:
time: 74.6 us; the launch traced here: 74.4 us
  blocking collectives  68.4 us (92%)
  Pallas kernels  5.25 us (7%)
    all_to_all x1, blocking collectives, local(): lax.all_to_all(reply, ('line', 'bus_z'), split_axis=0, concat_axis=0, til...  32 us
    all_to_all x1, blocking collectives, local(): lax.all_to_all(requests, 'line', split_axis=0, concat_axis=0, tiled=True)  24.3 us
    all_to_all x1, blocking collectives, local(): lax.all_to_all(partial_sens, 'bus_x', split_axis=0, concat_axis=0, tiled=...  12.1 us
    pallas_call x1, Pallas kernels, local(): call(pick_kernel, shape((peers, passes * sub_rows + 8, entries), F32), [I...  3.16 us

profile of v9, /device:TPU:1, one launch (start us, length us, event | category | flops | bytes accessed | tf_op | source)
XLA Modules:
  0.0 74.4 jit_solution(17482238314721332960)
XLA Ops:
  0.0 0.7 %pad_add_fusion.table_ref = s32[12,64]{1,0:T(8,128)S(1)} fusion(s32[1,64]{1,0:T(1,128)} %bitcast.20, s32[1,64]{1,0:T(1,128)} %bitcast.21, s32[2,64]{1,0:T(2,128)} %bitcast.19, s32[8,64]{1,0:T(8,128)} %bitcast.18), kind=kLoop, calls=%fused_computation | loop fusion | flops 2304 | bytes 6144 | tf_op jit(solution)/shard_map/concatenate | solution.py:372
  0.7 0.0 copy-start.1
  0.8 0.0 copy-start.2
  0.8 0.5 requests.1
  1.3 24.3 %all_to_all.25 = f32[64,1,128]{2,1,0:T(1,128)S(1)} all-to-all(f32[64,1,128]{2,1,0:T(1,128)S(1)} %bitcast.16), channel_id=1, replica_groups=mesh['line'=64,'bus_x'=4,'bus_z'=2] {'line'}, dimensions={0} | all-to-all | bytes 65536 | tf_op jit(solution)/shard_map/requests/all_to_all | solution.py:379
  25.5 0.0 copy-done.1
  25.5 0.0 copy-done.2
  25.5 0.0 copy-start
  25.6 3.2 %picks.1 = f32[4,40,768]{2,1,0:T(8,128)S(1)} custom-call(f32[64,128]{1,0:T(8,128)S(1)} %bitcast.14, f32[128,7552]{1,0:T(8,128)S(1)} %copy-done.1, f32[32,7552]{1,0:T(8,128)S(1)} %copy-done.2), custom_call_target="tpu_custom_call" | custom-call | flops 2969567232 | bytes 3866624 | tf_op jit(solution)/shard_map/picks/pallas_call | solution.py:381
  28.7 12.1 %all_to_all.26.got_ref = f32[4,40,768]{2,1,0:T(8,128)S(1)} all-to-all(f32[4,40,768]{2,1,0:T(8,128)S(1)} %picks.1), channel_id=1, replica_groups=mesh['line'=64,'bus_x'=4,'bus_z'=2] {'bus_x'}, dimensions={0} | all-to-all | bytes 983040 | tf_op jit(solution)/shard_map/picks/all_to_all | solution.py:397
  40.8 0.0 copy-done
  40.8 0.4 reply.1
  41.2 32.0 %all_to_all.27 = f32[128,1,1152]{2,1,0:T(1,128)S(1)} all-to-all(f32[128,1,1152]{2,1,0:T(1,128)S(1)} %bitcast.12), channel_id=1, replica_groups=mesh['line'=64,'bus_x'=4,'bus_z'=2] {'line','bus_z'}, dimensions={0} | all-to-all | bytes 1179648 | tf_op jit(solution)/shard_map/reply/all_to_all | solution.py:406
  73.2 1.2 %screen.1 = f32[8,16,64]{2,1,0:T(8,128)} custom-call(f32[1152,128]{1,0:T(8,128)S(1)} %bitcast.13, s32[12,64]{1,0:T(8,128)S(1)} %pad_add_fusion.table_ref), custom_call_target="tpu_custom_call" | custom-call | tf_op jit(solution)/shard_map/screen/pallas_call | solution.py:408
Async XLA Ops:
  0.7 24.8 %copy-start.1 = (f32[128,7552]{1,0:T(8,128)S(1)}, f32[128,7552]{1,0:T(8,128)}, u32[]{:S(2)}) copy-start(f32[128,7552]{1,0:T(8,128)} %s_ref.1) | copy-start | bytes 11599876
  0.8 24.8 %copy-start.2 = (f32[32,7552]{1,0:T(8,128)S(1)}, f32[32,7552]{1,0:T(8,128)}, u32[]{:S(2)}) copy-start(f32[32,7552]{1,0:T(8,128)} %inj_ref.1) | copy-start | bytes 2899972
  25.5 15.2 %copy-start = (f32[128]{0:T(128)S(1)}, f32[128]{0:T(128)}, u32[]{:S(2)}) copy-start(f32[128]{0:T(128)} %param.9) | copy-start | bytes 1540

commit v10 on v6

--- a/solution.py
+++ b/solution.py
@@ -12,10 +12,10 @@
 NN = (((1,), (0,)), ((), ()))
 HOURS = 32
 CAP = 12
-CHUNK = 2304
+CHUNK = 3072
 PASS = 2
 TILES = 6
-PACKED = 256
+PACKED = 160
 IN_VMEM = pl.BlockSpec(memory_space=pltpu.VMEM)
 IN_HBM = pl.BlockSpec(memory_space=pltpu.HBM)
 
@@ -29,16 +29,15 @@
     return high, (value - high.astype(F32)).astype(BF16)
 
 
-def request_kernel(mon_ref, ends_ref, off_ref, live_ref, out_ref):
-    slots, outages = mon_ref.shape
+def request_kernel(table_ref, out_ref):
+    outages = table_ref.shape[1]
+    slots = table_ref.shape[0] - 4
     lines = out_ref.shape[0]
-
-    def twice(row):
-        return jnp.concatenate([row, row], axis=1)
-
-    named = twice(mon_ref[...])
+    table = table_ref[...]
+    table = jnp.concatenate([table, table], axis=1)
+    named = table[:slots]
     line_row = iota((lines, 128), 0)
-    live = twice(live_ref[...])
+    live = table[slots + 3 : slots + 4]
     names = jnp.zeros((lines, 128), F32)
     asks = jnp.zeros((lines, 128), F32)
     for s in range(slots):
@@ -50,9 +49,9 @@
         names.astype(BF16), jnp.where(earlier, 1.0, 0.0).astype(BF16), NN, preferred_element_type=F32
     )
     rank = jnp.where(asks > 0.0, rank, -1.0)
-    start = twice(ends_ref[0:1, :]) + 1
-    end = twice(ends_ref[1:2, :]) + 1
-    place = twice(off_ref[...]) + 1
+    start = table[slots : slots + 1] + 1
+    end = table[slots + 1 : slots + 2] + 1
+    place = table[slots + 2 : slots + 3] + 1
     second = iota((1, 128), 1) // outages
     spot = iota((128, 128), 0)
     chosen, high, low = [], [], []
@@ -70,24 +69,12 @@
     out_ref[...] = 256.0 * high + low
 
 
-def flow_kernel(s_hbm, inj_hbm, part_ref, s_ref, inj_ref, flow_ref, s_sems, inj_sems):
+def flow_kernel(s_ref, inj_ref, part_ref, flow_ref):
     rows, width = s_ref.shape
     whole, rest = width // CHUNK, width % CHUNK
-
-    def copies(at, size, q):
-        cols = pl.ds(at, size)
-        return (
-            pltpu.make_async_copy(s_hbm.at[:, cols], s_ref.at[:, cols], s_sems.at[q]),
-            pltpu.make_async_copy(inj_hbm.at[:, cols], inj_ref.at[:, cols], inj_sems.at[q]),
-        )
-
-    def fetch(at, size, q):
-        for copy in copies(at, size, q):
-            copy.start()
-
-    def step(at, size, q):
-        for copy in copies(at, size, q):
-            copy.wait()
+    flow_ref[...] = jnp.zeros_like(flow_ref)
+
+    def step(at, size):
         cols = pl.ds(at, size)
         flow_ref[...] += lax.dot_general(
             jnp.concatenate(split2(inj_ref[:, cols]), axis=0),
@@ -96,17 +83,12 @@
             preferred_element_type=F32,
         )
 
-    for q in range(whole):
-        fetch(q * CHUNK, CHUNK, q)
-    fetch(whole * CHUNK, rest, whole)
-    flow_ref[...] = jnp.zeros_like(flow_ref)
-
     def body(q, carry):
-        step(pl.multiple_of(q * CHUNK, CHUNK), CHUNK, q)
+        step(pl.multiple_of(q * CHUNK, CHUNK), CHUNK)
         return carry
 
     lax.fori_loop(0, whole, body, 0)
-    step(whole * CHUNK, rest, whole)
+    step(whole * CHUNK, rest)
     part_ref[...] = (
         flow_ref[:HOURS, :rows]
         + (flow_ref[:HOURS, rows:] + flow_ref[HOURS:, :rows])
@@ -119,7 +101,6 @@
     s_hbm,
     out_ref,
     s_ref,
-    split_ref,
     turn_ref,
     perm_ref,
     from_ref,
@@ -134,6 +115,7 @@
     packed = from_ref.shape[0]
     deep = rows // peers
     whole, rest = width // CHUNK, width % CHUNK
+
 
     def copy(at, size, q):
         cols = pl.ds(at, size)
@@ -196,7 +178,7 @@
         to_ref[...] = jnp.broadcast_to(end, (packed, 128)).astype(jnp.int16)
         sum_ref[...] = jnp.zeros_like(sum_ref)
 
-    def pick(at, size):
+    def hot(at, size):
         columns = []
         for t in range(size // 128):
             spot = (iota((16, 128), 1) + (at + t * 128)).astype(jnp.int16)
@@ -204,9 +186,11 @@
             columns.append(
                 jnp.where(from_ref[...] == spot, one, jnp.where(to_ref[...] == spot, minus, zero))
             )
-        sum_ref[...] += lax.dot_general(
-            jnp.concatenate(columns, axis=1), split_ref[:, pl.ds(at, size)], NT, preferred_element_type=F32
-        )
+        return jnp.concatenate(columns, axis=1)
+
+    def multiply(left, at, size):
+        both = jnp.concatenate(split2(s_ref[:, pl.ds(at, size)]), axis=0)
+        return lax.dot_general(left, both, NT, preferred_element_type=F32)
 
     def close_block():
         turned = jnp.transpose(sum_ref[:, :rows] + sum_ref[:, rows:])
@@ -215,20 +199,17 @@
         )
         total_ref[...] += both[:rows] + both[rows:]
 
-    def step(at, size):
-        cols = pl.ds(at, size)
-        both = jnp.concatenate(split2(s_ref[:, cols]), axis=0)
-        split_ref[:, cols] = both
-        pick(at, size)
+    def pick(at, size):
+        sum_ref[...] += multiply(hot(at, size), at, size)
 
     open_block(0)
     copy(whole * CHUNK, rest, whole).wait()
-    step(whole * CHUNK, rest)
+    pick(whole * CHUNK, rest)
 
     def first_block(q, carry):
         at = pl.multiple_of(q * CHUNK, CHUNK)
         copy(at, CHUNK, q).wait()
-        step(at, CHUNK)
+        pick(at, CHUNK)
         return carry
 
     lax.fori_loop(0, whole, first_block, 0)
@@ -337,9 +318,8 @@
         put(p, 5, jnp.transpose(three)[:lines])
 
 
-def screen_kernel(got_ref, mon_ref, off_ref, live_ref, out_ref):
-    slots, outages = mon_ref.shape
-    sub = out_ref.shape[1]
+def screen_kernel(got_ref, table_ref, out_ref):
+    slots, sub, outages = out_ref.shape
     passes = lax.axis_size("bus_z")
     lines = got_ref.shape[0] // (passes * TILES)
     place = lax.axis_index("bus_x") * passes + lax.axis_index("bus_z")
@@ -356,7 +336,8 @@
     sums = [piece(tile(0, t) + tile(1, t)) for t in (4, 3, 5)]
     shared = jnp.concatenate([piece(tile(p, t)) for p in range(passes) for t in range(2)] + sums, axis=0)
     own = jnp.concatenate([piece(tile(p, t)) for p in range(passes) for t in range(2, 4)] + sums[2:], axis=0)
-    named = jnp.concatenate([mon_ref[...], mon_ref[...]], axis=1)
+    table = jnp.concatenate([table_ref[...], table_ref[...]], axis=1)
+    named = table[:slots]
     line_row = iota((lines, 128), 0)
     lane = iota((1, 128), 1)
     outage = lane % outages
@@ -391,8 +372,8 @@
         self_sens = jnp.where(mine, got_own[at : at + 1], self_sens)
     lost = jnp.concatenate(lost, axis=0)
     divisor = jnp.maximum(1.0 - self_sens, floor_value)
-    off = jnp.concatenate([off_ref[...], off_ref[...]], axis=1)
-    live = jnp.concatenate([live_ref[...], live_ref[...]], axis=1)
+    off = table[slots + 2 : slots + 3]
+    live = table[slots + 3 : slots + 4]
     row = iota((sub, 128), 0)
     for t in range(slots // 2):
         target = jnp.where(lane < outages, named[2 * t : 2 * t + 1], named[2 * t + 1 : 2 * t + 2])
@@ -437,31 +418,23 @@
     outages, slot_count = monitored.shape
     entries = CAP * line_count
     shape = jax.ShapeDtypeStruct
-    off_row = outage_offset.reshape(1, outages)
-    live_row = live_count.reshape(1, outages)
     rate_row = rating.reshape(1, block_rows)
-    named = monitored.T
+    table = jnp.concatenate(
+        [monitored.T, outage_ends.T, outage_offset.reshape(1, outages), live_count.reshape(1, outages)], axis=0
+    )
     with jax.named_scope("requests"):
-        requests = call(request_kernel, shape((line_count, 128), F32), [IN_VMEM] * 4, limit=56)(
-            named, outage_ends.T, off_row, live_row
+        requests = call(request_kernel, shape((line_count, 128), F32), [IN_VMEM], flops=10**10, moved=10**7)(
+            table
         )
         asked = lax.all_to_all(requests, "line", split_axis=0, concat_axis=0, tiled=True)
-    pieces = bus_width // CHUNK + 1
     with jax.named_scope("flows"):
         mine = call(
             flow_kernel,
             shape((HOURS, block_rows), F32),
-            [IN_HBM, IN_HBM],
-            scratch=(
-                pltpu.VMEM((block_rows, bus_width), F32),
-                pltpu.VMEM((HOURS, bus_width), F32),
-                pltpu.VMEM((2 * HOURS, 2 * block_rows), F32),
-                pltpu.SemaphoreType.DMA((pieces,)),
-                pltpu.SemaphoreType.DMA((pieces,)),
-            ),
+            [IN_VMEM] * 2,
+            scratch=(pltpu.VMEM((2 * HOURS, 2 * block_rows), F32),),
             flops=8 * HOURS * block_rows * bus_width,
             moved=4 * block_rows * bus_width,
-            limit=54,
         )(shift_factors, injection)
         other = lax.ppermute(mine, "bus_z", [(p, (p + 1) % passes) for p in range(passes)])
     with jax.named_scope("picks"):
@@ -471,14 +444,13 @@
             [IN_VMEM, IN_HBM],
             scratch=(
                 pltpu.VMEM((block_rows, bus_width), F32),
-                pltpu.VMEM((2 * block_rows, bus_width), BF16),
                 pltpu.VMEM((128, 128), F32),
                 pltpu.VMEM((PACKED, entries), BF16),
                 pltpu.VMEM((PACKED, 128), jnp.int16),
                 pltpu.VMEM((PACKED, 128), jnp.int16),
                 pltpu.VMEM((PACKED, 2 * block_rows), F32),
                 pltpu.VMEM((block_rows, entries), F32),
-                pltpu.SemaphoreType.DMA((pieces,)),
+                pltpu.SemaphoreType.DMA((bus_width // CHUNK + 1,)),
             ),
             flops=4 * entries * block_rows * bus_width,
             moved=4 * block_rows * bus_width,
@@ -498,8 +470,8 @@
         reply = reply.reshape(passes * line_count, TILES * 128)
         got = lax.all_to_all(reply, ("bus_z", "line"), split_axis=0, concat_axis=0, tiled=True)
     with jax.named_scope("screen"):
-        loading = call(screen_kernel, shape((slot_count, sub_rows, outages), F32), [IN_VMEM] * 4)(
-            got.reshape(-1, 128), named, off_row, live_row
+        loading = call(screen_kernel, shape((slot_count, sub_rows, outages), F32), [IN_VMEM] * 2)(
+            got.reshape(-1, 128), table
         )
     return jnp.transpose(loading, (2, 0, 1))
 

time: 76.6 us -> 76.2 us (level)
  Pallas kernels: 11.2 us -> 7.99 us
  local copies, waits for them, and re-layouts: 0.03 us -> 2.1 us
    pallas_call x2, Pallas kernels: 5.58 us -> 2.67 us  [the longest x1 1.56 us: local(): call(flow_kernel, shape((HOURS, block_rows), F32), [IN_VMEM] * 2, scratch...]
    unnamed x10 -> x6, local copies, waits for them, and re-layouts: 0.03 us -> 2.1 us
  transfers between devices with their start and end apart: 2 -> 2, of which waited for: 0 -> 0; matrix products, arithmetic and copies ran while one was open for 0% -> 0% of each run, Pallas kernels for 10% -> 7%
where the time goes in v10:
time: 76.2 us; the launch traced here: 75.9 us
  blocking collectives  42.5 us (56%)
  starting transfers between devices  22.5 us (30%)
  Pallas kernels  7.99 us (10%)
  local copies, waits for them, and re-layouts  2.1 us (3%)
    all_to_all x1, blocking collectives, local(): lax.all_to_all(reply, ('bus_z', 'line'), split_axis=0, concat_axis=0, til...  30.5 us
    all_to_all x1, starting transfers between devices, local(): lax.all_to_all(requests, 'line', split_axis=0, concat_axis=0, tiled=True)  14.6 us
    all_to_all x1, blocking collectives, local(): lax.all_to_all(partial_sens, 'bus_x', split_axis=0, concat_axis=0, tiled=...  12 us
    ppermute x1, starting transfers between devices, local(): lax.ppermute(mine, 'bus_z', [(p, (p + 1) % passes) for p in range(passes)])  7.94 us
    pallas_call x1, Pallas kernels, local(): call(pick_kernel, shape((peers, passes * sub_rows + 8, entries), F32), [I...  3.61 us
    unnamed x6, local copies, waits for them, and re-layouts  2.1 us
    pallas_call x1, Pallas kernels, local(): call(flow_kernel, shape((HOURS, block_rows), F32), [IN_VMEM] * 2, scratch...  1.56 us
  transfers between devices with their start and end apart: 2, of which 0 were waited for; matrix products, arithmetic and copies ran while one was open for 0% of the time, Pallas kernels for 7%

profile of v10, /device:TPU:1, one launch (start us, length us, event | category | flops | bytes accessed | tf_op | source)
XLA Modules:
  0.0 75.9 jit_solution(16326883667357639650)
XLA Ops:
  0.0 0.7 pad_add_fusion.table_ref
  0.7 0.0 copy-start.1
  0.8 1.1 %requests.1 = f32[64,128]{1,0:T(8,128)} custom-call(s32[12,64]{1,0:T(8,128)S(1)} %pad_add_fusion.table_ref), custom_call_target="tpu_custom_call" | custom-call | flops 10000000000 | bytes 10000000 | tf_op jit(solution)/shard_map/requests/pallas_call | solution.py:426
  1.9 14.6 %all-to-all-start = ((f32[64,1,128]{2,1,0:T(1,128)}), f32[64,1,128]{2,1,0:T(1,128)S(1)}, u32[]{:S(2)}, u32[]{:S(2)}) async-start(f32[64,1,128]{2,1,0:T(1,128)} %bitcast.5), calls=%async_computation | async-start | bytes 65536 | tf_op jit(solution)/shard_map/requests/all_to_all | solution.py:429
  16.4 0.0 copy-done.1
  16.5 0.0 copy-start
  16.5 2.1 %copy-done = f32[128,7552]{1,0:T(8,128)S(1)} copy-done((f32[128,7552]{1,0:T(8,128)S(1)}, f32[128,7552]{1,0:T(8,128)}, u32[]{:S(2)}) %copy-start) | copy-done | bytes 3866648
  18.6 1.6 %flows.1.mine_ref = f32[32,128]{1,0:T(8,128)S(1)} custom-call(f32[128,7552]{1,0:T(8,128)S(1)} %copy-done, f32[32,7552]{1,0:T(8,128)S(1)} %copy-done.1), custom_call_target="tpu_custom_call" | custom-call | flops 247463936 | bytes 3866624 | tf_op jit(solution)/shard_map/flows/pallas_call | solution.py:431
  20.1 7.9 %collective-permute-start = (f32[32,128]{1,0:T(8,128)S(1)}, f32[32,128]{1,0:T(8,128)S(1)}, u32[]{:S(2)}, u32[]{:S(2)}) collective-permute-start(f32[32,128]{1,0:T(8,128)S(1)} %flows.1.mine_ref), channel_id=1, source_target_pairs={{0,1},{1,0},{2,3},{3,2},{4,5},{5,4},{6,7},{7,6},{8,9},{9,8},{10,11... | collective-permute-start | bytes 49160 | tf_op jit(solution)/shard_map/flows/ppermute | solution.py:439
  28.1 0.0 all-to-all-done
  28.1 0.0 copy-start.2
  28.1 3.6 %picks.2.message_ref = f32[4,40,768]{2,1,0:T(8,128)S(1)} custom-call(f32[64,128]{1,0:T(8,128)S(1)} %bitcast.14, f32[128,7552]{1,0:T(8,128)} %s_ref.1), custom_call_target="tpu_custom_call" | custom-call | flops 2969567232 | bytes 3866624 | tf_op jit(solution)/shard_map/picks/pallas_call | solution.py:441
  31.7 0.0 collective-permute-done.other_ref
  31.8 12.0 %all_to_all.25.got_ref = f32[4,40,768]{2,1,0:T(8,128)S(1)} all-to-all(f32[4,40,768]{2,1,0:T(8,128)S(1)} %picks.3), channel_id=1, replica_groups=mesh['line'=64,'bus_x'=4,'bus_z'=2] {'bus_x'}, dimensions={0} | all-to-all | bytes 983040 | tf_op jit(solution)/shard_map/picks/all_to_all | solution.py:462
  43.7 0.0 copy-done.2
  43.7 0.4 reply.1
  44.1 30.5 %all_to_all.26 = f32[128,1,768]{2,1,0:T(1,128)S(1)} all-to-all(f32[128,1,768]{2,1,0:T(1,128)S(1)} %bitcast.12), channel_id=1, replica_groups=mesh['line'=64,'bus_x'=4,'bus_z'=2] {'bus_z','line'}, dimensions={0} | all-to-all | bytes 786432 | tf_op jit(solution)/shard_map/reply/all_to_all | solution.py:471
  74.6 1.3 %screen.1 = f32[8,16,64]{2,1,0:T(8,128)} custom-call(f32[768,128]{1,0:T(8,128)S(1)} %bitcast.13, s32[12,64]{1,0:T(8,128)S(1)} %pad_add_fusion.table_ref), custom_call_target="tpu_custom_call" | custom-call | tf_op jit(solution)/shard_map/screen/pallas_call | solution.py:473
  (1 shorter events, 0.0 us)
Async XLA Ops:
  0.7 15.7 %copy-start.1 = (f32[32,7552]{1,0:T(8,128)S(1)}, f32[32,7552]{1,0:T(8,128)}, u32[]{:S(2)}) copy-start(f32[32,7552]{1,0:T(8,128)} %inj_ref.1) | copy-start | bytes 2899972
  1.9 26.2 %all-to-all-start = ((f32[64,1,128]{2,1,0:T(1,128)}), f32[64,1,128]{2,1,0:T(1,128)S(1)}, u32[]{:S(2)}, u32[]{:S(2)}) async-start(f32[64,1,128]{2,1,0:T(1,128)} %bitcast.5), calls=%async_computation | async-start | bytes 65536 | tf_op jit(solution)/shard_map/requests/all_to_all | solution.py:429
  16.5 2.1 %copy-start = (f32[128,7552]{1,0:T(8,128)S(1)}, f32[128,7552]{1,0:T(8,128)}, u32[]{:S(2)}) copy-start(f32[128,7552]{1,0:T(8,128)} %s_ref.1) | copy-start | bytes 11599876
  20.1 11.6 %collective-permute-start = (f32[32,128]{1,0:T(8,128)S(1)}, f32[32,128]{1,0:T(8,128)S(1)}, u32[]{:S(2)}, u32[]{:S(2)}) collective-permute-start(f32[32,128]{1,0:T(8,128)S(1)} %flows.1.mine_ref), channel_id=1, source_target_pairs={{0,1},{1,0},{2,3},{3,2},{4,5},{5,4},{6,7},{7,6},{8,9},{9,8},{10,11... | collective-permute-start | bytes 49160 | tf_op jit(solution)/shard_map/flows/ppermute | solution.py:439
  28.1 15.6 %copy-start.2 = (f32[128]{0:T(128)S(1)}, f32[128]{0:T(128)}, u32[]{:S(2)}) copy-start(f32[128]{0:T(128)} %param.9) | copy-start | bytes 1540

commit v11 on v9

--- a/solution.py
+++ b/solution.py
@@ -129,7 +129,6 @@
     offs = table[5:6].astype(jnp.int32) - 1
     table_low = table.astype(BF16)
     one, minus, zero = jnp.asarray(1, BF16), jnp.asarray(-1, BF16), jnp.asarray(0, BF16)
-    total_ref[...] = jnp.zeros_like(total_ref)
 
     def open_block(block):
         perm = jnp.where(iota((packed, entries), 0) + block * packed == ranks, 1.0, 0.0).astype(BF16)
@@ -139,7 +138,6 @@
         end = (128.0 * ends[:, 2:3] + ends[:, 3:4] - 1.0).astype(jnp.int32)
         from_ref[...] = jnp.broadcast_to(start, (packed, 128)).astype(jnp.int16)
         to_ref[...] = jnp.broadcast_to(end, (packed, 128)).astype(jnp.int16)
-        sum_ref[...] = jnp.zeros_like(sum_ref)
 
     def hot(at, size):
         columns = []
@@ -160,21 +158,21 @@
         both = lax.dot_general(
             jnp.concatenate(split2(turned), axis=0), perm_ref[...], NN, preferred_element_type=F32
         )
-        total_ref[...] += both[:rows] + both[rows:]
+        return both[:rows] + both[rows:]
 
     def step(at, size):
         left = jnp.concatenate((hot(at, size),) + split2(inj_ref[:, pl.ds(at, size)]), axis=0)
-        sum_ref[...] += multiply(left, at, size)
+        return multiply(left, at, size)
 
     def pick(at, size):
-        sum_ref[:packed] += multiply(hot(at, size), at, size)
+        return multiply(hot(at, size), at, size)
 
     open_block(0)
-    step(whole * CHUNK, rest)
+    sum_ref[...] = step(whole * CHUNK, rest)
 
     def first_block(q, carry):
         at = pl.multiple_of(q * CHUNK, CHUNK)
-        step(at, CHUNK)
+        sum_ref[...] += step(at, CHUNK)
         return carry
 
     lax.fori_loop(0, whole, first_block, 0)
@@ -182,18 +180,18 @@
     part = (
         flows[:HOURS, :rows] + (flows[:HOURS, rows:] + flows[HOURS:, :rows]) + flows[HOURS:, rows:]
     )
-    close_block()
+    total_ref[...] = close_block()
 
     def other_block(block, carry):
         open_block(block)
-        pick(whole * CHUNK, rest)
+        sum_ref[:packed] = pick(whole * CHUNK, rest)
 
         def piece(q, carry):
-            pick(pl.multiple_of(q * CHUNK, CHUNK), CHUNK)
+            sum_ref[:packed] += pick(pl.multiple_of(q * CHUNK, CHUNK), CHUNK)
             return carry
 
         lax.fori_loop(0, whole, piece, 0)
-        close_block()
+        total_ref[...] += close_block()
         return carry
 
     lax.fori_loop(1, blocks, other_block, 0)

time: 74.6 us -> 74.6 us (level)
  no operation moved by 1% of the time
where the time goes in v11:
time: 74.6 us; the launch traced here: 74.4 us
  blocking collectives  68.4 us (92%)
  Pallas kernels  5.24 us (7%)
    all_to_all x1, blocking collectives, local(): lax.all_to_all(reply, ('line', 'bus_z'), split_axis=0, concat_axis=0, til...  32 us
    all_to_all x1, blocking collectives, local(): lax.all_to_all(requests, 'line', split_axis=0, concat_axis=0, tiled=True)  24.3 us
    all_to_all x1, blocking collectives, local(): lax.all_to_all(partial_sens, 'bus_x', split_axis=0, concat_axis=0, tiled=...  12.1 us
    pallas_call x1, Pallas kernels, local(): call(pick_kernel, shape((peers, passes * sub_rows + 8, entries), F32), [I...  3.15 us

profile of v11, /device:TPU:1, one launch (start us, length us, event | category | flops | bytes accessed | tf_op | source)
XLA Modules:
  0.0 74.4 jit_solution(9274438569456870215)
XLA Ops:
  0.0 0.7 %pad_add_fusion.table_ref = s32[12,64]{1,0:T(8,128)S(1)} fusion(s32[1,64]{1,0:T(1,128)} %bitcast.20, s32[1,64]{1,0:T(1,128)} %bitcast.21, s32[2,64]{1,0:T(2,128)} %bitcast.19, s32[8,64]{1,0:T(8,128)} %bitcast.18), kind=kLoop, calls=%fused_computation | loop fusion | flops 2304 | bytes 6144 | tf_op jit(solution)/shard_map/concatenate | solution.py:370
  0.7 0.0 copy-start.1
  0.8 0.0 copy-start.2
  0.8 0.5 requests.1
  1.3 24.3 %all_to_all.25 = f32[64,1,128]{2,1,0:T(1,128)S(1)} all-to-all(f32[64,1,128]{2,1,0:T(1,128)S(1)} %bitcast.16), channel_id=1, replica_groups=mesh['line'=64,'bus_x'=4,'bus_z'=2] {'line'}, dimensions={0} | all-to-all | bytes 65536 | tf_op jit(solution)/shard_map/requests/all_to_all | solution.py:377
  25.5 0.0 copy-done.1
  25.5 0.0 copy-done.2
  25.5 0.0 copy-start
  25.6 3.1 %picks.1 = f32[4,40,768]{2,1,0:T(8,128)S(1)} custom-call(f32[64,128]{1,0:T(8,128)S(1)} %bitcast.14, f32[128,7552]{1,0:T(8,128)S(1)} %copy-done.1, f32[32,7552]{1,0:T(8,128)S(1)} %copy-done.2), custom_call_target="tpu_custom_call" | custom-call | flops 2969567232 | bytes 3866624 | tf_op jit(solution)/shard_map/picks/pallas_call | solution.py:379
  28.7 12.1 %all_to_all.26.got_ref = f32[4,40,768]{2,1,0:T(8,128)S(1)} all-to-all(f32[4,40,768]{2,1,0:T(8,128)S(1)} %picks.1), channel_id=1, replica_groups=mesh['line'=64,'bus_x'=4,'bus_z'=2] {'bus_x'}, dimensions={0} | all-to-all | bytes 983040 | tf_op jit(solution)/shard_map/picks/all_to_all | solution.py:395
  40.8 0.0 copy-done
  40.8 0.4 reply.1
  41.1 32.0 %all_to_all.27 = f32[128,1,1152]{2,1,0:T(1,128)S(1)} all-to-all(f32[128,1,1152]{2,1,0:T(1,128)S(1)} %bitcast.12), channel_id=1, replica_groups=mesh['line'=64,'bus_x'=4,'bus_z'=2] {'line','bus_z'}, dimensions={0} | all-to-all | bytes 1179648 | tf_op jit(solution)/shard_map/reply/all_to_all | solution.py:404
  73.2 1.2 %screen.1 = f32[8,16,64]{2,1,0:T(8,128)} custom-call(f32[1152,128]{1,0:T(8,128)S(1)} %bitcast.13, s32[12,64]{1,0:T(8,128)S(1)} %pad_add_fusion.table_ref), custom_call_target="tpu_custom_call" | custom-call | tf_op jit(solution)/shard_map/screen/pallas_call | solution.py:406
Async XLA Ops:
  0.7 24.8 %copy-start.1 = (f32[128,7552]{1,0:T(8,128)S(1)}, f32[128,7552]{1,0:T(8,128)}, u32[]{:S(2)}) copy-start(f32[128,7552]{1,0:T(8,128)} %s_ref.1) | copy-start | bytes 11599876
  0.8 24.8 %copy-start.2 = (f32[32,7552]{1,0:T(8,128)S(1)}, f32[32,7552]{1,0:T(8,128)}, u32[]{:S(2)}) copy-start(f32[32,7552]{1,0:T(8,128)} %inj_ref.1) | copy-start | bytes 2899972
  25.5 15.2 %copy-start = (f32[128]{0:T(128)S(1)}, f32[128]{0:T(128)}, u32[]{:S(2)}) copy-start(f32[128]{0:T(128)} %param.9) | copy-start | bytes 1540

commit v12 on v11

--- a/solution.py
+++ b/solution.py
@@ -222,8 +222,7 @@
     lane = iota((HOURS, 128), 1)
     hour = iota((HOURS, 128), 0)
     f_high, f_low = split2(flows)
-    f_rest = (flows - f_high.astype(F32) - f_low.astype(F32)).astype(BF16)
-    f_all = jnp.concatenate([f_high, f_low, f_rest], axis=0)
+    f_all = jnp.concatenate([f_high, f_low], axis=0)
     req = req_ref[...]
     lane_line = iota((lines, 128), 1)
     hots = [
@@ -252,7 +251,7 @@
     for p in range(passes):
         wanted = iota((128, 128), 0) == (place + p) * sub + iota((128, 128), 1) % sub
         spread = lax.dot_general(f_all, jnp.where(wanted, 1.0, 0.0).astype(BF16), NN, preferred_element_type=F32)
-        spread = spread[:HOURS] + spread[HOURS : 2 * HOURS] + spread[2 * HOURS :]
+        spread = spread[:HOURS] + spread[HOURS:]
         spread = jnp.where(lane // sub == hour % 8, spread, 0.0)
         for t in range(4):
             row = jnp.sum(spread[8 * t : 8 * t + 8], axis=0, keepdims=True)

time: 74.6 us -> 74.6 us (level)
  no operation moved by 1% of the time
where the time goes in v12:
time: 74.6 us; the launch traced here: 74.4 us
  blocking collectives  68.4 us (92%)
  Pallas kernels  5.24 us (7%)
    all_to_all x1, blocking collectives, local(): lax.all_to_all(reply, ('line', 'bus_z'), split_axis=0, concat_axis=0, til...  32 us
    all_to_all x1, blocking collectives, local(): lax.all_to_all(requests, 'line', split_axis=0, concat_axis=0, tiled=True)  24.3 us
    all_to_all x1, blocking collectives, local(): lax.all_to_all(partial_sens, 'bus_x', split_axis=0, concat_axis=0, tiled=...  12.1 us
    pallas_call x1, Pallas kernels, local(): call(pick_kernel, shape((peers, passes * sub_rows + 8, entries), F32), [I...  3.15 us

profile of v12, /device:TPU:1, one launch (start us, length us, event | category | flops | bytes accessed | tf_op | source)
XLA Modules:
  0.0 74.4 jit_solution(6238039516490467482)
XLA Ops:
  0.0 0.7 %pad_add_fusion.table_ref = s32[12,64]{1,0:T(8,128)S(1)} fusion(s32[1,64]{1,0:T(1,128)} %bitcast.20, s32[1,64]{1,0:T(1,128)} %bitcast.21, s32[2,64]{1,0:T(2,128)} %bitcast.19, s32[8,64]{1,0:T(8,128)} %bitcast.18), kind=kLoop, calls=%fused_computation | loop fusion | flops 2304 | bytes 6144 | tf_op jit(solution)/shard_map/concatenate | solution.py:369
  0.7 0.0 copy-start.1
  0.8 0.0 copy-start.2
  0.8 0.5 requests.1
  1.3 24.3 %all_to_all.25 = f32[64,1,128]{2,1,0:T(1,128)S(1)} all-to-all(f32[64,1,128]{2,1,0:T(1,128)S(1)} %bitcast.16), channel_id=1, replica_groups=mesh['line'=64,'bus_x'=4,'bus_z'=2] {'line'}, dimensions={0} | all-to-all | bytes 65536 | tf_op jit(solution)/shard_map/requests/all_to_all | solution.py:376
  25.5 0.0 copy-done.1
  25.5 0.0 copy-done.2
  25.5 0.0 copy-start
  25.6 3.1 %picks.1 = f32[4,40,768]{2,1,0:T(8,128)S(1)} custom-call(f32[64,128]{1,0:T(8,128)S(1)} %bitcast.14, f32[128,7552]{1,0:T(8,128)S(1)} %copy-done.1, f32[32,7552]{1,0:T(8,128)S(1)} %copy-done.2), custom_call_target="tpu_custom_call" | custom-call | flops 2969567232 | bytes 3866624 | tf_op jit(solution)/shard_map/picks/pallas_call | solution.py:378
  28.7 12.1 %all_to_all.26.got_ref = f32[4,40,768]{2,1,0:T(8,128)S(1)} all-to-all(f32[4,40,768]{2,1,0:T(8,128)S(1)} %picks.1), channel_id=1, replica_groups=mesh['line'=64,'bus_x'=4,'bus_z'=2] {'bus_x'}, dimensions={0} | all-to-all | bytes 983040 | tf_op jit(solution)/shard_map/picks/all_to_all | solution.py:394
  40.8 0.0 copy-done
  40.8 0.4 reply.1
  41.1 32.0 %all_to_all.27 = f32[128,1,1152]{2,1,0:T(1,128)S(1)} all-to-all(f32[128,1,1152]{2,1,0:T(1,128)S(1)} %bitcast.12), channel_id=1, replica_groups=mesh['line'=64,'bus_x'=4,'bus_z'=2] {'line','bus_z'}, dimensions={0} | all-to-all | bytes 1179648 | tf_op jit(solution)/shard_map/reply/all_to_all | solution.py:403
  73.2 1.2 %screen.1 = f32[8,16,64]{2,1,0:T(8,128)} custom-call(f32[1152,128]{1,0:T(8,128)S(1)} %bitcast.13, s32[12,64]{1,0:T(8,128)S(1)} %pad_add_fusion.table_ref), custom_call_target="tpu_custom_call" | custom-call | tf_op jit(solution)/shard_map/screen/pallas_call | solution.py:405
Async XLA Ops:
  0.7 24.8 %copy-start.1 = (f32[128,7552]{1,0:T(8,128)S(1)}, f32[128,7552]{1,0:T(8,128)}, u32[]{:S(2)}) copy-start(f32[128,7552]{1,0:T(8,128)} %s_ref.1) | copy-start | bytes 11599876
  0.8 24.8 %copy-start.2 = (f32[32,7552]{1,0:T(8,128)S(1)}, f32[32,7552]{1,0:T(8,128)}, u32[]{:S(2)}) copy-start(f32[32,7552]{1,0:T(8,128)} %inj_ref.1) | copy-start | bytes 2899972
  25.5 15.2 %copy-start = (f32[128]{0:T(128)S(1)}, f32[128]{0:T(128)}, u32[]{:S(2)}) copy-start(f32[128]{0:T(128)} %param.9) | copy-start | bytes 1540
